TPU v7x, 32 devices: a whole 2x2x4 slice. The times are simulated.
32 devices in a mesh: samp: 4 (over z), pix: 8 (over y, x, core).
Axes of the slice: x: 2, y: 2, z: 4, core: 2. Of those that a mesh axis runs over, the one named last changes fastest.
Arguments:
- pixels: bfloat16 [16, 261, 16384], P('samp', None, 'pix'), may hold values from -6 to 6
- pixel_mask: int32 [16, 16384], P('samp', 'pix'), may hold values from 0 to 1, as said below
- proj_blocks: float32 [128, 4, 64, 128], P(('samp', 'pix')), may hold values from -1 to 1
- proj_left: float32 [128, 4, 64, 64], P(('samp', 'pix')), may hold values from -2097152 to 8388608, as said below
- proj_right: float32 [128, 4, 128, 128], P(('samp', 'pix')), may hold values from -1048576 to 4194304, as said below
- left_roots: float32 [128, 4, 64, 64], P(('samp', 'pix')), may hold values from -1 to 1, as said below
- right_roots: float32 [128, 4, 128, 128], P(('samp', 'pix')), may hold values from -1 to 1, as said below
- keyval_weight: float32 [261, 2048], P(None, ('samp', 'pix')), may hold values from -0.375 to 0.375
- keyval_second: float32 [261, 2048], P(None, ('samp', 'pix')), may hold values from 2750 to 11000
- latents: float32 [512, 1024], P('pix'), may hold values from -6 to 6
- latent_second: float32 [512, 1024], P('pix'), may hold values from 48 to 192
- gains: float32 [2309], replicated, may hold values from 0.5 to 1.5
- gain_second: float32 [2309], replicated, may hold values from 16384 to 70000
- mixed_grad: bfloat16 [16, 512, 1024], P('samp', 'pix'), may hold values from -6 to 6
Outputs:
- mixed: bfloat16 [16, 512, 1024], P('samp', 'pix')
- pixel_grad: float32 [16, 261, 16384], P('samp', None, 'pix')
- proj_grad: float32 [128, 4, 64, 128], P(('samp', 'pix'))
- left_new: float32 [128, 4, 64, 64], P(('samp', 'pix'))
- right_new: float32 [128, 4, 128, 128], P(('samp', 'pix'))
- proj_new: float32 [128, 4, 64, 128], P(('samp', 'pix'))
- keyval_grad: float32 [261, 2048], P(None, ('samp', 'pix'))
- keyval_second_new: float32 [261, 2048], P(None, ('samp', 'pix'))
- keyval_new: float32 [261, 2048], P(None, ('samp', 'pix'))
- latent_grad: float32 [512, 1024], P('pix')
- latent_second_new: float32 [512, 1024], P('pix')
- latent_new: float32 [512, 1024], P('pix')
- gain_grad: float32 [2309], replicated
- gain_second_new: float32 [2309], replicated
- gain_new: float32 [2309], replicated
Inputs may be any that keep to these rules, and one draw needn't show every extreme that they name: `pixel_mask`: an image's valid pixels come first: its mask is 1 on its first 5056, 9911 or 16384 pixels and 0 after; each run of 4 consecutive images holds one or more images with all 16384 valid. `proj_left`: each block is symmetric. `proj_right`: each block is symmetric. `left_roots`: each block is symmetric. `right_roots`: each block is symmetric.
All inputs are finite; a program needn't handle non-finite values.
Results may differ from a plain program's by a relative error of at most 0.035.
Values may be sent and summed in bfloat16 or wider, within the bound.
A program may use at most 256 MiB of HBM per device.

v0:
```python
import jax
import jax.numpy as jnp
from jax import lax
from jax.sharding import PartitionSpec as P

EPSILON = 1e-05
NEGATIVE = -1e30
HIGHEST = lax.Precision.HIGHEST
STAT_DECAY = 0.5
MATRIX_RATE = 0.5
KEYVAL_RATE = 0.05
LATENT_RATE = 0.7
GAIN_RATE = 0.6
MOMENT_FLOOR = 1e-08


def matmul(former, latter):
    return jnp.dot(former, latter, preferred_element_type=jnp.float32)


def contract(former, latter, former_dim, latter_dim):
    return lax.dot_general(
        former,
        latter,
        (((former_dim,), (latter_dim,)), ((), ())),
        preferred_element_type=jnp.float32,
    )


def gelu_exact(values):
    return jax.nn.gelu(values, approximate=False)


def normalize_parts(values, axis):
    row_mean = jnp.mean(values, axis=axis, keepdims=True)
    centered = values - row_mean
    variance = jnp.mean(centered * centered, axis=axis, keepdims=True)
    inverse = lax.rsqrt(variance + EPSILON)
    return (centered * inverse, inverse)


def normalize_back(grad_hat, normal_hat, inverse, axis):
    first_mean = jnp.mean(grad_hat, axis=axis, keepdims=True)
    second_mean = jnp.mean(grad_hat * normal_hat, axis=axis, keepdims=True)
    return inverse * (grad_hat - first_mean - normal_hat * second_mean)


def assemble(blocks, model_width, row_block, col_block):
    shaped = blocks.reshape(
        model_width // row_block, model_width // col_block, row_block, col_block
    )
    return shaped.transpose(0, 2, 1, 3).reshape(model_width, model_width)


def block_outer(left_rows, right_rows, row_block, col_block):
    row_count, width = left_rows.shape
    left_blocks = left_rows.reshape(row_count, width // row_block, row_block)
    right_blocks = right_rows.reshape(row_count, width // col_block, col_block)
    outer = jnp.einsum(
        "rxa,ryb->xyab", left_blocks, right_blocks, preferred_element_type=jnp.float32
    )
    return outer.reshape(-1, row_block, col_block)


def moment_step(weight, grad, second, rate):
    second_new = STAT_DECAY * second + (1.0 - STAT_DECAY) * grad * grad
    return (second_new, weight - rate * grad / (jnp.sqrt(second_new) + MOMENT_FLOOR))


def body(
    pixels,
    pixel_mask,
    proj_blocks,
    proj_left,
    proj_right,
    left_roots,
    right_roots,
    keyval_weight,
    keyval_second,
    latents,
    latent_second,
    gains,
    gain_second,
    mixed_grad,
):
    batches = pixels.shape[0]
    channels = pixels.shape[1]
    shard_pixels = pixels.shape[2]
    model_width = latents.shape[1]
    lat_rows = latents.shape[0]
    groups = lax.axis_size("pix")
    all_rows = lat_rows * groups
    owned_count = proj_blocks.shape[0]
    row_block = proj_blocks.shape[2]
    col_block = proj_blocks.shape[3]
    score_scale = model_width ** (-0.5)
    proj_all, keyval_all = (
        lax.all_gather(proj_blocks.astype(jnp.bfloat16), ("samp", "pix"), axis=0, tiled=True),
        lax.all_gather(keyval_weight.astype(jnp.bfloat16), ("samp", "pix"), axis=1, tiled=True),
    )
    query_weight = assemble(proj_all[:, 0], model_width, row_block, col_block)
    output_weight = assemble(proj_all[:, 1], model_width, row_block, col_block)
    mlp_in = assemble(proj_all[:, 2], model_width, row_block, col_block)
    mlp_out = assemble(proj_all[:, 3], model_width, row_block, col_block)
    latent_all = lax.all_gather(latents.astype(jnp.bfloat16), "pix", axis=0, tiled=True).astype(
        latents.dtype
    )
    lat_gain = gains[:model_width]
    in_gain = gains[model_width : model_width + channels]
    mlp_gain = gains[model_width + channels :]
    lat_hat, lat_inverse = normalize_parts(latent_all, 1)
    lat_normed = (lat_hat * lat_gain[None, :]).astype(jnp.bfloat16)
    query = matmul(lat_normed, query_weight).astype(jnp.bfloat16)

    def pixel_inputs(image_shard):
        normal_hat, inverse = normalize_parts(image_shard.astype(jnp.float32), 0)
        normed = (normal_hat * in_gain[:, None]).astype(jnp.bfloat16)
        return (normal_hat, inverse, normed)

    def shard_forward(image_shard, valid_cols):
        normal_hat, inverse, normed = pixel_inputs(image_shard)
        keyval = contract(normed, keyval_all, 0, 0).astype(jnp.bfloat16)
        key_rows = keyval[:, :model_width]
        value_rows = keyval[:, model_width:]
        scores = contract(query, key_rows, 1, 1) * score_scale
        masked = jnp.where(valid_cols[None, :], scores, NEGATIVE)
        shard_top = jnp.max(masked, axis=1).astype(jnp.bfloat16)
        weights = jnp.exp(
            jnp.where(
                valid_cols[None, :], scores - shard_top.astype(jnp.float32)[:, None], NEGATIVE
            )
        )
        shard_total = jnp.sum(weights, axis=1).astype(jnp.bfloat16)
        shard_numer = matmul(weights.astype(jnp.bfloat16), value_rows).astype(jnp.bfloat16)
        return (shard_numer, shard_top, shard_total, keyval)

    def shard_skip(image_shard, valid_cols):
        return (
            jnp.zeros((all_rows, model_width), jnp.bfloat16),
            jnp.full((all_rows,), NEGATIVE, jnp.float32).astype(jnp.bfloat16),
            jnp.zeros((all_rows,), jnp.bfloat16),
            jnp.zeros((shard_pixels, 2 * model_width), jnp.bfloat16),
        )

    def shard_backward(image_shard, valid_cols, keyval, shard_top, back_numer, back_total):
        normal_hat, inverse, normed = pixel_inputs(image_shard)
        key_rows = keyval[:, :model_width]
        value_rows = keyval[:, model_width:]
        scores = contract(query, key_rows, 1, 1) * score_scale
        weights = jnp.exp(
            jnp.where(
                valid_cols[None, :], scores - shard_top.astype(jnp.float32)[:, None], NEGATIVE
            )
        )
        grad_weights = (
            contract(back_numer, value_rows, 1, 1) + back_total.astype(jnp.float32)[:, None]
        )
        grad_scores = (weights * grad_weights).astype(jnp.bfloat16)
        query_term = matmul(grad_scores, key_rows) * score_scale
        grad_keys = contract(grad_scores, query, 0, 0) * score_scale
        grad_values = contract(weights.astype(jnp.bfloat16), back_numer, 0, 0)
        grad_keyval = jnp.concatenate([grad_keys, grad_values], axis=1).astype(jnp.bfloat16)
        keyval_term = matmul(normed, grad_keyval)
        grad_normed = contract(keyval_all, grad_keyval, 1, 1)
        gain_term = jnp.sum(grad_normed * normal_hat, axis=1)
        pixel_term = normalize_back(grad_normed * in_gain[:, None], normal_hat, inverse, 0)
        return (query_term, keyval_term, gain_term, pixel_term)

    def backward_skip(image_shard, valid_cols, keyval, shard_top, back_numer, back_total):
        return (
            jnp.zeros((all_rows, model_width), jnp.float32),
            jnp.zeros((channels, 2 * model_width), jnp.float32),
            jnp.zeros((channels,), jnp.float32),
            jnp.zeros((channels, shard_pixels), jnp.float32),
        )

    query_acc = jnp.zeros((all_rows, model_width), jnp.float32)
    in_gain_acc = jnp.zeros((channels,), jnp.float32)
    mlp_gain_acc = jnp.zeros((model_width,), jnp.float32)
    residual_acc = jnp.zeros((lat_rows, model_width), jnp.float32)
    triple_owned = jnp.zeros((owned_count, 3, row_block, col_block), jnp.float32)
    keyval_owned = jnp.zeros(keyval_weight.shape, jnp.float32)
    mixed_list = []
    pixel_list = []
    for batch_slot in range(batches):
        image_shard = pixels[batch_slot]
        valid_cols = pixel_mask[batch_slot] == 1
        has_pixels = jnp.any(valid_cols)
        shard_numer, shard_top, shard_total, keyval = lax.cond(
            has_pixels, shard_forward, shard_skip, image_shard, valid_cols
        )
        outgoing = (
            shard_numer.reshape(groups, lat_rows, model_width),
            shard_top.reshape(groups, lat_rows),
            shard_total.reshape(groups, lat_rows),
        )
        numer_in = lax.all_to_all(outgoing[0], "pix", split_axis=0, concat_axis=0, tiled=True)
        top_in = lax.all_to_all(outgoing[1], "pix", split_axis=0, concat_axis=0, tiled=True)
        total_in = lax.all_to_all(outgoing[2], "pix", split_axis=0, concat_axis=0, tiled=True)
        top_value = top_in.astype(jnp.float32)
        global_top = jnp.max(top_value, axis=0)
        factor = jnp.exp(top_value - global_top[None, :])
        denominator = jnp.sum(factor * total_in.astype(jnp.float32), axis=0)
        summed = jnp.einsum("gr,grd->rd", factor, numer_in, preferred_element_type=jnp.float32)
        attended = summed / denominator[:, None]
        weight_share = (factor / denominator[None, :]).T
        attended, weight_share = (attended, weight_share)
        attended_low = attended.astype(jnp.bfloat16)
        middle = latents + matmul(attended_low, output_weight)
        mid_hat, mid_inverse = normalize_parts(middle, 1)
        mid_normed = (mid_hat * mlp_gain[None, :]).astype(jnp.bfloat16)
        pre_act = matmul(mid_normed, mlp_in)
        unused_value, gelu_pull = jax.vjp(gelu_exact, pre_act)
        hidden_low = gelu_exact(pre_act).astype(jnp.bfloat16)
        mixed_rows = middle + matmul(hidden_low, mlp_out)
        mixed_list.append(mixed_rows.astype(jnp.bfloat16))
        grad_rows = mixed_grad[batch_slot]
        grad_hidden = contract(grad_rows, mlp_out, 1, 1).astype(jnp.bfloat16)
        (slope_grad,) = gelu_pull(grad_hidden.astype(jnp.float32))
        grad_pre = slope_grad.astype(jnp.bfloat16)
        grad_mid_normed = contract(grad_pre, mlp_in, 1, 1)
        mlp_gain_acc = mlp_gain_acc + jnp.sum(grad_mid_normed * mid_hat, axis=0)
        grad_mid = (
            grad_rows.astype(jnp.float32)
            + normalize_back(grad_mid_normed * mlp_gain[None, :], mid_hat, mid_inverse, 1)
        ).astype(jnp.bfloat16)
        grad_attended = contract(grad_mid, output_weight, 1, 1).astype(jnp.bfloat16)
        grad_att_value = grad_attended.astype(jnp.float32)
        row_delta = jnp.sum(attended * grad_att_value, axis=1)
        share_by_source = weight_share.T
        grad_numer = (share_by_source[:, :, None] * grad_att_value[None, :, :]).astype(jnp.bfloat16)
        grad_total = (-share_by_source * row_delta[None, :]).astype(jnp.bfloat16)
        out_term = block_outer(attended_low, grad_mid, row_block, col_block)
        in_term = block_outer(mid_normed, grad_pre, row_block, col_block)
        down_term = block_outer(hidden_low, grad_rows, row_block, col_block)
        triple_term = jnp.stack([out_term, in_term, down_term], axis=1)
        residual_acc = residual_acc + grad_mid.astype(jnp.float32)
        back_numer, back_total = (
            lax.all_to_all(grad_numer, "pix", split_axis=0, concat_axis=0, tiled=True),
            lax.all_to_all(grad_total, "pix", split_axis=0, concat_axis=0, tiled=True),
        )
        back_numer = back_numer.reshape(all_rows, model_width)
        back_total = back_total.reshape(all_rows)
        query_term, keyval_term, gain_term, pixel_term = lax.cond(
            has_pixels,
            shard_backward,
            backward_skip,
            image_shard,
            valid_cols,
            keyval,
            shard_top,
            back_numer,
            back_total,
        )
        query_acc = query_acc + query_term
        in_gain_acc = in_gain_acc + gain_term
        pixel_list.append(pixel_term)
        got_triple, got_keyval = (
            lax.psum_scatter(triple_term, ("samp", "pix"), scatter_dimension=0, tiled=True),
            lax.psum_scatter(keyval_term, ("samp", "pix"), scatter_dimension=1, tiled=True),
        )
        triple_owned = triple_owned + got_triple
        keyval_owned = keyval_owned + got_keyval
    query_sum, in_gain_sum, mlp_gain_sum = lax.psum(
        (query_acc, in_gain_acc, mlp_gain_acc), ("samp", "pix")
    )
    grad_query_low = query_sum.astype(jnp.bfloat16)
    grad_lat_normed = contract(grad_query_low, query_weight, 1, 1)
    lat_gain_grad = jnp.sum(grad_lat_normed * lat_hat, axis=0)
    latent_path = normalize_back(grad_lat_normed * lat_gain[None, :], lat_hat, lat_inverse, 1)
    row_start = lax.axis_index("pix") * lat_rows
    own_path = lax.dynamic_slice_in_dim(latent_path, row_start, lat_rows, 0)
    residual_total = lax.psum(residual_acc.astype(jnp.bfloat16), "samp").astype(jnp.float32)
    latent_grad = residual_total + own_path
    first_block = lax.axis_index(("samp", "pix")) * owned_count
    col_count = model_width // col_block
    query_list = []
    for offset in range(owned_count):
        block_index = first_block + offset
        block_row = block_index // col_count * row_block
        block_col = block_index % col_count * col_block
        normed_slice = lax.dynamic_slice_in_dim(lat_normed, block_row, row_block, 1)
        grad_slice = lax.dynamic_slice_in_dim(grad_query_low, block_col, col_block, 1)
        query_list.append(contract(normed_slice, grad_slice, 0, 0))
    query_grad = jnp.stack(query_list, axis=0)
    proj_grad = jnp.concatenate([query_grad[:, None], triple_owned], axis=1)
    left_new = STAT_DECAY * proj_left + (1.0 - STAT_DECAY) * jnp.einsum(
        "nsab,nscb->nsac", proj_grad, proj_grad, precision=HIGHEST
    )
    right_new = STAT_DECAY * proj_right + (1.0 - STAT_DECAY) * jnp.einsum(
        "nsab,nsac->nsbc", proj_grad, proj_grad, precision=HIGHEST
    )
    partial_step = jnp.einsum("nsab,nsbc->nsac", left_roots, proj_grad, precision=HIGHEST)
    direction = jnp.einsum("nsac,nscd->nsad", partial_step, right_roots, precision=HIGHEST)
    proj_new = proj_blocks - MATRIX_RATE * direction
    keyval_second_new, keyval_new = moment_step(
        keyval_weight, keyval_owned, keyval_second, KEYVAL_RATE
    )
    latent_second_new, latent_new = moment_step(latents, latent_grad, latent_second, LATENT_RATE)
    gain_grad = jnp.concatenate([lat_gain_grad, in_gain_sum, mlp_gain_sum], axis=0)
    gain_second_new, gain_new = moment_step(gains, gain_grad, gain_second, GAIN_RATE)
    mixed = jnp.stack(mixed_list, axis=0)
    pixel_grad = jnp.stack(pixel_list, axis=0)
    return (
        mixed,
        pixel_grad,
        proj_grad,
        left_new,
        right_new,
        proj_new,
        keyval_owned,
        keyval_second_new,
        keyval_new,
        latent_grad,
        latent_second_new,
        latent_new,
        gain_grad,
        gain_second_new,
        gain_new,
    )


def solution(mesh):
    placed = (
        P("samp", None, "pix"),
        P("samp", "pix"),
        P(("samp", "pix"), None, None, None),
        P(("samp", "pix"), None, None, None),
        P(("samp", "pix"), None, None, None),
        P(("samp", "pix"), None, None, None),
        P(("samp", "pix"), None, None, None),
        P(None, ("samp", "pix")),
        P(None, ("samp", "pix")),
        P("pix", None),
        P("pix", None),
        P(),
        P(),
        P("samp", "pix", None),
    )
    return jax.shard_map(
        body,
        mesh=mesh,
        in_specs=placed,
        out_specs=(
            P("samp", "pix", None),
            P("samp", None, "pix"),
            P(("samp", "pix"), None, None, None),
            P(("samp", "pix"), None, None, None),
            P(("samp", "pix"), None, None, None),
            P(("samp", "pix"), None, None, None),
            P(None, ("samp", "pix")),
            P(None, ("samp", "pix")),
            P(None, ("samp", "pix")),
            P("pix", None),
            P("pix", None),
            P("pix", None),
            P(),
            P(),
            P(),
        ),
        check_vma=False,
    )
```

profile of v0, /device:TPU:0, one launch (start us, length us, event | category | flops | bytes accessed | tf_op | source)
XLA Modules:
  0.0 995.1 jit_solution(7194930955076245933)
XLA Ops:
  12.5 13.6 %fusion.596 = (bf16[1,261,2048]{2,0,1:T(2,128)(2,1)}, bf16[1,261,2048]{2,0,1:T(2,128)(2,1)}, bf16[1,261,2048]{2,0,1:T(2,128)(2,1)}, bf16[1,261,2048]{2,0,1:T(2,128)(2,1)}) fusion(bf16[4,261,2048]{2,0,1:T(4,128)(2,1)} %param.30), kind=kLoop, calls=%fused_computation.718 | loop fusion | bytes 8552448 | tf_op jit(solution)/shard_map/slice | solution.py:186
  41.3 76.4 %all-gather.8.cloned.1.call-done = bf16[128,4,64,128]{3,2,1,0:T(8,128)(2,1)} async-done(((bf16[4,4,64,128]{3,2,1,0:T(8,128)(2,1)}), bf16[128,4,64,128]{3,2,1,0:T(8,128)(2,1)}) %all-gather.8.cloned.1.call-update) | async-done | bytes 8388624 | tf_op jit(solution)/shard_map/all_gather | solution.py:98
  129.0 45.7 %all-gather.4.cloned.1.call-done = bf16[261,2048]{0,1:T(8,128)(2,1)} async-done(((bf16[261,64]{0,1:T(8,128)(2,1)}), bf16[261,2048]{0,1:T(8,128)(2,1)}) %all-gather.4.cloned.1.call-update) | async-done | bytes 1069072 | tf_op jit(solution)/shard_map/all_gather | solution.py:99
  174.6 20.8 %conditional.11 = (bf16[512,1024]{1,0:T(8,128)(2,1)}, bf16[512]{0:T(512)(128)(2,1)}, bf16[512]{0:T(512)(128)(2,1)S(1)}, bf16[2048,2048]{1,0:T(8,128)(2,1)}) conditional(s32[]{:T(128)} %convert_element_type.532, () %tuple.86, (pred[2048]{0:T(1024)(128)(4,1)S(1)}, bf16[261,2048]{1,0:T(8,128)(2,1)S(1)}, f32[261]{0:T(512)S(1)}, ...), branch_computations={%region_36.37_spmd, %region_37.42_spmd} | conditional | flops 6506528256 | bytes 44294252 | solution.py:189
  176.2 7.1 convolution_convert_fusion.3
  213.2 20.9 %conditional.10 = (bf16[512,1024]{1,0:T(8,128)(2,1)}, bf16[512]{0:T(512)(128)(2,1)}, bf16[512]{0:T(512)(128)(2,1)S(1)}, bf16[2048,2048]{1,0:T(8,128)(2,1)}) conditional(s32[]{:T(128)} %convert_element_type.523, () %tuple.84, (pred[2048]{0:T(1024)(128)(4,1)S(1)}, bf16[261,2048]{1,0:T(8,128)(2,1)S(1)}, f32[261]{0:T(512)S(1)}, ...), branch_computations={%region_25.26_spmd, %region_26.31_spmd} | conditional | flops 6506528256 | bytes 44294252 | solution.py:189
  214.8 7.1 convolution_convert_fusion.2
  255.6 20.1 %conditional.8 = (bf16[512,1024]{1,0:T(8,128)(2,1)}, bf16[512]{0:T(512)(128)(2,1)}, bf16[512]{0:T(512)(128)(2,1)S(1)}, bf16[2048,2048]{1,0:T(8,128)(2,1)}) conditional(s32[]{:T(128)} %convert_element_type.499, () %tuple.80, (pred[2048]{0:T(1024)(128)(4,1)S(1)}, bf16[261,2048]{1,0:T(8,128)(2,1)S(1)}, f32[261]{0:T(512)S(1)}, ...), branch_computations={%region_3.0_spmd, %region_4.9_spmd} | conditional | flops 6506528256 | bytes 35823668 | solution.py:189
  256.5 7.2 convolution_convert_fusion
  290.2 20.1 %conditional.9 = (bf16[512,1024]{1,0:T(8,128)(2,1)}, bf16[512]{0:T(512)(128)(2,1)}, bf16[512]{0:T(512)(128)(2,1)S(1)}, bf16[2048,2048]{1,0:T(8,128)(2,1)}) conditional(s32[]{:T(128)} %convert_element_type.514, () %tuple.82, (pred[2048]{0:T(1024)(128)(4,1)S(1)}, bf16[261,2048]{1,0:T(8,128)(2,1)S(1)}, f32[261]{0:T(512)S(1)}, ...), branch_computations={%region_14.15_spmd, %region_15.20_spmd} | conditional | flops 6506528256 | bytes 35823668 | solution.py:189
  290.9 7.2 convolution_convert_fusion.1
  344.9 10.7 %all-to-all-done.10 = bf16[8,64,1024]{2,1,0:T(8,128)(2,1)} async-done(((bf16[8,64,1024]{2,1,0:T(8,128)(2,1)}), bf16[8,64,1024]{2,1,0:T(8,128)(2,1)}, u32[]{:S(2)}, u32[]{:S(2)}) %all-to-all-start.10) | async-done | bytes 1048608 | tf_op jit(solution)/shard_map/all_to_all | solution.py:197
  366.8 8.5 all-to-all-done.7
  387.2 7.7 all-to-all-done.1
  509.2 8.9 all-to-all-done.14
  529.9 7.0 all-to-all-done.16
  549.2 39.5 %conditional.12 = (f32[512,1024]{1,0:T(8,128)}, f32[261,2048]{1,0:T(8,128)}, f32[261]{0:T(512)S(1)}, f32[1,261,2048]{2,0,1:T(1,128)S(1)}) conditional(s32[]{:T(128)} %convert_element_type.499, () %tuple.88, (pred[2048]{0:T(1024)(128)(4,1)S(1)}, bf16[2048,2048]{1,0:T(8,128)(2,1)}, bf16[512,1024]{1,0:T(8,128)(2,1)S(1)}, bf16[512]{0:T(512)(128)(2,1)}, ...), branch_computations={%region_49.50_spmd, %region_50.56_spmd} | conditional | flops 15182097408 | bytes 120348904 | solution.py:244
  590.0 39.4 %conditional.13 = (f32[512,1024]{1,0:T(8,128)}, f32[261,2048]{1,0:T(8,128)}, f32[261]{0:T(512)S(1)}, f32[1,261,2048]{2,0,1:T(1,128)S(1)}) conditional(s32[]{:T(128)} %convert_element_type.514, () %tuple.90, (pred[2048]{0:T(1024)(128)(4,1)S(1)}, bf16[2048,2048]{1,0:T(8,128)(2,1)}, bf16[512,1024]{1,0:T(8,128)(2,1)}, bf16[512]{0:T(512)(128)(2,1)}, ...), branch_computations={%region_59.60_spmd, %region_60.66_spmd} | conditional | flops 15182097408 | bytes 120348904 | solution.py:244
  630.9 37.8 %conditional.14 = (f32[512,1024]{1,0:T(8,128)}, f32[261,2048]{1,0:T(8,128)}, f32[261]{0:T(512)S(1)}, f32[1,261,2048]{2,0,1:T(1,128)}) conditional(s32[]{:T(128)} %convert_element_type.523, () %tuple.92, (pred[2048]{0:T(1024)(128)(4,1)S(1)}, bf16[2048,2048]{1,0:T(8,128)(2,1)}, bf16[512,1024]{1,0:T(8,128)(2,1)}, bf16[512]{0:T(512)(128)(2,1)}, ...), branch_computations={%region_69.0_spmd, %region_70.76_spmd} | conditional | flops 15182097408 | bytes 115990768 | solution.py:244
  668.7 39.7 %conditional.15 = (f32[512,1024]{1,0:T(8,128)}, f32[261,2048]{1,0:T(8,128)S(1)}, f32[261]{0:T(512)S(1)}, f32[1,261,2048]{2,0,1:T(1,128)S(1)}) conditional(s32[]{:T(128)} %convert_element_type.532, () %tuple.94, (pred[2048]{0:T(1024)(128)(4,1)S(1)}, bf16[2048,2048]{1,0:T(8,128)(2,1)}, bf16[512,1024]{1,0:T(8,128)(2,1)}, bf16[512]{0:T(512)(128)(2,1)}, ...), branch_computations={%region_79.0_spmd, %region_80.86_spmd} | conditional | flops 15182097408 | bytes 124707064 | solution.py:244
  756.3 15.6 %fusion.273 = f32[128,3,64,128]{3,2,1,0:T(8,128)} fusion(f32[128,1,64,128]{3,2,1,0:T(8,128)S(1)} %bitcast.621, f32[128,1,64,128]{3,2,1,0:T(8,128)} %bitcast.619, f32[128,1,64,128]{3,2,1,0:T(8,128)} %bitcast.618, f32[128,1,64,128]{3,2,1,0:T(8,128)S(1)} %bitcast.612, f32[128,1,64,128]{3,2,1,0:T(8,128)S(1)} %bitcast.614, f32[128,1,64,128]{3,2,1,0:T(8,128)S(1)} %bitcast.613, ...), kind=kLoop, calls=%fused_computation.306 | loop fusion | flops 34603008 | bytes 62914560 | tf_op jit(solution)/shard_map/add | solution.py:262
  786.1 70.1 %all-reduce.5 = (bf16[512,1024]{1,0:T(8,128)(2,1)S(1)}, f32[261]{0:T(512)S(1)}, f32[1024]{0:T(1024)S(1)}) all-reduce(f32[512,1024]{1,0:T(8,128)} %add_add_fusion.1, f32[261]{0:T(512)S(1)} %add_add_fusion.3, f32[1024]{0:T(1024)S(1)} %add_add_fusion.2), channel_id=1, replica_groups=mesh['samp'=4,'pix'=8] {'samp','pix'}, use_global_device_ids=true, to_apply=%region_86.87 | all-reduce | flops 525573 | bytes 3156008 | tf_op jit(solution)/shard_map/psum | solution.py:264
  871.7 11.1 %pad_maximum_fusion.20 = f32[4,261,2048]{2,0,1:T(4,128)} fusion(f32[1,261,2048]{2,0,1:T(1,128)} %copy-done.35, f32[1,261,2048]{2,0,1:T(1,128)} %get-tuple-element.551, f32[1,261,2048]{2,0,1:T(1,128)} %copy-done.33, f32[1,261,2048]{2,0,1:T(1,128)S(1)} %copy-done.31), kind=kLoop, calls=%fused_computation.307 | loop fusion | flops 6414336 | bytes 17104896 | tf_op jit(solution)/shard_map/stack | solution.py:303
  886.4 93.4 %reduce-scatter.5.cloned.1.call-done = f32[4,3,64,128]{3,2,1,0:T(8,128)} async-done(((f32[128,3,64,128]{3,2,1,0:T(8,128)}), f32[4,3,64,128]{3,2,1,0:T(8,128)}) %reduce-scatter.5.cloned.1.call-update) | async-done | bytes 393232 | tf_op jit(solution)/shard_map/reduce_scatter | solution.py:259
  (739 shorter events, 576.1 us)
Async XLA Ops:
  7.2 29.5 %all-gather.6.cloned.1.call-start = ((), (), s32[]{:S(2)}) async-start(), calls=%async_computation.23 | async-start | bytes 1179648 | tf_op jit(solution)/shard_map/all_gather | solution.py:105
  9.0 108.7 %all-gather.8.cloned.1.call-start = ((), (), s32[]{:S(2)}) async-start(), calls=%async_computation.24 | async-start | bytes 8650752 | tf_op jit(solution)/shard_map/all_gather | solution.py:98
  10.8 163.8 %all-gather.4.cloned.1.call-start = ((), (), s32[]{:S(2)}) async-start(), calls=%async_computation.22 | async-start | bytes 1622016 | tf_op jit(solution)/shard_map/all_gather | solution.py:99
  196.8 7.8 all-to-all-start.9
  204.6 30.8 %all-to-all-start.11 = ((bf16[8,1,64]{2,1,0:T(2,128)(2,1)}), bf16[8,1,64]{2,1,0:T(2,128)(2,1)S(1)}, u32[]{:S(2)}, u32[]{:S(2)}) async-start(bf16[8,1,64]{2,1,0:T(2,128)(2,1)} %all_to_all.123), calls=%async_computation.11 | async-start | bytes 8192 | tf_op jit(solution)/shard_map/all_to_all | solution.py:199
  235.4 8.7 all-to-all-start.6
  244.1 32.9 %all-to-all-start.8 = ((bf16[8,1,64]{2,1,0:T(2,128)(2,1)}), bf16[8,1,64]{2,1,0:T(2,128)(2,1)S(1)}, u32[]{:S(2)}, u32[]{:S(2)}) async-start(bf16[8,1,64]{2,1,0:T(2,128)(2,1)} %all_to_all.121), calls=%async_computation.8 | async-start | bytes 8192 | tf_op jit(solution)/shard_map/all_to_all | solution.py:199
  277.0 35.3 %all-to-all-start = ((bf16[8,1,64]{2,1,0:T(2,128)(2,1)}), bf16[8,1,64]{2,1,0:T(2,128)(2,1)S(1)}, u32[]{:S(2)}, u32[]{:S(2)}) async-start(bf16[8,1,64]{2,1,0:T(2,128)(2,1)} %all_to_all.116), calls=%async_computation | async-start | bytes 8192 | tf_op jit(solution)/shard_map/all_to_all | solution.py:198
  312.3 7.9 all-to-all-start.2
  320.2 7.8 all-to-all-start.3
  328.0 7.8 all-to-all-start.5
  335.9 19.7 %all-to-all-start.10 = ((bf16[8,64,1024]{2,1,0:T(8,128)(2,1)}), bf16[8,64,1024]{2,1,0:T(8,128)(2,1)}, u32[]{:S(2)}, u32[]{:S(2)}) async-start(bf16[8,64,1024]{2,1,0:T(8,128)(2,1)} %bitcast.44), calls=%async_computation.10 | async-start | bytes 2097152 | tf_op jit(solution)/shard_map/all_to_all | solution.py:197
  355.6 19.7 %all-to-all-start.7 = ((bf16[8,64,1024]{2,1,0:T(8,128)(2,1)}), bf16[8,64,1024]{2,1,0:T(8,128)(2,1)}, u32[]{:S(2)}, u32[]{:S(2)}) async-start(bf16[8,64,1024]{2,1,0:T(8,128)(2,1)} %bitcast.37), calls=%async_computation.7 | async-start | bytes 2097152 | tf_op jit(solution)/shard_map/all_to_all | solution.py:197
  375.3 19.7 %all-to-all-start.1 = ((bf16[8,64,1024]{2,1,0:T(8,128)(2,1)}), bf16[8,64,1024]{2,1,0:T(8,128)(2,1)}, u32[]{:S(2)}, u32[]{:S(2)}) async-start(bf16[8,64,1024]{2,1,0:T(8,128)(2,1)} %bitcast.17), calls=%async_computation.1 | async-start | bytes 2097152 | tf_op jit(solution)/shard_map/all_to_all | solution.py:197
  395.0 21.1 %all-to-all-start.4 = ((bf16[8,64,1024]{2,1,0:T(8,128)(2,1)}), bf16[8,64,1024]{2,1,0:T(8,128)(2,1)}, u32[]{:S(2)}, u32[]{:S(2)}) async-start(bf16[8,64,1024]{2,1,0:T(8,128)(2,1)} %bitcast.30), calls=%async_computation.4 | async-start | bytes 2097152 | tf_op jit(solution)/shard_map/all_to_all | solution.py:197
  435.0 12.7 %all-to-all-start.13 = ((bf16[8,1,64]{2,1,0:T(2,128)(2,1)}), bf16[8,1,64]{2,1,0:T(2,128)(2,1)}, u32[]{:S(2)}, u32[]{:S(2)}) async-start(bf16[8,1,64]{2,1,0:T(2,128)(2,1)} %copy.413), calls=%async_computation.13 | async-start | bytes 8192 | tf_op jit(solution)/shard_map/all_to_all | solution.py:240
  447.7 8.8 all-to-all-start.15
  473.3 24.9 %all-to-all-start.12 = ((bf16[8,64,1024]{2,1,0:T(8,128)(2,1)}), bf16[8,64,1024]{2,1,0:T(8,128)(2,1)}, u32[]{:S(2)}, u32[]{:S(2)}) async-start(bf16[8,64,1024]{2,1,0:T(8,128)(2,1)} %multiply_convert_fusion.11), calls=%async_computation.12 | async-start | bytes 2097152 | tf_op jit(solution)/shard_map/all_to_all | solution.py:239
  477.6 391.8 %all-reduce.4.cloned.1.call-start = ((), (), s32[]{:S(2)}) async-start(), calls=%async_computation.25 | async-start | bytes 262144 | tf_op jit(solution)/shard_map/psum | solution.py:273
  498.3 19.8 %all-to-all-start.14 = ((bf16[8,64,1024]{2,1,0:T(8,128)(2,1)}), bf16[8,64,1024]{2,1,0:T(8,128)(2,1)}, u32[]{:S(2)}, u32[]{:S(2)}) async-start(bf16[8,64,1024]{2,1,0:T(8,128)(2,1)} %multiply_convert_fusion.10), calls=%async_computation.14 | async-start | bytes 2097152 | tf_op jit(solution)/shard_map/all_to_all | solution.py:239
  518.1 18.9 %all-to-all-start.16 = ((bf16[8,64,1024]{2,1,0:T(8,128)(2,1)}), bf16[8,64,1024]{2,1,0:T(8,128)(2,1)S(1)}, u32[]{:S(2)}, u32[]{:S(2)}) async-start(bf16[8,64,1024]{2,1,0:T(8,128)(2,1)} %multiply_convert_fusion.9), calls=%async_computation.16 | async-start | bytes 2097152 | tf_op jit(solution)/shard_map/all_to_all | solution.py:239
  537.0 131.7 %all-to-all-start.18 = ((bf16[8,64,1024]{2,1,0:T(8,128)(2,1)}), bf16[8,64,1024]{2,1,0:T(8,128)(2,1)}, u32[]{:S(2)}, u32[]{:S(2)}) async-start(bf16[8,64,1024]{2,1,0:T(8,128)(2,1)} %multiply_convert_fusion.8), calls=%async_computation.18 | async-start | bytes 2097152 | tf_op jit(solution)/shard_map/all_to_all | solution.py:239
  541.2 341.6 %reduce-scatter.7.cloned.1.call-start = ((), (), s32[]{:S(2)}) async-start(), calls=%async_computation.27 | async-start | bytes 3244032
  715.9 264.0 %reduce-scatter.5.cloned.1.call-start = ((), (), s32[]{:S(2)}) async-start(), calls=%async_computation.26 | async-start | bytes 12976128 | tf_op jit(solution)/shard_map/reduce_scatter | solution.py:259
  (200 other events, 4448.6 us)
Sparse Core Ops, SparseCore 0:
  10.5 26.1 all-gather.5
  40.1 77.4 all-gather.7
  121.1 53.5 all-gather.3
  480.8 35.4 all-reduce.3
  716.0 101.7 reduce-scatter.6
  824.8 155.0 reduce-scatter.4
where the time goes:
time: 1000 us; the launch traced here: 995 us
  matrix products  298 us (30%)
  waiting for transfers between devices  292 us (29%)
  local copies, waits for them, and re-layouts  147 us (15%)
  other arithmetic  89.1 us (9%)
  starting transfers between devices  77.2 us (8%)
  blocking collectives  70.1 us (7%)
  between operations  19.1 us (2%)
    dot_general x45, matrix products, contract(): lax.dot_general(former, latter, (((former_dim,), (latter_dim,)), ((), ())...  169 us
    reduce_scatter x1, waiting for transfers between devices, body(): lax.psum_scatter(triple_term, ('samp', 'pix'), scatter_dimension=0, tiled...  93.4 us
    dot_general x25, matrix products, matmul(): return jnp.dot(former, latter, preferred_element_type=jnp.float32)  83.8 us
    all_gather x1, waiting for transfers between devices, body(): lax.all_gather(proj_blocks.astype(jnp.bfloat16), ('samp', 'pix'), axis=0,...  76.4 us
    psum x1, blocking collectives, body(): lax.psum((query_acc, in_gain_acc, mlp_gain_acc), ('samp', 'pix'))  70.1 us
    unnamed x367, local copies, waits for them, and re-layouts  48.9 us
    all_gather x1, waiting for transfers between devices, body(): lax.all_gather(keyval_weight.astype(jnp.bfloat16), ('samp', 'pix'), axis=...  45.7 us
    dot_general x12, matrix products, block_outer(): jnp.einsum('rxa,ryb->xyab', left_blocks, right_blocks, preferred_element_...  29.8 us
  transfers between devices with their start and end apart: 26, of which 17 were waited for; matrix products, arithmetic and copies ran while one was open for 45% of the time, Pallas kernels for 0%

commit v1 on v0

v1 whole, which is shorter than its diff:
```python
import jax
import jax.numpy as jnp
from jax import lax
from jax.sharding import PartitionSpec as P

EPSILON = 1e-05
NEGATIVE = -1e30
HIGHEST = lax.Precision.HIGHEST
STAT_DECAY = 0.5
MATRIX_RATE = 0.5
KEYVAL_RATE = 0.05
LATENT_RATE = 0.7
GAIN_RATE = 0.6
MOMENT_FLOOR = 1e-08
BF = jnp.bfloat16


def matmul(former, latter):
    return jnp.dot(former, latter, preferred_element_type=jnp.float32)


def contract(former, latter, former_dim, latter_dim):
    return lax.dot_general(
        former,
        latter,
        (((former_dim,), (latter_dim,)), ((), ())),
        preferred_element_type=jnp.float32,
    )


def gelu_exact(values):
    return jax.nn.gelu(values, approximate=False)


def normalize_parts(values, axis):
    row_mean = jnp.mean(values, axis=axis, keepdims=True)
    centered = values - row_mean
    variance = jnp.mean(centered * centered, axis=axis, keepdims=True)
    inverse = lax.rsqrt(variance + EPSILON)
    return (centered * inverse, inverse)


def normalize_back(grad_hat, normal_hat, inverse, axis):
    first_mean = jnp.mean(grad_hat, axis=axis, keepdims=True)
    second_mean = jnp.mean(grad_hat * normal_hat, axis=axis, keepdims=True)
    return inverse * (grad_hat - first_mean - normal_hat * second_mean)


def assemble(blocks, model_width, row_block, col_block):
    shaped = blocks.reshape(
        model_width // row_block, model_width // col_block, row_block, col_block
    )
    return shaped.transpose(0, 2, 1, 3).reshape(model_width, model_width)


def split_blocks(matrix, row_block, col_block):
    rows, cols = matrix.shape
    shaped = matrix.reshape(rows // row_block, row_block, cols // col_block, col_block)
    return shaped.transpose(0, 2, 1, 3).reshape(-1, row_block, col_block)


def moment_step(weight, grad, second, rate):
    second_new = STAT_DECAY * second + (1.0 - STAT_DECAY) * grad * grad
    return (second_new, weight - rate * grad / (jnp.sqrt(second_new) + MOMENT_FLOOR))


def body(
    pixels,
    pixel_mask,
    proj_blocks,
    proj_left,
    proj_right,
    left_roots,
    right_roots,
    keyval_weight,
    keyval_second,
    latents,
    latent_second,
    gains,
    gain_second,
    mixed_grad,
):
    batches, channels, shard_pixels = pixels.shape
    lat_rows, width = latents.shape
    groups = lax.axis_size("pix")
    all_rows = lat_rows * groups
    owned_count, _, row_block, col_block = proj_blocks.shape
    scale = width ** (-0.5)
    everyone = ("samp", "pix")

    latent_all = lax.all_gather(latents.astype(BF), "pix", axis=0, tiled=True).astype(jnp.float32)
    query_blocks = lax.all_gather(proj_blocks[:, 0].astype(BF), everyone, axis=0, tiled=True)
    keyval_t = lax.all_gather(keyval_weight.T.astype(BF), everyone, axis=0, tiled=True)
    rest_blocks = lax.all_gather(proj_blocks[:, 1:].astype(BF), everyone, axis=0, tiled=True)
    query_weight = assemble(query_blocks, width, row_block, col_block)
    output_weight = assemble(rest_blocks[:, 0], width, row_block, col_block)
    mlp_in = assemble(rest_blocks[:, 1], width, row_block, col_block)
    mlp_out = assemble(rest_blocks[:, 2], width, row_block, col_block)
    key_t = keyval_t[:width]
    value_t = keyval_t[width:]
    lat_gain = gains[:width]
    in_gain = gains[width : width + channels]
    mlp_gain = gains[width + channels :]
    lat_hat, lat_inverse = normalize_parts(latent_all, 1)
    lat_normed = (lat_hat * lat_gain[None, :]).astype(BF)
    query = matmul(lat_normed, query_weight).astype(BF)
    pixel_query = (matmul(query, key_t) * scale).astype(BF)

    kept = []
    packed = []
    for slot in range(batches):
        normal_hat, inverse = normalize_parts(pixels[slot].astype(jnp.float32), 0)
        normed = (normal_hat * in_gain[:, None]).astype(BF)
        valid = pixel_mask[slot] == 1
        scores = jnp.where(valid[None, :], matmul(pixel_query, normed), NEGATIVE)
        top = jnp.max(scores, axis=1).astype(BF)
        weights = jnp.where(
            valid[None, :], jnp.exp(scores - top.astype(jnp.float32)[:, None]), 0.0
        )
        total = jnp.sum(weights, axis=1).astype(BF)
        weights = weights.astype(BF)
        numer = contract(weights, normed, 1, 1).astype(BF)
        kept.append((normed, top, weights))
        packed.append(jnp.concatenate([numer, top[:, None], total[:, None]], axis=1))
    outgoing = jnp.stack(packed, axis=0).reshape(batches, groups, lat_rows, channels + 2)
    outgoing = outgoing.transpose(1, 0, 2, 3).reshape(groups, batches * lat_rows, channels + 2)
    incoming = lax.all_to_all(outgoing, "pix", split_axis=0, concat_axis=0, tiled=True)
    top_in = incoming[:, :, channels].astype(jnp.float32)
    total_in = incoming[:, :, channels + 1].astype(jnp.float32)
    peak = jnp.max(top_in, axis=0)
    factor = jnp.exp(top_in - peak[None, :])
    denominator = jnp.sum(factor * total_in, axis=0)
    summed = jnp.sum(factor[:, :, None] * incoming[:, :, :channels].astype(jnp.float32), axis=0)
    attended_chan = (summed / denominator[:, None]).astype(BF)

    attended = contract(attended_chan, value_t, 1, 1)
    attended_low = attended.astype(BF)
    latents_tiled = jnp.tile(latents, (batches, 1))
    middle = latents_tiled + matmul(attended_low, output_weight)
    mid_hat, mid_inverse = normalize_parts(middle, 1)
    mid_normed = (mid_hat * mlp_gain[None, :]).astype(BF)
    pre_act = matmul(mid_normed, mlp_in)
    hidden, gelu_pull = jax.vjp(gelu_exact, pre_act)
    hidden_low = hidden.astype(BF)
    mixed = (middle + matmul(hidden_low, mlp_out)).astype(BF)
    grad_rows = mixed_grad.reshape(batches * lat_rows, width)
    grad_hidden = contract(grad_rows, mlp_out, 1, 1).astype(BF)
    (slope_grad,) = gelu_pull(grad_hidden.astype(jnp.float32))
    grad_pre = slope_grad.astype(BF)
    grad_mid_normed = contract(grad_pre, mlp_in, 1, 1)
    mlp_gain_part = jnp.sum(grad_mid_normed * mid_hat, axis=0)
    grad_mid = (
        grad_rows.astype(jnp.float32)
        + normalize_back(grad_mid_normed * mlp_gain[None, :], mid_hat, mid_inverse, 1)
    ).astype(BF)
    grad_attended = contract(grad_mid, output_weight, 1, 1).astype(BF)
    row_delta = jnp.sum(attended * grad_attended.astype(jnp.float32), axis=1)
    grad_chan = (matmul(grad_attended, value_t) / denominator[:, None]).astype(BF)
    delta_low = (row_delta / denominator).astype(BF)
    back_own = jnp.concatenate([grad_chan, peak.astype(BF)[:, None], delta_low[:, None]], axis=1)
    back_own = back_own.reshape(batches, lat_rows, channels + 2)
    back_all = lax.all_gather(back_own, "pix", axis=1, tiled=True)

    out_term = split_blocks(contract(attended_low, grad_mid, 0, 0).astype(BF), row_block, col_block)
    in_term = split_blocks(contract(mid_normed, grad_pre, 0, 0).astype(BF), row_block, col_block)
    down_term = split_blocks(contract(hidden_low, grad_rows, 0, 0).astype(BF), row_block, col_block)
    triple_term = jnp.stack([out_term, in_term, down_term], axis=1)
    triple_owned = lax.psum_scatter(triple_term, everyone, scatter_dimension=0, tiled=True)
    residual = jnp.sum(grad_mid.astype(jnp.float32).reshape(batches, lat_rows, width), axis=0)
    residual_total = lax.psum(residual.astype(BF), "samp").astype(jnp.float32)

    query_acc = jnp.zeros((all_rows, channels), jnp.float32)
    in_gain_part = jnp.zeros((channels,), jnp.float32)
    pixel_list = []
    for slot in range(batches):
        normed, top, weights = kept[slot]
        back = back_all[slot]
        share = jnp.exp(top.astype(jnp.float32) - back[:, channels].astype(jnp.float32))
        back_chan = (back[:, :channels].astype(jnp.float32) * share[:, None]).astype(BF)
        back_total = share * back[:, channels + 1].astype(jnp.float32)
        grad_weights = matmul(back_chan, normed) - back_total[:, None]
        grad_scores = (weights.astype(jnp.float32) * grad_weights).astype(BF)
        query_acc = query_acc + contract(grad_scores, normed, 1, 1)
        grad_normed = contract(pixel_query, grad_scores, 0, 0) + contract(back_chan, weights, 0, 0)
        normal_hat, inverse = normalize_parts(pixels[slot].astype(jnp.float32), 0)
        in_gain_part = in_gain_part + jnp.sum(grad_normed * normal_hat, axis=1)
        pixel_list.append(
            normalize_back(grad_normed * in_gain[:, None], normal_hat, inverse, 0)
        )
    pixel_grad = jnp.stack(pixel_list, axis=0)

    query_sum, in_gain_sum, mlp_gain_sum = lax.psum(
        (query_acc, in_gain_part, mlp_gain_part), everyone
    )
    value_term = contract(grad_attended, attended_chan, 0, 0)
    key_term = contract(query, query_acc.astype(BF), 0, 0) * scale
    keyval_term = jnp.concatenate([key_term, value_term], axis=0).astype(BF)
    keyval_grad = lax.psum_scatter(keyval_term, everyone, scatter_dimension=0, tiled=True)
    keyval_grad = keyval_grad.astype(jnp.float32).T

    grad_query = (contract(query_sum.astype(BF), key_t, 1, 1) * scale).astype(BF)
    grad_lat_normed = contract(grad_query, query_weight, 1, 1)
    lat_gain_grad = jnp.sum(grad_lat_normed * lat_hat, axis=0)
    latent_path = normalize_back(grad_lat_normed * lat_gain[None, :], lat_hat, lat_inverse, 1)
    row_start = lax.axis_index("pix") * lat_rows
    own_path = lax.dynamic_slice_in_dim(latent_path, row_start, lat_rows, 0)
    latent_grad = residual_total + own_path
    first_block = lax.axis_index(everyone) * owned_count
    col_count = width // col_block
    query_list = []
    for offset in range(owned_count):
        block_index = first_block + offset
        block_row = block_index // col_count * row_block
        block_col = block_index % col_count * col_block
        normed_slice = lax.dynamic_slice_in_dim(lat_normed, block_row, row_block, 1)
        grad_slice = lax.dynamic_slice_in_dim(grad_query, block_col, col_block, 1)
        query_list.append(contract(normed_slice, grad_slice, 0, 0))
    query_grad = jnp.stack(query_list, axis=0)
    proj_grad = jnp.concatenate([query_grad[:, None], triple_owned.astype(jnp.float32)], axis=1)
    left_new = STAT_DECAY * proj_left + (1.0 - STAT_DECAY) * jnp.einsum(
        "nsab,nscb->nsac", proj_grad, proj_grad, precision=HIGHEST
    )
    right_new = STAT_DECAY * proj_right + (1.0 - STAT_DECAY) * jnp.einsum(
        "nsab,nsac->nsbc", proj_grad, proj_grad, precision=HIGHEST
    )
    partial_step = jnp.einsum("nsab,nsbc->nsac", left_roots, proj_grad, precision=HIGHEST)
    direction = jnp.einsum("nsac,nscd->nsad", partial_step, right_roots, precision=HIGHEST)
    proj_new = proj_blocks - MATRIX_RATE * direction
    keyval_second_new, keyval_new = moment_step(
        keyval_weight, keyval_grad, keyval_second, KEYVAL_RATE
    )
    latent_second_new, latent_new = moment_step(latents, latent_grad, latent_second, LATENT_RATE)
    gain_grad = jnp.concatenate([lat_gain_grad, in_gain_sum, mlp_gain_sum], axis=0)
    gain_second_new, gain_new = moment_step(gains, gain_grad, gain_second, GAIN_RATE)
    return (
        mixed.reshape(batches, lat_rows, width),
        pixel_grad,
        proj_grad,
        left_new,
        right_new,
        proj_new,
        keyval_grad,
        keyval_second_new,
        keyval_new,
        latent_grad,
        latent_second_new,
        latent_new,
        gain_grad,
        gain_second_new,
        gain_new,
    )


def solution(mesh):
    blocks = P(("samp", "pix"), None, None, None)
    columns = P(None, ("samp", "pix"))
    rows = P("pix", None)
    return jax.shard_map(
        body,
        mesh=mesh,
        in_specs=(
            P("samp", None, "pix"),
            P("samp", "pix"),
            blocks,
            blocks,
            blocks,
            blocks,
            blocks,
            columns,
            columns,
            rows,
            rows,
            P(),
            P(),
            P("samp", "pix", None),
        ),
        out_specs=(
            P("samp", "pix", None),
            P("samp", None, "pix"),
            blocks,
            blocks,
            blocks,
            blocks,
            columns,
            columns,
            columns,
            rows,
            rows,
            rows,
            P(),
            P(),
            P(),
        ),
        check_vma=False,
    )
```

time: 1000 us -> 584 us (0.58)
  matrix products: 298 us -> 93.5 us
  starting transfers between devices: 77.2 us -> 0.91 us
  waiting for transfers between devices: 292 us -> 230 us
  local copies, waits for them, and re-layouts: 147 us -> 115 us
  other arithmetic: 89.1 us -> 57.1 us
    dot_general x45 -> x31, matrix products: 169 us -> 48.7 us  [contract(): lax.dot_general(former, latter, (((former_dim,), (latter_dim,)), ((), ())...]
    all_to_all x20 -> x0, starting transfers between devices: 76.9 us -> none  [the longest x4 17.4 us: body(): lax.all_to_all(outgoing[0], 'pix', split_axis=0, concat_axis=0, tiled=True)]
    all_to_all x20 -> x0, waiting for transfers between devices: 71.1 us -> none  [the longest x4 26.9 us: body(): lax.all_to_all(outgoing[0], 'pix', split_axis=0, concat_axis=0, tiled=True)]
    dot_general x25 -> x14, matrix products: 83.8 us -> 37.8 us  [matmul(): return jnp.dot(former, latter, preferred_element_type=jnp.float32)]
    dot_general x16 -> x0, matrix products: 38.1 us -> none  [the longest x12 29.8 us: block_outer(): jnp.einsum('rxa,ryb->xyab', left_blocks, right_blocks, preferred_element_...]
    add x5 -> x1, other arithmetic: 25.4 us -> 0.01 us  [body(): in_gain_part = in_gain_part + jnp.sum(grad_normed * normal_hat, axis=1)]
    reduce_scatter x1, waiting for transfers between devices: 93.4 us -> 117 us  [body(): lax.psum_scatter(triple_term, everyone, scatter_dimension=0, tiled=True)]
    psum x1, blocking collectives: 70.1 us -> 48 us  [body(): lax.psum((query_acc, in_gain_part, mlp_gain_part), everyone)]
  transfers between devices with their start and end apart: 26 -> 8, of which waited for: 17 -> 5; matrix products, arithmetic and copies ran while one was open for 45% -> 37% of each run, Pallas kernels for 0% -> 0%
where the time goes in v1:
time: 584 us; the launch traced here: 580 us
  waiting for transfers between devices  230 us (39%)
  local copies, waits for them, and re-layouts  115 us (20%)
  matrix products  93.5 us (16%)
  blocking collectives  67.2 us (12%)
  other arithmetic  57.1 us (10%)
  between operations  16.1 us (3%)
    reduce_scatter x1, waiting for transfers between devices, body(): lax.psum_scatter(triple_term, everyone, scatter_dimension=0, tiled=True)  117 us
    all_gather x1, waiting for transfers between devices, body(): lax.all_gather(proj_blocks[:, 0].astype(BF), everyone, axis=0, tiled=True)  55.3 us
    all_gather x1, waiting for transfers between devices, body(): lax.all_gather(keyval_weight.T.astype(BF), everyone, axis=0, tiled=True)  50.2 us
    dot_general x31, matrix products, contract(): lax.dot_general(former, latter, (((former_dim,), (latter_dim,)), ((), ())...  48.7 us
    psum x1, blocking collectives, body(): lax.psum((query_acc, in_gain_part, mlp_gain_part), everyone)  48 us
    unnamed x245, local copies, waits for them, and re-layouts  43.1 us
    dot_general x14, matrix products, matmul(): return jnp.dot(former, latter, preferred_element_type=jnp.float32)  37.8 us
    all_to_all x1, blocking collectives, body(): lax.all_to_all(outgoing, 'pix', split_axis=0, concat_axis=0, tiled=True)  19.2 us
  transfers between devices with their start and end apart: 8, of which 5 were waited for; matrix products, arithmetic and copies ran while one was open for 37% of the time, Pallas kernels for 0%

profile of v1, /device:TPU:0, one launch (start us, length us, event | category | flops | bytes accessed | tf_op | source)
XLA Modules:
  0.0 579.5 jit_solution(16156354770857035918)
XLA Ops:
  14.5 12.4 %fusion.206 = (bf16[1,261,2048]{2,0,1:T(2,128)(2,1)S(1)}, bf16[1,261,2048]{2,0,1:T(2,128)(2,1)S(1)}, bf16[1,261,2048]{2,0,1:T(2,128)(2,1)S(1)}, bf16[1,261,2048]{2,0,1:T(2,128)(2,1)S(1)}) fusion(bf16[4,261,2048]{2,0,1:T(4,128)(2,1)} %param.14), kind=kLoop, calls=%fused_computation.312 | loop fusion | bytes 8552448 | tf_op jit(solution)/shard_map/slice | solution.py:112
  33.5 3.2 all-gather.7.cloned.1.call-done
  41.3 55.3 %all-gather.15.cloned.1.call-done = bf16[128,1,64,128]{3,2,1,0:T(8,128)(2,1)} async-done(((bf16[4,1,64,128]{3,2,1,0:T(8,128)(2,1)}), bf16[128,1,64,128]{3,2,1,0:T(8,128)(2,1)}) %all-gather.15.cloned.1.call-update) | async-done | bytes 2097168 | tf_op jit(solution)/shard_map/all_gather | solution.py:92
  96.6 3.4 copy.110
  103.7 50.2 %all-gather.9.cloned.1.call-done = bf16[2048,261]{1,0:T(8,128)(2,1)} async-done(((bf16[64,261]{1,0:T(8,128)(2,1)}), bf16[2048,261]{1,0:T(8,128)(2,1)}) %all-gather.9.cloned.1.call-update) | async-done | bytes 1069072 | tf_op jit(solution)/shard_map/all_gather | solution.py:93
  155.8 3.5 select_reduce_fusion
  160.7 5.0 select_reduce_fusion.2
  167.9 4.1 select_reduce_fusion.1
  174.8 4.6 select_reduce_fusion.3
  182.1 6.0 %fusion.5 = (bf16[512,2048]{1,0:T(8,128)(2,1)}, bf16[512]{0:T(512)(128)(2,1)}, bf16[512]{0:T(512)(128)(2,1)}, bf16[512,2048]{1,0:T(8,128)(2,1)}) fusion(f32[512,2048]{1,0:T(8,128)} %get-tuple-element.164, f32[512]{0:T(512)} %convert_element_type.538, pred[2048]{0:T(1024)(128)(4,1)} %get-tuple-element.96, f32[512]{0:T(512)} %convert_element_type.548, ...), kind=kLoop, calls=%fused_computation.19 | loop fusion | flops 10484736 | bytes 12593152 | tf_op jit(solution)/shard_map/convert_element_type | solution.py:121
  199.7 6.7 %fusion.1 = (bf16[512,2048]{1,0:T(8,128)(2,1)}, bf16[512]{0:T(512)(128)(2,1)S(1)}, bf16[512]{0:T(512)(128)(2,1)S(1)}, bf16[512,2048]{1,0:T(8,128)(2,1)}) fusion(f32[512,2048]{1,0:T(8,128)} %get-tuple-element.168, f32[512]{0:T(512)S(1)} %copy-done.94, pred[2048]{0:T(1024)(128)(4,1)S(1)} %copy-done.101, f32[512]{0:T(512)S(1)} %convert_element_type.528, ...), kind=kLoop, calls=%fused_computation.15 | loop fusion | flops 10484736 | bytes 12593152 | tf_op jit(solution)/shard_map/convert_element_type | solution.py:121
  213.2 3.4 convolution_convert_fusion.3
  218.6 4.1 maximum_bitcast_fusion
  226.6 19.2 %all_to_all.5 = bf16[8,256,263]{1,2,0:T(8,128)(2,1)S(1)} all-to-all(bf16[8,256,263]{1,2,0:T(8,128)(2,1)} %copy.128), channel_id=1, replica_groups=mesh['samp'=4,'pix'=8] {'pix'}, dimensions={0} | all-to-all | bytes 2154496 | tf_op jit(solution)/shard_map/all_to_all | solution.py:127
  253.4 4.4 fusion.205
  264.5 3.7 multiply_convert_fusion.6
  298.8 4.6 all-gather.13.cloned.1.call-done
  314.7 3.6 multiply_convert_fusion.3
  343.6 3.2 pad_maximum_fusion.1
  365.7 4.1 pad_maximum_fusion
  369.8 12.5 %copy.149 = f32[4,261,2048]{2,0,1:T(4,128)} copy(f32[4,261,2048]{2,1,0:T(8,128)} %pad_maximum_fusion) | data formatting | bytes 17104896
  382.4 48.0 %all-reduce.5 = (bf16[512,261]{0,1:T(8,128)(2,1)S(1)}, f32[261]{0:T(512)S(1)}, f32[1024]{0:T(1024)S(1)}) all-reduce(f32[512,261]{0,1:T(8,128)S(1)} %copy-done.30, f32[261]{0:T(512)S(1)} %add_add_fusion, f32[1024]{0:T(1024)S(1)} %copy-done.107), channel_id=1, replica_groups=mesh['samp'=4,'pix'=8] {'samp','pix'}, use_global_device_ids=true, to_apply=%region_34.35 | all-reduce | flops 134917 | bytes 812072 | tf_op jit(solution)/shard_map/psum | solution.py:192
  432.6 3.6 fusion.196
  447.6 116.7 %reduce-scatter.5.cloned.1.call-done = bf16[4,3,64,128]{3,2,1,0:T(8,128)(2,1)} async-done(((bf16[128,3,64,128]{3,2,1,0:T(8,128)(2,1)}), bf16[4,3,64,128]{3,2,1,0:T(8,128)(2,1)}) %reduce-scatter.5.cloned.1.call-update) | async-done | bytes 196624 | tf_op jit(solution)/shard_map/reduce_scatter | solution.py:168
  (412 shorter events, 178.0 us)
Async XLA Ops:
  7.2 563.4 %copy-start = (f32[4,4,128,128]{3,2,1,0:T(8,128)S(1)}, f32[4,4,128,128]{3,2,1,0:T(8,128)}, u32[]{:S(2)}) copy-start(f32[4,4,128,128]{3,2,1,0:T(8,128)} %param.20) | copy-start | bytes 3145732
  7.2 29.5 %all-gather.7.cloned.1.call-start = ((), (), s32[]{:S(2)}) async-start(), calls=%async_computation.3 | async-start | bytes 1179648 | tf_op jit(solution)/shard_map/all_gather | solution.py:91
  9.0 87.6 %all-gather.15.cloned.1.call-start = ((), (), s32[]{:S(2)}) async-start(), calls=%async_computation.9 | async-start | bytes 2162688 | tf_op jit(solution)/shard_map/all_gather | solution.py:92
  10.8 143.1 %all-gather.9.cloned.1.call-start = ((), (), s32[]{:S(2)}) async-start(), calls=%async_computation.4 | async-start | bytes 1622016 | tf_op jit(solution)/shard_map/all_gather | solution.py:93
  12.4 241.1 %all-gather.11.cloned.1.call-start = ((), (), s32[]{:S(2)}) async-start(), calls=%async_computation.5 | async-start | bytes 6488064 | tf_op jit(solution)/shard_map/all_gather | solution.py:94
  13.1 290.2 %all-gather.13.cloned.1.call-start = ((), (), s32[]{:S(2)}) async-start(), calls=%async_computation.6 | async-start | bytes 1769472 | tf_op jit(solution)/shard_map/all_gather | solution.py:162
  27.7 180.5 %copy-start.68 = (f32[2048]{0:T(1024)}, f32[2048]{0:T(1024)S(1)}, u32[]{:S(2)}) copy-start(f32[2048]{0:T(1024)S(1)} %broadcast_multiply_fusion.12) | copy-start | bytes 24580
  28.9 162.5 %copy-start.2 = (bf16[1,261,2048]{2,1,0:T(8,128)(2,1)}, bf16[1,261,2048]{2,1,0:T(8,128)(2,1)S(1)}, u32[]{:S(2)}) copy-start(bf16[1,261,2048]{2,1,0:T(8,128)(2,1)S(1)} %get-tuple-element.121) | copy-start | bytes 3207172
  28.9 162.4 %copy-start.72 = (f32[2048]{0:T(1024)}, f32[2048]{0:T(1024)S(1)}, u32[]{:S(2)}) copy-start(f32[2048]{0:T(1024)S(1)} %broadcast_multiply_fusion.10) | copy-start | bytes 24580
  30.1 183.1 %copy-start.70 = (f32[2048]{0:T(1024)}, f32[2048]{0:T(1024)S(1)}, u32[]{:S(2)}) copy-start(f32[2048]{0:T(1024)S(1)} %broadcast_multiply_fusion.11) | copy-start | bytes 24580
  32.9 67.2 %copy-start.98 = (f32[1024]{0:T(1024)}, f32[1024]{0:T(1024)S(1)}, u32[]{:S(2)}) copy-start(f32[1024]{0:T(1024)S(1)} %get-tuple-element.150) | copy-start | bytes 12292
  32.9 175.4 %copy-start.80 = (f32[2048]{0:T(1024)}, f32[2048]{0:T(1024)S(1)}, u32[]{:S(2)}) copy-start(f32[2048]{0:T(1024)S(1)} %add_rsqrt_fusion.3) | copy-start | bytes 24580
  33.5 179.7 %copy-start.82 = (f32[2048]{0:T(1024)}, f32[2048]{0:T(1024)S(1)}, u32[]{:S(2)}) copy-start(f32[2048]{0:T(1024)S(1)} %add_rsqrt_fusion.2) | copy-start | bytes 24580
  33.5 162.8 %copy-start.74 = (f32[2048]{0:T(1024)}, f32[2048]{0:T(1024)S(1)}, u32[]{:S(2)}) copy-start(f32[2048]{0:T(1024)S(1)} %add_rsqrt_fusion) | copy-start | bytes 24580
  38.3 61.8 %copy-start.96 = (f32[512]{0:T(512)}, f32[512]{0:T(512)S(1)}, u32[]{:S(2)}) copy-start(f32[512]{0:T(512)S(1)} %broadcast_multiply_fusion.15) | copy-start | bytes 6148
  39.9 60.1 %copy-start.105 = (f32[512]{0:T(512)}, f32[512]{0:T(512)S(1)}, u32[]{:S(2)}) copy-start(f32[512]{0:T(512)S(1)} %add_rsqrt_fusion.4) | copy-start | bytes 6148
  103.7 52.1 %copy-start.88 = (f32[261]{0:T(512)S(1)}, f32[261]{0:T(512)}, u32[]{:S(2)}) copy-start(f32[261]{0:T(512)} %slice.122) | copy-start | bytes 3136
  103.7 52.1 %copy-start.104 = (pred[2048]{0:T(1024)(128)(4,1)S(1)}, pred[2048]{0:T(1024)(128)(4,1)}, u32[]{:S(2)}) copy-start(pred[2048]{0:T(1024)(128)(4,1)} %get-tuple-element.95) | copy-start | bytes 6148
  279.8 162.2 %all-reduce.4.cloned.1.call-start = ((), (), s32[]{:S(2)}) async-start(), calls=%async_computation.8 | async-start | bytes 262144 | tf_op jit(solution)/shard_map/psum | solution.py:170
  298.4 145.9 %reduce-scatter.7.cloned.1.call-start = ((), (), s32[]{:S(2)}) async-start(), calls=%async_computation.10 | async-start | bytes 1622016
  334.7 229.7 %reduce-scatter.5.cloned.1.call-start = ((), (), s32[]{:S(2)}) async-start(), calls=%async_computation.7 | async-start | bytes 6488064 | tf_op jit(solution)/shard_map/reduce_scatter | solution.py:168
  382.4 50.2 %copy-start.106 = (f32[512]{0:T(512)S(1)}, f32[512]{0:T(512)}, u32[]{:S(2)}) copy-start(f32[512]{0:T(512)} %copy-done.105) | copy-start | bytes 6148
  442.0 123.4 %copy-start.59 = (f32[4,4,64,64]{3,2,1,0:T(8,128)S(1)}, f32[4,4,64,64]{3,2,1,0:T(8,128)}, u32[]{:S(2)}) copy-start(f32[4,4,64,64]{3,2,1,0:T(8,128)} %param.19) | copy-start | bytes 786436
  445.3 120.6 %copy-start.62 = (f32[4,4,64,64]{3,2,1,0:T(8,128)S(1)}, f32[4,4,64,64]{3,2,1,0:T(8,128)}, u32[]{:S(2)}) copy-start(f32[4,4,64,64]{3,2,1,0:T(8,128)} %param.17) | copy-start | bytes 786436
  (101 other events, 550.5 us)
Sparse Core Ops, SparseCore 0:
  10.5 26.1 all-gather.6
  40.2 56.3 all-gather.14
  100.0 53.7 all-gather.8
  157.1 68.3 all-gather.10
  279.9 23.4 all-gather.12
  306.1 34.4 all-reduce.3
  346.7 97.2 reduce-scatter.6
  450.6 113.7 reduce-scatter.4

commit v2 on v1

--- a/solution.py
+++ b/solution.py
@@ -1,6 +1,11 @@
+import functools
+import math
+
 import jax
 import jax.numpy as jnp
 from jax import lax
+from jax.experimental import pallas as pl
+from jax.experimental.pallas import tpu as pltpu
 from jax.sharding import PartitionSpec as P
 
 EPSILON = 1e-05
@@ -13,6 +18,7 @@
 GAIN_RATE = 0.6
 MOMENT_FLOOR = 1e-08
 BF = jnp.bfloat16
+MESH = pl.DeviceIdType.MESH
 
 
 def matmul(former, latter):
@@ -62,6 +68,444 @@
 def moment_step(weight, grad, second, rate):
     second_new = STAT_DECAY * second + (1.0 - STAT_DECAY) * grad * grad
     return (second_new, weight - rate * grad / (jnp.sqrt(second_new) + MOMENT_FLOOR))
+
+
+def ceil_to(value, step):
+    return -(-value // step) * step
+
+
+class Links:
+    def __init__(self, send_sems, recv_sems):
+        self.send_sems = send_sems
+        self.recv_sems = recv_sems
+        self.used = 0
+        self.started = []
+
+    def push(self, source, target, samp, pix):
+        copy = pltpu.make_async_remote_copy(
+            src_ref=source,
+            dst_ref=target,
+            send_sem=self.send_sems.at[self.used],
+            recv_sem=self.recv_sems.at[self.used],
+            device_id=(samp, pix),
+            device_id_type=MESH,
+        )
+        self.used += 1
+        copy.start()
+        self.started.append(copy)
+        return copy
+
+    def drain(self):
+        for copy in self.started:
+            copy.wait_send()
+        self.started = []
+
+
+class Place:
+    def __init__(self, nz, ny, nx):
+        self.nz, self.ny, self.nx = nz, ny, nx
+        self.group = ny * nx * 2
+        self.z = lax.axis_index("samp")
+        self.p = lax.axis_index("pix")
+        self.c = lax.rem(self.p, 2)
+        self.x = lax.rem(self.p // 2, nx)
+        self.y = self.p // (2 * nx)
+
+    def pix(self, y, x, c):
+        return (y * self.nx + x) * 2 + c
+
+    def barrier(self):
+        semaphore = pltpu.get_barrier_semaphore()
+        for step in range(1, self.nz):
+            pl.semaphore_signal(
+                semaphore,
+                inc=1,
+                device_id=(lax.rem(self.z + step, self.nz), self.p),
+                device_id_type=MESH,
+            )
+        for step in range(1, self.group):
+            pl.semaphore_signal(
+                semaphore,
+                inc=1,
+                device_id=(self.z, lax.rem(self.p + step, self.group)),
+                device_id_type=MESH,
+            )
+        pl.semaphore_wait(semaphore, self.nz - 1 + self.group - 1)
+
+    def push_z(self, links, array, sub=()):
+        copies = []
+        for step in range(1, self.nz):
+            own = array.at[(self.z, self.y, self.x, self.c) + sub]
+            copies.append(links.push(own, own, lax.rem(self.z - step + self.nz, self.nz), self.p))
+        return copies
+
+    def push_first(self, links, array, lead, sub, along):
+        own = array.at[lead + (self.y, self.x, self.c) + sub]
+        copies = []
+        if along == "x":
+            for step in range(1, self.nx):
+                other = self.pix(self.y, lax.rem(self.x + step, self.nx), self.c)
+                copies.append(links.push(own, own, self.z, other))
+        else:
+            for step in range(1, self.ny):
+                other = self.pix(lax.rem(self.y + step, self.ny), self.x, self.c)
+                copies.append(links.push(own, own, self.z, other))
+        return copies
+
+    def push_second(self, links, array, lead, sub, first):
+        copies = []
+        if first == "x":
+            held = array.at[lead + (self.y, slice(None), self.c) + sub]
+            for step in range(1, self.ny):
+                other = self.pix(lax.rem(self.y + step, self.ny), self.x, self.c)
+                copies.append(links.push(held, held, self.z, other))
+        else:
+            held = array.at[lead + (slice(None), self.x, self.c) + sub]
+            for step in range(1, self.nx):
+                other = self.pix(self.y, lax.rem(self.x + step, self.nx), self.c)
+                copies.append(links.push(held, held, self.z, other))
+        return copies
+
+    def push_core(self, links, array, lead):
+        held = array.at[lead + (slice(None), slice(None), self.c)]
+        return [links.push(held, held, self.z, self.p + 1 - 2 * self.c)]
+
+
+def arrived(copies):
+    for copy in copies:
+        copy.wait_recv()
+
+
+def column_block(array, place, index, col_blocks, owned, sub=()):
+    every = slice(None)
+    if 2 * owned == col_blocks:
+        block = array[(every, every, every, index // owned) + sub + (index % owned,)]
+    else:
+        block = array[(every, every, index // 2, index % 2) + sub + (0,)]
+    return block.reshape(-1, block.shape[-1])
+
+
+def column_pair(array, place, pair, col_blocks, owned, sub=()):
+    return jnp.concatenate(
+        [
+            column_block(array, place, 2 * pair, col_blocks, owned, sub),
+            column_block(array, place, 2 * pair + 1, col_blocks, owned, sub),
+        ],
+        axis=1,
+    )
+
+
+def front_kernel(
+    dims,
+    pixels,
+    mask,
+    gain_cols,
+    lat_gain,
+    own_proj,
+    own_keyval,
+    own_latents,
+    all_query,
+    all_keyval,
+    all_latents,
+    all_mats,
+    normed_out,
+    inverse_out,
+    weights_out,
+    sent_out,
+    landed,
+    pixel_query,
+    mats_own,
+    g_query,
+    g_keyval,
+    g_latents,
+    lat_normed,
+    query,
+    normed,
+    weights,
+    outgoing,
+    send_sems,
+    recv_sems,
+    local_sems,
+):
+    batches, channels, shard_pixels = pixels.shape
+    lat_rows, width = own_latents.shape
+    owned, _, row_block, col_block = own_proj.shape
+    col_blocks = width // col_block
+    padded = normed.shape[1]
+    main = channels // 16 * 16
+    place = Place(*dims)
+    links = Links(send_sems, recv_sems)
+    z, y, x, c, p = place.z, place.y, place.x, place.c, place.p
+    half_rows = row_block // 2
+    half_width = width // 2
+    every = slice(None)
+
+    g_query[z, y, x, c] = own_proj[:, 0].astype(BF)
+    g_keyval[z, y, x, c] = own_keyval[...]
+    g_latents[y, x, c] = own_latents[...]
+    for mat in range(3):
+        mats_own[mat] = own_proj[:, mat + 1].astype(BF)
+    local = []
+
+    def local_copy(source, target):
+        copy = pltpu.make_async_copy(source, target, local_sems.at[len(local)])
+        copy.start()
+        local.append(copy)
+        return copy
+
+    own_mats_copy = local_copy(mats_own, all_mats.at[z, y, x, c])
+    place.barrier()
+
+    sub_a = (every, pl.ds(0, half_rows))
+    sub_b = (every, pl.ds(half_rows, half_rows))
+
+    def first_of(step):
+        zz = lax.rem(z + step, place.nz)
+        copies = place.push_first(links, g_query, (zz,), sub_a, "x")
+        copies += place.push_first(links, g_query, (zz,), sub_b, "y")
+        copies += place.push_first(links, g_keyval, (zz,), (), "xy"[step % 2])
+        return copies
+
+    def second_of(step):
+        zz = lax.rem(z + step, place.nz)
+        copies = place.push_second(links, g_query, (zz,), sub_a, "x")
+        copies += place.push_second(links, g_query, (zz,), sub_b, "y")
+        copies += place.push_second(links, g_keyval, (zz,), (), "xy"[step % 2])
+        return copies
+
+    z_query = place.push_z(links, g_query)
+    z_keyval = place.push_z(links, g_keyval)
+    firsts = [first_of(0)]
+    lat_a = (every, pl.ds(0, half_width))
+    lat_b = (every, pl.ds(half_width, half_width))
+    lat_first = place.push_first(links, g_latents, (), lat_a, "x")
+    lat_first += place.push_first(links, g_latents, (), lat_b, "y")
+
+    lane_chunk = 128
+    bias_row = channels - main
+
+    def norm_image(image):
+        @pl.loop(0, shard_pixels // lane_chunk)
+        def _(chunk):
+            cols = pl.ds(pl.multiple_of(chunk * lane_chunk, lane_chunk), lane_chunk)
+            top = pixels[image, 0:main, cols].astype(jnp.float32)
+            tail = pixels[image, main:channels, cols].astype(jnp.float32)
+            mean = (
+                jnp.sum(top, axis=0, keepdims=True) + jnp.sum(tail, axis=0, keepdims=True)
+            ) / channels
+            top = top - mean
+            tail = tail - mean
+            variance = (
+                jnp.sum(top * top, axis=0, keepdims=True)
+                + jnp.sum(tail * tail, axis=0, keepdims=True)
+            ) / channels
+            inverse = lax.rsqrt(variance + EPSILON)
+            inverse_out[image : image + 1, cols] = inverse
+            normed[image, 0:main, cols] = (top * inverse * gain_cols[0:main, :]).astype(BF)
+            tail = tail * inverse * gain_cols[main:channels, :]
+            bias = jnp.where(mask[image : image + 1, cols] == 1, 0.0, NEGATIVE)
+            row = lax.broadcasted_iota(jnp.int32, (padded - main, lane_chunk), 0)
+            rest = jnp.where(row == bias_row + 1, 1.0, 0.0)
+            rest = jnp.where(row == bias_row, bias, rest)
+            for index in range(channels - main):
+                rest = jnp.where(row == index, tail[index : index + 1], rest)
+            normed[image, main:padded, cols] = rest.astype(BF)
+
+        local_copy(normed.at[image], normed_out.at[image])
+
+    norm_image(0)
+    for step in range(1, place.nz):
+        z_query[step - 1].wait_recv()
+        z_keyval[step - 1].wait_recv()
+        firsts.append(first_of(step))
+    own_mats_copy.wait()
+    z_mats = place.push_z(links, all_mats)
+    norm_image(1)
+    seconds = []
+    for step in range(place.nz):
+        arrived(firsts[step])
+        seconds += second_of(step)
+    arrived(lat_first)
+    seconds += place.push_second(links, g_latents, (), lat_a, "x")
+    seconds += place.push_second(links, g_latents, (), lat_b, "y")
+    norm_image(2)
+    arrived(seconds)
+    cores = place.push_core(links, g_query, (every,))
+    cores += place.push_core(links, g_keyval, (every,))
+    cores += place.push_core(links, g_latents, ())
+    norm_image(3)
+
+    out_sub = 0
+    mats_a = [((0, every, pl.ds(0, half_rows)), "x"), ((1,), "x")]
+    mats_b = [((0, every, pl.ds(half_rows, half_rows)), "y"), ((2,), "y")]
+
+    arrived(z_mats)
+    firsts_m = []
+    for sub, along in mats_a + mats_b:
+        firsts_m += place.push_first(links, all_mats, (every,), sub, along)
+
+    arrived(cores)
+    for yy in range(place.ny):
+        for xx in range(place.nx):
+            for cc in range(2):
+                rows = pl.ds(((yy * place.nx + xx) * 2 + cc) * lat_rows, lat_rows)
+                values = g_latents[yy, xx, cc].astype(jnp.float32)
+                mean = jnp.mean(values, axis=1, keepdims=True)
+                values = values - mean
+                variance = jnp.mean(values * values, axis=1, keepdims=True)
+                values = values * lax.rsqrt(variance + EPSILON) * lat_gain[...]
+                lat_normed[rows, :] = values.astype(BF)
+    local_copy(g_query, all_query)
+    local_copy(g_keyval, all_keyval)
+    local_copy(g_latents, all_latents)
+    for pair in range(col_blocks // 2):
+        query[:, 2 * col_block * pair : 2 * col_block * (pair + 1)] = jnp.dot(
+            lat_normed[...],
+            column_pair(g_query, place, pair, col_blocks, owned),
+            preferred_element_type=jnp.float32,
+        ).astype(BF)
+    key_t = g_keyval[0 : place.nz // 2]
+    key_t = key_t.reshape(width, key_t.shape[-1])
+    projected = jnp.dot(query[...], key_t, preferred_element_type=jnp.float32) * width ** (-0.5)
+    lane = lax.broadcasted_iota(jnp.int32, projected.shape, 1)
+    pixel_query[...] = jnp.where(lane == channels, 1.0, projected).astype(BF)
+
+    all_rows = lat_rows * place.group
+    tile = min(256, all_rows)
+
+    def attend(image):
+        @pl.loop(0, all_rows // tile)
+        def _(step):
+            rows = pl.ds(pl.multiple_of(step * tile, tile), tile)
+            scores = jnp.dot(
+                pixel_query[rows, 0:padded], normed[image], preferred_element_type=jnp.float32
+            )
+            top = jnp.max(scores, axis=1, keepdims=True)
+            top = jnp.maximum(top, 0.1 * NEGATIVE).astype(BF).astype(jnp.float32)
+            share = jnp.exp(scores - top).astype(BF)
+            weights[image, rows, :] = share
+            numer = lax.dot_general(
+                share,
+                normed[image],
+                (((1,), (1,)), ((), ())),
+                preferred_element_type=jnp.float32,
+            )
+            lane = lax.broadcasted_iota(jnp.int32, numer.shape, 1)
+            outgoing[image, rows, 0:padded] = jnp.where(lane == channels, top, numer).astype(BF)
+
+        local_copy(weights.at[image], weights_out.at[image])
+        local_copy(outgoing.at[image], sent_out.at[image])
+        own_rows = pl.ds(pl.multiple_of(p * lat_rows, lat_rows), lat_rows)
+        local_copy(outgoing.at[image, own_rows], landed.at[p, image])
+        copies = []
+        for step in range(1, place.group):
+            q = lax.rem(p + step, place.group)
+            rows = pl.ds(pl.multiple_of(q * lat_rows, lat_rows), lat_rows)
+            copies.append(links.push(outgoing.at[image, rows], landed.at[p, image], z, q))
+        return copies
+
+    sent = attend(0)
+    arrived(firsts_m)
+    seconds_m = []
+    for sub, along in mats_a + mats_b:
+        seconds_m += place.push_second(links, all_mats, (every,), sub, along)
+    sent += attend(1)
+    sent += attend(2)
+    arrived(seconds_m)
+    core_m = place.push_core(links, all_mats, (every,))
+    sent += attend(3)
+    arrived(sent)
+    arrived(core_m)
+    links.drain()
+    for copy in local[1:]:
+        copy.wait()
+
+
+def front_copies(nz, ny, nx, batches):
+    plane_first = lambda a, b: a * (nx - 1) + b * (ny - 1)
+    count = 2 * (nz - 1)
+    for step in range(nz):
+        ab = plane_first(1, 1) + (plane_first(1, 0) if step % 2 == 0 else plane_first(0, 1))
+        ba = plane_first(1, 1) + (plane_first(0, 1) if step % 2 == 0 else plane_first(1, 0))
+        count += ab + ba
+    count += 2 * plane_first(1, 1)
+    count += 3 + (nz - 1) + 2 * plane_first(2, 2) + 1
+    count += batches * (2 * nx * ny - 1)
+    return count
+
+
+def front(dims, pixels, pixel_mask, in_gain, lat_gain, proj_blocks, keyval_weight, latents):
+    nz, ny, nx = dims
+    batches, channels, shard_pixels = pixels.shape
+    lat_rows, width = latents.shape
+    owned, mats, row_block, col_block = proj_blocks.shape
+    keyval_rows = keyval_weight.shape[1]
+    group = 2 * ny * nx
+    all_rows = lat_rows * group
+    padded = ceil_to(channels + 2, 16)
+    lanes = ceil_to(padded, 128)
+    gain_cols = jnp.broadcast_to(
+        jnp.pad(in_gain, (0, ceil_to(channels, 8) - channels))[:, None],
+        (ceil_to(channels, 8), 128),
+    )
+    own_keyval = jnp.pad(keyval_weight.T.astype(BF), ((0, 0), (0, lanes - channels)))
+    vmem = pl.BlockSpec(memory_space=pltpu.VMEM)
+    anywhere = pl.BlockSpec(memory_space=pl.ANY)
+    cube = (nz, ny, nx, 2)
+    copies = front_copies(nz, ny, nx, batches)
+    return pl.pallas_call(
+        functools.partial(front_kernel, dims),
+        out_shape=(
+            jax.ShapeDtypeStruct(cube + (owned, row_block, col_block), BF),
+            jax.ShapeDtypeStruct(cube + (keyval_rows, lanes), BF),
+            jax.ShapeDtypeStruct(cube[1:] + (lat_rows, width), BF),
+            jax.ShapeDtypeStruct(cube + (3, owned, row_block, col_block), BF),
+            jax.ShapeDtypeStruct((batches, padded, shard_pixels), BF),
+            jax.ShapeDtypeStruct((batches, shard_pixels), jnp.float32),
+            jax.ShapeDtypeStruct((batches, all_rows, shard_pixels), BF),
+            jax.ShapeDtypeStruct((batches, all_rows, lanes), BF),
+            jax.ShapeDtypeStruct((group, batches, lat_rows, lanes), BF),
+            jax.ShapeDtypeStruct((all_rows, lanes), BF),
+        ),
+        in_specs=[vmem] * 7,
+        out_specs=(
+            anywhere,
+            anywhere,
+            anywhere,
+            anywhere,
+            anywhere,
+            vmem,
+            anywhere,
+            anywhere,
+            anywhere,
+            vmem,
+        ),
+        scratch_shapes=[
+            pltpu.VMEM((3, owned, row_block, col_block), BF),
+            pltpu.VMEM(cube + (owned, row_block, col_block), BF),
+            pltpu.VMEM(cube + (keyval_rows, lanes), BF),
+            pltpu.VMEM(cube[1:] + (lat_rows, width), BF),
+            pltpu.VMEM((all_rows, width), BF),
+            pltpu.VMEM((all_rows, width), BF),
+            pltpu.VMEM((batches, padded, shard_pixels), BF),
+            pltpu.VMEM((batches, all_rows, shard_pixels), BF),
+            pltpu.VMEM((batches, all_rows, lanes), BF),
+            pltpu.SemaphoreType.DMA((copies,)),
+            pltpu.SemaphoreType.DMA((copies,)),
+            pltpu.SemaphoreType.DMA((4 + 4 * batches,)),
+        ],
+        compiler_params=pltpu.CompilerParams(
+            collective_id=0, has_side_effects=True, vmem_limit_bytes=56 * 2**20
+        ),
+    )(
+        pixels,
+        pixel_mask,
+        gain_cols,
+        lat_gain[None, :],
+        proj_blocks,
+        own_keyval,
+        latents.astype(BF),
+    )
 
 
 def body(
@@ -88,43 +532,38 @@
     scale = width ** (-0.5)
     everyone = ("samp", "pix")
 
-    latent_all = lax.all_gather(latents.astype(BF), "pix", axis=0, tiled=True).astype(jnp.float32)
-    query_blocks = lax.all_gather(proj_blocks[:, 0].astype(BF), everyone, axis=0, tiled=True)
-    keyval_t = lax.all_gather(keyval_weight.T.astype(BF), everyone, axis=0, tiled=True)
-    rest_blocks = lax.all_gather(proj_blocks[:, 1:].astype(BF), everyone, axis=0, tiled=True)
-    query_weight = assemble(query_blocks, width, row_block, col_block)
-    output_weight = assemble(rest_blocks[:, 0], width, row_block, col_block)
-    mlp_in = assemble(rest_blocks[:, 1], width, row_block, col_block)
-    mlp_out = assemble(rest_blocks[:, 2], width, row_block, col_block)
-    key_t = keyval_t[:width]
-    value_t = keyval_t[width:]
     lat_gain = gains[:width]
     in_gain = gains[width : width + channels]
     mlp_gain = gains[width + channels :]
+    side = math.isqrt(groups // 2)
+    dims = (lax.axis_size("samp"), side, side)
+    (
+        query_blocks,
+        keyval_t,
+        latent_all,
+        mats,
+        normed_all,
+        inverse_all,
+        weights_all,
+        sent_all,
+        landed,
+        pixel_query,
+    ) = front(dims, pixels, pixel_mask, in_gain, lat_gain, proj_blocks, keyval_weight, latents)
+    latent_all = latent_all.reshape(all_rows, width).astype(jnp.float32)
+    keyval_t = keyval_t.reshape(2 * width, -1)[:, :channels]
+    pixel_query = pixel_query[:, :channels]
+    query_weight = assemble(query_blocks, width, row_block, col_block)
+    rest_blocks = mats.reshape(-1, 3, owned_count, row_block, col_block).swapaxes(0, 1)
+    output_weight = assemble(rest_blocks[0], width, row_block, col_block)
+    mlp_in = assemble(rest_blocks[1], width, row_block, col_block)
+    mlp_out = assemble(rest_blocks[2], width, row_block, col_block)
+    key_t = keyval_t[:width]
+    value_t = keyval_t[width:]
     lat_hat, lat_inverse = normalize_parts(latent_all, 1)
     lat_normed = (lat_hat * lat_gain[None, :]).astype(BF)
     query = matmul(lat_normed, query_weight).astype(BF)
-    pixel_query = (matmul(query, key_t) * scale).astype(BF)
-
-    kept = []
-    packed = []
-    for slot in range(batches):
-        normal_hat, inverse = normalize_parts(pixels[slot].astype(jnp.float32), 0)
-        normed = (normal_hat * in_gain[:, None]).astype(BF)
-        valid = pixel_mask[slot] == 1
-        scores = jnp.where(valid[None, :], matmul(pixel_query, normed), NEGATIVE)
-        top = jnp.max(scores, axis=1).astype(BF)
-        weights = jnp.where(
-            valid[None, :], jnp.exp(scores - top.astype(jnp.float32)[:, None]), 0.0
-        )
-        total = jnp.sum(weights, axis=1).astype(BF)
-        weights = weights.astype(BF)
-        numer = contract(weights, normed, 1, 1).astype(BF)
-        kept.append((normed, top, weights))
-        packed.append(jnp.concatenate([numer, top[:, None], total[:, None]], axis=1))
-    outgoing = jnp.stack(packed, axis=0).reshape(batches, groups, lat_rows, channels + 2)
-    outgoing = outgoing.transpose(1, 0, 2, 3).reshape(groups, batches * lat_rows, channels + 2)
-    incoming = lax.all_to_all(outgoing, "pix", split_axis=0, concat_axis=0, tiled=True)
+
+    incoming = landed.reshape(groups, batches * lat_rows, -1)
     top_in = incoming[:, :, channels].astype(jnp.float32)
     total_in = incoming[:, :, channels + 1].astype(jnp.float32)
     peak = jnp.max(top_in, axis=0)
@@ -173,7 +612,9 @@
     in_gain_part = jnp.zeros((channels,), jnp.float32)
     pixel_list = []
     for slot in range(batches):
-        normed, top, weights = kept[slot]
+        normed = normed_all[slot, :channels]
+        top = sent_all[slot, :, channels]
+        weights = weights_all[slot]
         back = back_all[slot]
         share = jnp.exp(top.astype(jnp.float32) - back[:, channels].astype(jnp.float32))
         back_chan = (back[:, :channels].astype(jnp.float32) * share[:, None]).astype(BF)

time: 584 us -> 435 us (0.74)
  waiting for transfers between devices: 230 us -> 99.4 us
  Pallas kernels: 0 us -> 84.3 us
  local copies, waits for them, and re-layouts: 115 us -> 67.5 us
  other arithmetic: 57.1 us -> 34.2 us
  blocking collectives: 67.2 us -> 47.3 us
  matrix products: 93.5 us -> 77.6 us
    all_gather x4 -> x0, waiting for transfers between devices: 109 us -> none  [the longest x1 55.3 us: body(): lax.all_gather(proj_blocks[:, 0].astype(BF), everyone, axis=0, tiled=True)]
    pallas_call x0 -> x1, Pallas kernels: none -> 84.3 us  [front(): pl.pallas_call(functools.partial(front_kernel, dims), out_shape=(jax.Shap...]
    reduce_scatter x1, waiting for transfers between devices: 117 us -> 91 us  [body(): lax.psum_scatter(triple_term, everyone, scatter_dimension=0, tiled=True)]
    all_to_all x1 -> x0, blocking collectives: 19.2 us -> none  [body(): lax.all_to_all(outgoing, 'pix', split_axis=0, concat_axis=0, tiled=True)]
    dot_general x14 -> x8, matrix products: 37.8 us -> 20.1 us  [matmul(): return jnp.dot(former, latter, preferred_element_type=jnp.float32)]
    convert_element_type x12 -> x0, local copies, waits for them, and re-layouts: 17.3 us -> none  [the longest x4 6.54 us: body(): numer = contract(weights, normed, 1, 1).astype(BF)]
    slice x4 -> x1, local copies, waits for them, and re-layouts: 18.1 us -> 1.5 us  [body(): mlp_out = assemble(rest_blocks[2], width, row_block, col_block)]
    convert_element_type x8 -> x3, other arithmetic: 17.6 us -> 4.02 us  [the longest x1 1.62 us: front(): latents.astype(BF)]
  transfers between devices with their start and end apart: 8 -> 4, of which waited for: 5 -> 2; matrix products, arithmetic and copies ran while one was open for 37% -> 29% of each run, Pallas kernels for 0% -> 0%
where the time goes in v2:
time: 435 us; the launch traced here: 427 us
  waiting for transfers between devices  99.4 us (23%)
  Pallas kernels  84.3 us (19%)
  matrix products  77.6 us (18%)
  local copies, waits for them, and re-layouts  67.5 us (16%)
  blocking collectives  47.3 us (11%)
  other arithmetic  34.2 us (8%)
  between operations  16.8 us (4%)
    reduce_scatter x1, waiting for transfers between devices, body(): lax.psum_scatter(triple_term, everyone, scatter_dimension=0, tiled=True)  91 us
    pallas_call x1, Pallas kernels, front(): pl.pallas_call(functools.partial(front_kernel, dims), out_shape=(jax.Shap...  84.3 us
    dot_general x27, matrix products, contract(): lax.dot_general(former, latter, (((former_dim,), (latter_dim,)), ((), ())...  48 us
    psum x1, blocking collectives, body(): lax.psum((query_acc, in_gain_part, mlp_gain_part), everyone)  47.3 us
    unnamed x132, local copies, waits for them, and re-layouts  33.7 us
    dot_general x8, matrix products, matmul(): return jnp.dot(former, latter, preferred_element_type=jnp.float32)  20.1 us
    slice x5, local copies, waits for them, and re-layouts, body(): back = back_all[slot]  9.22 us
  transfers between devices with their start and end apart: 4, of which 2 were waited for; matrix products, arithmetic and copies ran while one was open for 29% of the time, Pallas kernels for 0%

profile of v2, /device:TPU:0, one launch (start us, length us, event | category | flops | bytes accessed | tf_op | source)
XLA Modules:
  0.0 427.4 jit_solution(15865449257182633689)
XLA Ops:
  12.7 6.6 %copy.100.pixels = bf16[4,261,2048]{2,1,0:T(8,128)(2,1)} copy(bf16[4,261,2048]{2,0,1:T(4,128)(2,1)} %param.14) | data formatting | bytes 8552448 | tf_op args[0]
  20.7 84.3 %shard_map.253 = (bf16[4,2,2,2,4,64,128]{6,5,4,3,2,1,0:T(8,128)(2,1)}, bf16[4,2,2,2,64,384]{5,4,3,2,1,0:T(8,128)(2,1)}, bf16[2,2,2,64,1024]{4,3,2,1,0:T(8,128)(2...) custom-call(bf16[4,261,2048]{2,1,0:T(8,128)(2,1)} %copy.100.pixels, ...), custom_call_target="tpu_custom_call" | custom-call | tf_op jit(solution)/shard_map/pallas_call | solution.py:456
  109.9 4.3 %copy_bitcast_fusion = bf16[3,32,4,64,128]{4,3,2,1,0:T(8,128)(2,1)S(1)} fusion(bf16[4,2,2,2,3,4,64,128]{7,6,5,4,3,2,1,0:T(8,128)(2,1)} %get-tuple-element.26), kind=kLoop, calls=%fused_computation.2 | loop fusion | bytes 12582912 | tf_op jit(solution)/shard_map/transpose | solution.py:556
  122.8 4.1 multiply_convert_fusion.7
  143.3 3.1 copy.124
  149.3 8.4 %all-gather.2.cloned.1.call-done = bf16[4,512,263]{2,1,0:T(8,128)(2,1)} async-done(((bf16[4,64,263]{2,1,0:T(8,128)(2,1)}), bf16[4,512,263]{2,1,0:T(8,128)(2,1)}) %all-gather.2.cloned.1.call-update) | async-done | bytes 1077264 | tf_op jit(solution)/shard_map/all_gather | solution.py:601
  166.9 3.4 multiply_convert_fusion.3
  170.4 2.8 fusion.118
  173.3 4.0 multiply_convert_fusion.2
  183.8 4.4 %fusion.91 = bf16[1024,261]{0,1:T(8,128)(2,1)} fusion(bf16[512,1024]{1,0:T(8,128)(2,1)} %bitcast.396, bf16[128,8,8,128]{3,2,1,0:T(8,128)(2,1)} %bitcast.387, f32[512,261]{0,1:T(8,128)} %convolution_add_fusion.5), kind=kOutput, calls=%fused_computation.127 | convolution fusion | flops 1348612608 | bytes 4214784 | tf_op jit(solution)/shard_map/dot_general | solution.py:29
  190.5 2.6 copy.132
  200.5 3.2 pad_maximum_fusion.1
  205.3 3.6 convert_reduce_fusion.3
  210.2 3.3 fusion.104
  218.3 2.6 fusion.149
  223.6 3.8 fusion.34
  231.7 2.6 fusion.46
  237.0 4.2 pad_maximum_fusion
  241.1 12.4 %copy.127 = f32[4,261,2048]{2,0,1:T(4,128)} copy(f32[4,261,2048]{2,1,0:T(8,128)} %pad_maximum_fusion) | data formatting | bytes 17104896
  253.6 47.3 %all-reduce.7 = (bf16[512,261]{0,1:T(8,128)(2,1)S(1)}, f32[261]{0:T(512)S(1)}, f32[1024]{0:T(1024)S(1)}) all-reduce(f32[512,261]{0,1:T(8,128)} %convolution_add_fusion.5, f32[261]{0:T(512)S(1)} %add_add_fusion, f32[1024]{0:T(1024)S(1)} %copy-done.43), channel_id=1, replica_groups=mesh['samp'=4,'pix'=8] {'samp','pix'}, use_global_device_ids=true, to_apply=%region_26.27 | all-reduce | flops 134917 | bytes 812072 | tf_op jit(solution)/shard_map/psum | solution.py:633
  303.1 4.0 fusion.189
  318.7 91.0 %reduce-scatter.5.cloned.1.call-done = bf16[4,3,64,128]{3,2,1,0:T(8,128)(2,1)} async-done(((bf16[128,3,64,128]{3,2,1,0:T(8,128)(2,1)}), bf16[4,3,64,128]{3,2,1,0:T(8,128)(2,1)}) %reduce-scatter.5.cloned.1.call-update) | async-done | bytes 196624 | tf_op jit(solution)/shard_map/reduce_scatter | solution.py:607
  412.6 2.8 fusion.108
  415.4 2.8 fusion.84
  (254 shorter events, 98.9 us)
Async XLA Ops:
  8.0 410.2 %copy-start = (f32[4,4,128,128]{3,2,1,0:T(8,128)S(1)}, f32[4,4,128,128]{3,2,1,0:T(8,128)}, u32[]{:S(2)}) copy-start(f32[4,4,128,128]{3,2,1,0:T(8,128)} %param.20) | copy-start | bytes 3145732
  8.0 149.6 %all-gather.2.cloned.1.call-start = ((), (), s32[]{:S(2)}) async-start(), calls=%async_computation.2 | async-start | bytes 1769472 | tf_op jit(solution)/shard_map/all_gather | solution.py:601
  117.5 9.5 %copy-start.14 = (bf16[16,64,8,128]{3,2,1,0:T(8,128)(2,1)}, bf16[16,64,8,128]{3,2,1,0:T(8,128)(2,1)S(1)}, u32[]{:S(2)}) copy-start(bf16[16,64,8,128]{3,2,1,0:T(8,128)(2,1)S(1)} %copy.107) | copy-start | bytes 6291460
  121.6 8.4 %copy-start.7 = (f32[256,1024]{1,0:T(8,128)}, f32[256,1024]{1,0:T(8,128)S(1)}, u32[]{:S(2)}) copy-start(f32[256,1024]{1,0:T(8,128)S(1)} %fusion.139) | copy-start | bytes 3145732
  134.5 178.6 %all-reduce.6.cloned.1.call-start = ((), (), s32[]{:S(2)}) async-start(), calls=%async_computation.4 | async-start | bytes 262144 | tf_op jit(solution)/shard_map/psum | solution.py:609
  135.4 180.0 %reduce-scatter.7.cloned.1.call-start = ((), (), s32[]{:S(2)}) async-start(), calls=%async_computation.5 | async-start | bytes 1622016
  166.9 10.5 %slice-start.2 = ((s8[8388608]{0:T(1024)(128)(4,1)}), s8[4194304]{0:T(1024)(128)(4,1)S(1)}, s32[]{:S(2)}) async-start(s8[8388608]{0:T(1024)(128)(4,1)} %bitcast.383), calls=%async_computation.8 | async-start | bytes 8388608
  170.4 7.0 %slice-start.3 = ((s8[8388608]{0:T(1024)(128)(4,1)}), s8[4194304]{0:T(1024)(128)(4,1)S(1)}, s32[]{:S(2)}) async-start(s8[8388608]{0:T(1024)(128)(4,1)} %bitcast.383), calls=%async_computation.9 | async-start | bytes 8388608
  170.4 7.0 %slice-start.6 = ((s8[4456448]{0:T(1024)(128)(4,1)}), s8[4194304]{0:T(1024)(128)(4,1)S(1)}, s32[]{:S(2)}) async-start(s8[4456448]{0:T(1024)(128)(4,1)} %bitcast.421), calls=%async_computation.12 | async-start | bytes 8388608
  193.1 216.6 %reduce-scatter.5.cloned.1.call-start = ((), (), s32[]{:S(2)}) async-start(), calls=%async_computation.3 | async-start | bytes 6488064 | tf_op jit(solution)/shard_map/reduce_scatter | solution.py:607
  210.2 13.3 %slice-start = ((s8[4325376]{0:T(1024)(128)(4,1)}), s8[131072]{0:T(1024)(128)(4,1)S(1)}, s32[]{:S(2)}) async-start(s8[4325376]{0:T(1024)(128)(4,1)} %bitcast.360), calls=%async_computation.6 | async-start | bytes 262144
  221.0 8.8 %slice-start.4 = ((s8[8388608]{0:T(1024)(128)(4,1)}), s8[4194304]{0:T(1024)(128)(4,1)S(1)}, s32[]{:S(2)}) async-start(s8[8388608]{0:T(1024)(128)(4,1)} %bitcast.385), calls=%async_computation.10 | async-start | bytes 8388608
  223.5 6.3 %slice-start.5 = ((s8[8388608]{0:T(1024)(128)(4,1)}), s8[4194304]{0:T(1024)(128)(4,1)S(1)}, s32[]{:S(2)}) async-start(s8[8388608]{0:T(1024)(128)(4,1)} %bitcast.385), calls=%async_computation.11 | async-start | bytes 8388608
  241.1 12.4 %copy-start.43 = (f32[1024]{0:T(1024)S(1)}, f32[1024]{0:T(1024)}, u32[]{:S(2)}) copy-start(f32[1024]{0:T(1024)} %get-tuple-element.116) | copy-start | bytes 12292
  253.6 49.4 %copy-start.48 = (f32[512]{0:T(512)S(1)}, f32[512]{0:T(512)}, u32[]{:S(2)}) copy-start(f32[512]{0:T(512)} %div.163) | copy-start | bytes 6148
  253.6 49.4 %copy-start.49 = (f32[512]{0:T(512)S(1)}, f32[512]{0:T(512)}, u32[]{:S(2)}) copy-start(f32[512]{0:T(512)} %rsqrt.58) | copy-start | bytes 6148
  303.0 9.5 %copy-start.36 = (f32[2309]{0:T(1024)S(1)}, f32[2309]{0:T(1024)}, u32[]{:S(2)}) copy-start(f32[2309]{0:T(1024)} %param.25) | copy-start | bytes 27712
  303.0 9.5 %copy-start.42 = (f32[2309]{0:T(1024)S(1)}, f32[2309]{0:T(1024)}, u32[]{:S(2)}) copy-start(f32[2309]{0:T(1024)} %param.26) | copy-start | bytes 27712
  303.0 10.1 %copy-start.11 = (f32[64,1024]{1,0:T(8,128)S(1)}, f32[64,1024]{1,0:T(8,128)}, u32[]{:S(2)}) copy-start(f32[64,1024]{1,0:T(8,128)} %param.23) | copy-start | bytes 786436
  303.0 10.1 %copy-start.33 = (f32[64,1024]{1,0:T(8,128)S(1)}, f32[64,1024]{1,0:T(8,128)}, u32[]{:S(2)}) copy-start(f32[64,1024]{1,0:T(8,128)} %param.24) | copy-start | bytes 786436
  307.1 9.2 %copy-start.25 = (f32[261,64]{1,0:T(8,128)S(1)}, f32[261,64]{1,0:T(8,128)}, u32[]{:S(2)}) copy-start(f32[261,64]{1,0:T(8,128)} %copy.126) | copy-start | bytes 200452
  307.3 9.8 %copy-start.35 = (f32[2309]{0:T(1024)}, f32[2309]{0:T(1024)S(1)}, u32[]{:S(2)}) copy-start(f32[2309]{0:T(1024)S(1)} %concatenate.20) | copy-start | bytes 27712
  410.7 7.6 %copy-start.1 = (f32[4,4,64,128]{3,2,1,0:T(8,128)}, f32[4,4,64,128]{3,2,1,0:T(8,128)S(1)}, u32[]{:S(2)}) copy-start(f32[4,4,64,128]{3,2,1,0:T(8,128)S(1)} %pad_maximum_fusion.3) | copy-start | bytes 1572868
  412.6 5.7 %copy-start.12 = (f32[4,4,64,128]{3,2,1,0:T(8,128)S(1)}, f32[4,4,64,128]{3,2,1,0:T(8,128)}, u32[]{:S(2)}) copy-start(f32[4,4,64,128]{3,2,1,0:T(8,128)} %own_proj.1) | copy-start | bytes 1572868
  (39 other events, 105.7 us)
Sparse Core Ops, SparseCore 0:
  134.6 22.9 all-gather.1
  193.2 97.0 reduce-scatter.6
  296.0 113.6 reduce-scatter.4
Sparse Core Ops, SparseCore 1:
  138.0 31.5 all-reduce.5

commit v3 on v2

--- a/solution.py
+++ b/solution.py
@@ -19,6 +19,7 @@
 MOMENT_FLOOR = 1e-08
 BF = jnp.bfloat16
 MESH = pl.DeviceIdType.MESH
+NT = (((1,), (1,)), ((), ()))
 
 
 def matmul(former, latter):
@@ -81,7 +82,7 @@
         self.used = 0
         self.started = []
 
-    def push(self, source, target, samp, pix):
+    def make(self, source, target, samp, pix):
         copy = pltpu.make_async_remote_copy(
             src_ref=source,
             dst_ref=target,
@@ -91,6 +92,10 @@
             device_id_type=MESH,
         )
         self.used += 1
+        return copy
+
+    def push(self, source, target, samp, pix):
+        copy = self.make(source, target, samp, pix)
         copy.start()
         self.started.append(copy)
         return copy
@@ -214,6 +219,7 @@
     sent_out,
     landed,
     pixel_query,
+    query_out,
     mats_own,
     g_query,
     g_keyval,
@@ -364,6 +370,7 @@
             column_pair(g_query, place, pair, col_blocks, owned),
             preferred_element_type=jnp.float32,
         ).astype(BF)
+    local_copy(query, query_out)
     key_t = g_keyval[0 : place.nz // 2]
     key_t = key_t.reshape(width, key_t.shape[-1])
     projected = jnp.dot(query[...], key_t, preferred_element_type=jnp.float32) * width ** (-0.5)
@@ -385,10 +392,7 @@
             share = jnp.exp(scores - top).astype(BF)
             weights[image, rows, :] = share
             numer = lax.dot_general(
-                share,
-                normed[image],
-                (((1,), (1,)), ((), ())),
-                preferred_element_type=jnp.float32,
+                share, normed[image], NT, preferred_element_type=jnp.float32
             )
             lane = lax.broadcasted_iota(jnp.int32, numer.shape, 1)
             outgoing[image, rows, 0:padded] = jnp.where(lane == channels, top, numer).astype(BF)
@@ -466,6 +470,7 @@
             jax.ShapeDtypeStruct((batches, all_rows, lanes), BF),
             jax.ShapeDtypeStruct((group, batches, lat_rows, lanes), BF),
             jax.ShapeDtypeStruct((all_rows, lanes), BF),
+            jax.ShapeDtypeStruct((all_rows, width), BF),
         ),
         in_specs=[vmem] * 7,
         out_specs=(
@@ -479,6 +484,7 @@
             anywhere,
             anywhere,
             vmem,
+            anywhere,
         ),
         scratch_shapes=[
             pltpu.VMEM((3, owned, row_block, col_block), BF),
@@ -492,7 +498,7 @@
             pltpu.VMEM((batches, all_rows, lanes), BF),
             pltpu.SemaphoreType.DMA((copies,)),
             pltpu.SemaphoreType.DMA((copies,)),
-            pltpu.SemaphoreType.DMA((4 + 4 * batches,)),
+            pltpu.SemaphoreType.DMA((5 + 4 * batches,)),
         ],
         compiler_params=pltpu.CompilerParams(
             collective_id=0, has_side_effects=True, vmem_limit_bytes=56 * 2**20
@@ -505,6 +511,693 @@
         proj_blocks,
         own_keyval,
         latents.astype(BF),
+    )
+
+
+def add_low(former, latter):
+    return (former.astype(jnp.float32) + latter.astype(jnp.float32)).astype(BF)
+
+
+class Reduce:
+    def __init__(self, place, links, term, buffers, along, base=0):
+        self.place, self.links, self.term, self.along = place, links, term, along
+        self.by_core, self.by_first, self.by_second, self.by_z = buffers
+        self.base = base
+        self.waiting = []
+
+    def wait(self):
+        arrived(self.waiting)
+        self.waiting = []
+
+    def push_core(self):
+        place = self.place
+        every = slice(None)
+        self.waiting = [
+            self.links.push(
+                self.term.at[every, every, every, 1 - place.c],
+                self.by_core,
+                place.z,
+                place.p + 1 - 2 * place.c,
+            )
+        ]
+
+    def push_first(self):
+        place = self.place
+        self.wait()
+
+        @pl.loop(0, self.by_core.shape[0])
+        def _(level):
+            self.by_core[level] = add_low(
+                self.by_core[level], self.term[level, :, :, place.c]
+            )
+
+        every = slice(None)
+        for step in range(1, place.nx if self.along == "x" else place.ny):
+            if self.along == "x":
+                xx = lax.rem(place.x + step, place.nx)
+                source = self.by_core.at[every, every, xx]
+                target = place.pix(place.y, xx, place.c)
+            else:
+                yy = lax.rem(place.y + step, place.ny)
+                source = self.by_core.at[every, yy]
+                target = place.pix(yy, place.x, place.c)
+            self.waiting.append(
+                self.links.push(source, self.by_first.at[step - 1], place.z, target)
+            )
+
+    def push_second(self):
+        place = self.place
+        self.wait()
+        if self.along == "x":
+            held = self.by_core[:, :, place.x].astype(jnp.float32)
+        else:
+            held = self.by_core[:, place.y].astype(jnp.float32)
+        for slot in range(self.by_first.shape[0]):
+            held = held + self.by_first[slot].astype(jnp.float32)
+        self.by_first[0] = held.astype(BF)
+        every = slice(None)
+        for step in range(1, place.ny if self.along == "x" else place.nx):
+            if self.along == "x":
+                other = lax.rem(place.y + step, place.ny)
+                target = place.pix(other, place.x, place.c)
+            else:
+                other = lax.rem(place.x + step, place.nx)
+                target = place.pix(place.y, other, place.c)
+            self.waiting.append(
+                self.links.push(
+                    self.by_first.at[0, every, other],
+                    self.by_second.at[step - 1],
+                    place.z,
+                    target,
+                )
+            )
+
+    def push_z(self):
+        place = self.place
+        self.wait()
+        mine = place.y if self.along == "x" else place.x
+        held = self.by_first[0, :, mine].astype(jnp.float32)
+        for slot in range(self.by_second.shape[0]):
+            held = held + self.by_second[slot].astype(jnp.float32)
+        self.by_second[0] = held.astype(BF)
+        self.sends = []
+        for step in range(1, place.nz):
+            zz = lax.rem(place.z - step + place.nz, place.nz)
+            if self.base == 0:
+                self.waiting.append(
+                    self.links.push(
+                        self.by_second.at[0, zz], self.by_z.at[step - 1], zz, place.p
+                    )
+                )
+            else:
+                level = jnp.maximum(zz - self.base, 0)
+                copy = self.links.make(
+                    self.by_second.at[0, level], self.by_z.at[step - 1], zz, place.p
+                )
+                pl.when(zz >= self.base)(copy.start)
+                self.sends.append((zz, copy))
+
+    def total(self):
+        place = self.place
+        level = place.z
+        if self.base == 0:
+            self.wait()
+        else:
+            level = jnp.maximum(place.z - self.base, 0)
+
+            @pl.when(place.z >= self.base)
+            def _():
+                for _, copy in self.sends:
+                    copy.wait_recv()
+
+            for zz, copy in self.sends:
+                pl.when(zz >= self.base)(copy.wait_send)
+        held = self.by_second[0, level].astype(jnp.float32)
+        return held, [self.by_z.at[slot] for slot in range(self.by_z.shape[0])]
+
+
+def block_index(block, col_blocks, owned):
+    every = slice(None)
+    if 2 * owned == col_blocks:
+        return (every, every, every, block // owned, block % owned)
+    return (every, every, block // 2, block % 2, 0)
+
+
+def back_kernel(
+    dims,
+    channels,
+    landed,
+    all_keyval,
+    all_mats,
+    normed_all,
+    inverse,
+    weights_all,
+    sent_all,
+    pixel_query,
+    latents,
+    mlp_gain,
+    grad_rows,
+    gain_cols,
+    gain_back,
+    mixed,
+    pixel_grad,
+    mats_grad,
+    value_grad,
+    query_total,
+    gain_total,
+    residual_total,
+    came,
+    values,
+    mats,
+    normed,
+    weights,
+    tops,
+    attended_chan,
+    attended,
+    middle,
+    mid_hat,
+    mid_inverse,
+    mid_normed,
+    slope,
+    hidden,
+    grad_pre,
+    grad_mid_normed,
+    grad_mid,
+    grad_attended,
+    shares,
+    query_turned,
+    query_acc,
+    gain_acc,
+    staged,
+    terms,
+    buffers,
+    query_low,
+    query_came,
+    query_levels,
+    gain_plane,
+    gain_levels,
+    residual_levels,
+    send_sems,
+    recv_sems,
+    local_sems,
+):
+    place = Place(*dims)
+    links = Links(send_sems, recv_sems)
+    z, y, x, c, p = place.z, place.y, place.x, place.c, place.p
+    group, batches, lat_rows, lanes = landed.shape
+    rows = batches * lat_rows
+    all_rows = group * lat_rows
+    width = latents.shape[1]
+    padded, shard_pixels = normed_all.shape[1:]
+    owned, row_block, col_block = all_mats.shape[5:]
+    col_blocks = width // col_block
+    every = slice(None)
+    tile = 256
+    tiles = width // tile
+    local = []
+
+    def local_copy(source, target):
+        copy = pltpu.make_async_copy(source, target, local_sems.at[len(local)])
+        copy.start()
+        local.append(copy)
+        return copy
+
+    came_copy = local_copy(landed, came)
+    values_copy = local_copy(all_keyval.at[pl.ds(place.nz // 2, place.nz // 2)], values)
+    mats_copies = []
+    for mat in range(3):
+        copies = []
+        for block in range(col_blocks):
+            where = block_index(block, col_blocks, owned)
+            source = all_mats.at[where[:4] + (mat,) + where[4:]]
+            cols = pl.ds(block * col_block, col_block)
+            lead = (mat,) + (every,) * (len(mats.shape) - 2)
+            copies.append(local_copy(source, mats.at[lead + (cols,)]))
+        mats_copies.append(copies)
+    tops_copy = local_copy(sent_all.at[:, :, pl.ds(lanes - 128, 128)], tops)
+
+    def fetch(image):
+        slot = image % 2
+        return [
+            local_copy(normed_all.at[image], normed.at[slot]),
+            local_copy(weights_all.at[image], weights.at[slot]),
+        ]
+
+    fetched = [fetch(0), fetch(1)]
+    place.barrier()
+
+    def columns_of(mat, index):
+        lead = (mat,) + (every,) * (len(mats.shape) - 2)
+        return mats[lead + (slice(index * tile, (index + 1) * tile),)].reshape(width, tile)
+
+    def rows_of(mat, index):
+        return mats[mat, index].reshape(-1, width)
+
+    row_tile = width // place.nz
+
+    came_copy.wait()
+    lane = lax.broadcasted_iota(jnp.int32, (rows, lanes), 1)
+    parts = [came[g].reshape(rows, lanes).astype(jnp.float32) for g in range(group)]
+    top = [part[:, channels : channels + 1] for part in parts]
+    peak = functools.reduce(jnp.maximum, top)
+    factor = [jnp.exp(value - peak) for value in top]
+    denominator = sum(f * part[:, channels + 1 : channels + 2] for f, part in zip(factor, parts))
+    summed = sum(f * part for f, part in zip(factor, parts))
+    attended_chan[...] = jnp.where(lane < channels, summed / denominator, 0.0).astype(BF)
+
+    values_copy.wait()
+    value_t = values[...].reshape(width, lanes)
+    attended[...] = lax.dot_general(
+        attended_chan[...], value_t, NT, preferred_element_type=jnp.float32
+    ).astype(BF)
+    arrived_local(mats_copies[0])
+    for index in range(tiles):
+        cols = slice(index * tile, (index + 1) * tile)
+        own = latents[:, cols]
+        middle[:, cols] = jnp.concatenate([own] * batches, axis=0) + jnp.dot(
+            attended[...], columns_of(0, index), preferred_element_type=jnp.float32
+        )
+
+    @pl.loop(0, rows // lat_rows)
+    def _(step):
+        part = pl.ds(pl.multiple_of(step * lat_rows, lat_rows), lat_rows)
+        value = middle[part, :]
+        value = value - jnp.mean(value, axis=1, keepdims=True)
+        scale = lax.rsqrt(jnp.mean(value * value, axis=1, keepdims=True) + EPSILON)
+        value = value * scale
+        mid_hat[part, :] = value
+        mid_inverse[part, :] = jnp.broadcast_to(scale, (lat_rows, 128))
+        mid_normed[part, :] = (value * mlp_gain[...]).astype(BF)
+
+    arrived_local(mats_copies[1])
+    for index in range(tiles):
+        cols = slice(index * tile, (index + 1) * tile)
+        pre = jnp.dot(mid_normed[...], columns_of(1, index), preferred_element_type=jnp.float32)
+        below = 0.5 + 0.5 * lax.erf(pre * 0.5**0.5)
+        hidden[:, cols] = (pre * below).astype(BF)
+        slope[:, cols] = below + pre * jnp.exp(-0.5 * pre * pre) * (0.5 / math.pi) ** 0.5
+
+    half_rows = row_block // 2
+
+    def store_term(targets, left, right):
+        turned = left[...].T
+        for pair in range(col_blocks // 2):
+            cols = slice(2 * pair * col_block, 2 * (pair + 1) * col_block)
+            product = jnp.dot(turned, right[:, cols], preferred_element_type=jnp.float32).astype(
+                BF
+            )
+            for side in range(2):
+                where = block_index(2 * pair + side, col_blocks, owned)
+                block = product[:, side * col_block : (side + 1) * col_block]
+                taken = 0
+                for target in targets:
+                    height = target.shape[-2]
+                    pieces = block.reshape(-1, row_block, col_block)[:, taken : taken + height]
+                    taken += height
+                    shape = target.shape
+                    lead = shape[:3] if 2 * owned == col_blocks else shape[:2]
+                    target[where] = pieces.reshape(lead + (height, col_block))
+
+    jobs = [
+        Reduce(place, links, terms[0], buffers[0], "y"),
+        Reduce(place, links, terms[1], buffers[1], "x"),
+        Reduce(place, links, terms[2], buffers[2], "x"),
+        Reduce(place, links, terms[3], buffers[3], "y"),
+        Reduce(place, links, terms[4], buffers[4], "x", place.nz // 2),
+    ]
+    down, inward, out_a, out_b, value_job = jobs
+    store_term([terms[0]], hidden, grad_rows)
+    down.push_core()
+
+    arrived_local(mats_copies[2])
+    for index in range(place.nz):
+        cols = slice(index * row_tile, (index + 1) * row_tile)
+        grad_hidden = lax.dot_general(
+            grad_rows[...], rows_of(2, index), NT, preferred_element_type=jnp.float32
+        )
+        grad_pre[:, cols] = (
+            grad_hidden.astype(BF).astype(jnp.float32) * slope[:, cols]
+        ).astype(BF)
+    down.push_first()
+    gain_plane[p] = jnp.zeros(gain_plane.shape[1:], jnp.float32)
+    for index in range(place.nz):
+        cols = slice(index * row_tile, (index + 1) * row_tile)
+        part = lax.dot_general(
+            grad_pre[...], rows_of(1, index), NT, preferred_element_type=jnp.float32
+        )
+        grad_mid_normed[:, cols] = part
+        summed_rows = jnp.sum(part * mid_hat[:, cols], axis=0, keepdims=True)
+        for sub in range(row_tile // 128):
+            row = index * (row_tile // 128) + sub
+            gain_plane[p, row : row + 1, :] = summed_rows[:, sub * 128 : (sub + 1) * 128]
+
+    @pl.loop(0, rows // lat_rows)
+    def _(step):
+        part = pl.ds(pl.multiple_of(step * lat_rows, lat_rows), lat_rows)
+        grad = grad_mid_normed[part, :] * mlp_gain[...]
+        hat = mid_hat[part, :]
+        grad = (
+            grad
+            - jnp.mean(grad, axis=1, keepdims=True)
+            - hat * jnp.mean(grad * hat, axis=1, keepdims=True)
+        ) * mid_inverse[part, 0:1]
+        grad_mid[part, :] = (grad_rows[part, :].astype(jnp.float32) + grad).astype(BF)
+
+    for index in range(place.nz):
+        cols = slice(index * row_tile, (index + 1) * row_tile)
+        grad_attended[:, cols] = lax.dot_general(
+            grad_mid[...], rows_of(0, index), NT, preferred_element_type=jnp.float32
+        ).astype(BF)
+    grad_chan = jnp.dot(grad_attended[...], value_t, preferred_element_type=jnp.float32)
+    row_delta = jnp.sum(attended_chan[...].astype(jnp.float32) * grad_chan, axis=1, keepdims=True)
+    back = jnp.where(lane == channels + 1, row_delta, grad_chan) / denominator
+    back = jnp.where(lane == channels, peak, back)
+    shares[y, x, c] = back.astype(BF).reshape(batches, lat_rows, lanes)
+
+    share_first = []
+    for image in range(batches):
+        share_first.append(
+            place.push_first(links, shares, (), (image,), "xy"[image % 2])
+        )
+    store_term([terms[1]], mid_normed, grad_pre)
+    inward.push_core()
+    share_second = []
+    for image in range(batches):
+        arrived(share_first[image])
+        share_second.append(
+            place.push_second(links, shares, (), (image,), "xy"[image % 2])
+        )
+    store_term([terms[2], terms[3]], attended, grad_mid)
+    out_a.push_core()
+    out_b.push_core()
+    share_core = []
+    for image in range(batches):
+        arrived(share_second[image])
+        held = shares.at[:, :, c, image]
+        share_core.append([links.push(held, held, z, p + 1 - 2 * c)])
+    terms[4][...] = (
+        jnp.dot(grad_attended[...].T, attended_chan[...], preferred_element_type=jnp.float32)
+        .astype(BF)
+        .reshape(terms[4].shape)
+    )
+    value_job.push_core()
+    residual = sum(
+        grad_mid[image * lat_rows : (image + 1) * lat_rows].astype(jnp.float32)
+        for image in range(batches)
+    )
+    residual_levels[z] = residual.astype(BF)
+    residual_sent = []
+    for step in range(1, place.nz):
+        level = residual_levels.at[z]
+        residual_sent.append(
+            links.push(level, level, lax.rem(z + step, place.nz), p)
+        )
+    inward.push_first()
+    down.push_second()
+
+    lane_all = lax.broadcasted_iota(jnp.int32, (all_rows, lanes), 1)
+    query_turned[...] = jnp.where(
+        lane_all < channels, pixel_query[...].astype(jnp.float32), 0.0
+    ).T[0:padded].astype(BF)
+    query_acc[...] = jnp.zeros(query_acc.shape, jnp.float32)
+    gain_acc[...] = jnp.zeros(gain_acc.shape, jnp.float32)
+    chunk = min(512, shard_pixels)
+    staged_out = []
+    tops_copy.wait()
+
+    def attend_back(image):
+        slot = image % 2
+        arrived(share_core[image])
+        arrived_local(fetched[image])
+        if image >= 2:
+            staged_out[image - 2].wait()
+        back = shares[:, :, :, image].reshape(all_rows, lanes).astype(jnp.float32)
+        top = tops[image].astype(jnp.float32)[:, channels - (lanes - 128) :][:, 0:1]
+        share = jnp.exp(top - back[:, channels : channels + 1])
+        back = jnp.where(lane_all == channels, 0.0, back * share)
+        back = jnp.where(lane_all > channels + 1, 0.0, back)
+        back_low = jnp.where(lane_all == channels + 1, -back, back).astype(BF)[:, 0:padded]
+        back_turned = jnp.where(lane_all < channels, back, 0.0).T[0:padded].astype(BF)
+
+        @pl.loop(0, shard_pixels // chunk)
+        def _(step):
+            cols = pl.ds(pl.multiple_of(step * chunk, chunk), chunk)
+            normed_chunk = normed[slot, :, cols]
+            share_chunk = weights[slot, :, cols]
+            grad_weights = jnp.dot(back_low, normed_chunk, preferred_element_type=jnp.float32)
+            grad_scores = (share_chunk.astype(jnp.float32) * grad_weights).astype(BF)
+            query_acc[:, 0:padded] += lax.dot_general(
+                grad_scores, normed_chunk, NT, preferred_element_type=jnp.float32
+            )
+            grad_normed = jnp.dot(
+                query_turned[...], grad_scores, preferred_element_type=jnp.float32
+            ) + jnp.dot(back_turned, share_chunk, preferred_element_type=jnp.float32)
+            normal = normed_chunk.astype(jnp.float32)
+            product = grad_normed * normal
+            folded = sum(product[:, at : at + 128] for at in range(0, chunk, 128))
+            gain_acc[0:padded, :] += folded
+            second_mean = jnp.sum(product, axis=0, keepdims=True) / channels
+            spread = jnp.concatenate([gain_cols[...]] * (chunk // 128), axis=1)
+            spread_back = jnp.concatenate([gain_back[...]] * (chunk // 128), axis=1)
+            grad_hat = grad_normed * spread
+            first_mean = jnp.sum(grad_hat, axis=0, keepdims=True) / channels
+            result = (grad_hat - first_mean - normal * spread_back * second_mean) * inverse[
+                image : image + 1, cols
+            ]
+            staged[slot, :, cols] = result[0:channels]
+
+        staged_out.append(local_copy(staged.at[slot], pixel_grad.at[image]))
+        if image + 2 < batches:
+            fetched.append(fetch(image + 2))
+
+    attend_back(0)
+    out_a.push_first()
+    out_b.push_first()
+    value_job.push_first()
+    inward.push_second()
+    down.push_z()
+    attend_back(1)
+    out_a.push_second()
+    out_b.push_second()
+    value_job.push_second()
+    inward.push_z()
+    attend_back(2)
+    out_a.push_z()
+    out_b.push_z()
+    value_job.push_z()
+    attend_back(3)
+
+    query_low[...] = query_acc[...].astype(BF)
+    query_sent = []
+    for step in range(1, group):
+        q = lax.rem(p + step, group)
+        part = pl.ds(pl.multiple_of(q * lat_rows, lat_rows), lat_rows)
+        query_sent.append(links.push(query_low.at[part], query_came.at[step - 1], z, q))
+    gain_rows = lax.dot_general(
+        jnp.ones((8, 128), jnp.float32),
+        gain_acc[...],
+        NT,
+        precision=HIGHEST,
+        preferred_element_type=jnp.float32,
+    )
+    for sub in range(lanes // 128):
+        row = width // 128 + sub
+        gain_plane[p, row : row + 1, :] = gain_rows[0:1, sub * 128 : (sub + 1) * 128]
+    gain_sent = []
+    for step in range(1, group):
+        own = gain_plane.at[p]
+        gain_sent.append(links.push(own, own, z, lax.rem(p + step, group)))
+
+    def finish(job, target):
+        held, came_z = job.total()
+        for part in came_z:
+            held = held + part[...].astype(jnp.float32)
+        target[...] = held
+
+    finish(down, mats_grad.at[2])
+    finish(inward, mats_grad.at[1])
+    finish(out_a, mats_grad.at[0, :, pl.ds(0, half_rows)])
+    finish(out_b, mats_grad.at[0, :, pl.ds(half_rows, half_rows)])
+
+    arrived(query_sent)
+    own_rows = pl.ds(pl.multiple_of(p * lat_rows, lat_rows), lat_rows)
+    held = query_acc[own_rows, :]
+    for slot in range(group - 1):
+        held = held + query_came[slot].astype(jnp.float32)
+    query_levels[z] = held.astype(BF)
+    query_up = []
+    for step in range(1, place.nz):
+        own = query_levels.at[z]
+        query_up.append(links.push(own, own, lax.rem(z + step, place.nz), p))
+    arrived(gain_sent)
+    gain_levels[z] = sum(gain_plane[g] for g in range(group))
+    gain_up = []
+    for step in range(1, place.nz):
+        own = gain_levels.at[z]
+        gain_up.append(links.push(own, own, lax.rem(z + step, place.nz), p))
+
+    held, came_z = value_job.total()
+    above = place.z >= place.nz // 2
+    for part in came_z:
+        held = held + part[...].astype(jnp.float32)
+    value_grad[...] = jnp.where(above, held, 0.0)
+    arrived(residual_sent)
+    residual_total[...] = sum(residual_levels[zz].astype(jnp.float32) for zz in range(place.nz))
+
+    arrived(query_up)
+    query_total[p] = sum(query_levels[zz].astype(jnp.float32) for zz in range(place.nz)).astype(BF)
+    query_all = []
+    for step in range(1, group):
+        own = query_total.at[p]
+        query_all.append(links.push(own, own, z, lax.rem(p + step, group)))
+    arrived(gain_up)
+    gain_total[...] = sum(gain_levels[zz] for zz in range(place.nz))
+    for index in range(tiles):
+        cols = slice(index * tile, (index + 1) * tile)
+        mixed[:, cols] = (
+            middle[:, cols]
+            + jnp.dot(hidden[...], columns_of(2, index), preferred_element_type=jnp.float32)
+        ).astype(BF)
+    arrived(query_all)
+    links.drain()
+    for copy in staged_out[batches - 2 :]:
+        copy.wait()
+
+
+def arrived_local(copies):
+    for copy in copies:
+        copy.wait()
+
+
+def back_copies(nz, ny, nx, batches):
+    group = 2 * ny * nx
+    both = nx + ny - 2
+    count = batches // 2 * 2 * both + batches
+    count += 5 * (1 + both + nz - 1)
+    count += 2 * (nz - 1) + group - 1 + group - 1 + nz - 1 + group - 1
+    return count
+
+
+def back(dims, channels, gathered, latents, mlp_gain, in_gain, mixed_grad):
+    landed, all_keyval, all_mats, normed_all, inverse, weights_all, sent_all, pixel_query = gathered
+    nz, ny, nx = dims
+    group, batches, lat_rows, lanes = landed.shape
+    rows = batches * lat_rows
+    all_rows = group * lat_rows
+    width = latents.shape[1]
+    padded, shard_pixels = normed_all.shape[1:]
+    owned, row_block, col_block = all_mats.shape[5:]
+    keyval_rows = all_keyval.shape[4]
+    half_rows = row_block // 2
+    column = jnp.pad(in_gain, (0, padded - channels))[:, None]
+    column_back = jnp.pad(1.0 / in_gain, (0, padded - channels))[:, None]
+    gain_cols = jnp.broadcast_to(column, (padded, 128))
+    gain_back = jnp.broadcast_to(column_back, (padded, 128))
+    vmem = pl.BlockSpec(memory_space=pltpu.VMEM)
+    anywhere = pl.BlockSpec(memory_space=pl.ANY)
+    lead = (nz, ny, nx) if 2 * owned * col_block == width else (nz, ny)
+    cube = (nz, ny, nx, 2)
+    inners = [
+        (nz, (owned, row_block, col_block), "y"),
+        (nz, (owned, row_block, col_block), "x"),
+        (nz, (owned, half_rows, col_block), "x"),
+        (nz, (owned, half_rows, col_block), "y"),
+        (nz // 2, (keyval_rows, lanes), "x"),
+    ]
+    terms = [pltpu.VMEM((levels, ny, nx, 2) + inner, BF) for levels, inner, _ in inners]
+    buffers = []
+    for levels, inner, along in inners:
+        one, two = (nx, ny) if along == "x" else (ny, nx)
+        buffers.append(
+            [
+                pltpu.VMEM((levels, ny, nx) + inner, BF),
+                pltpu.VMEM((one - 1, levels, two) + inner, BF),
+                pltpu.VMEM((two - 1, levels) + inner, BF),
+                pltpu.VMEM((nz - 1,) + inner, BF),
+            ]
+        )
+    wide = lambda kind: pltpu.VMEM((rows, width), kind)
+    copies = back_copies(nz, ny, nx, batches)
+    return pl.pallas_call(
+        functools.partial(back_kernel, dims, channels),
+        out_shape=(
+            jax.ShapeDtypeStruct((rows, width), BF),
+            jax.ShapeDtypeStruct((batches, channels, shard_pixels), jnp.float32),
+            jax.ShapeDtypeStruct((3, owned, row_block, col_block), jnp.float32),
+            jax.ShapeDtypeStruct((keyval_rows, lanes), jnp.float32),
+            jax.ShapeDtypeStruct((group, lat_rows, lanes), BF),
+            jax.ShapeDtypeStruct((16, 128), jnp.float32),
+            jax.ShapeDtypeStruct((lat_rows, width), jnp.float32),
+        ),
+        in_specs=[
+            anywhere,
+            anywhere,
+            anywhere,
+            anywhere,
+            vmem,
+            anywhere,
+            anywhere,
+            vmem,
+            vmem,
+            vmem,
+            vmem,
+            vmem,
+            vmem,
+        ],
+        out_specs=(vmem, anywhere, vmem, vmem, vmem, vmem, vmem),
+        scratch_shapes=[
+            pltpu.VMEM((group, batches, lat_rows, lanes), BF),
+            pltpu.VMEM((nz // 2, ny, nx, 2, keyval_rows, lanes), BF),
+            pltpu.VMEM((3,) + lead + (row_block, width), BF),
+            pltpu.VMEM((2, padded, shard_pixels), BF),
+            pltpu.VMEM((2, all_rows, shard_pixels), BF),
+            pltpu.VMEM((batches, all_rows, 128), BF),
+            pltpu.VMEM((rows, lanes), BF),
+            wide(BF),
+            wide(jnp.float32),
+            wide(jnp.float32),
+            pltpu.VMEM((rows, 128), jnp.float32),
+            wide(BF),
+            wide(jnp.float32),
+            wide(BF),
+            wide(BF),
+            wide(jnp.float32),
+            wide(BF),
+            wide(BF),
+            pltpu.VMEM(cube[1:] + (batches, lat_rows, lanes), BF),
+            pltpu.VMEM((padded, all_rows), BF),
+            pltpu.VMEM((all_rows, lanes), jnp.float32),
+            pltpu.VMEM((lanes, 128), jnp.float32),
+            pltpu.VMEM((2, channels, shard_pixels), jnp.float32),
+            terms,
+            buffers,
+            pltpu.VMEM((all_rows, lanes), BF),
+            pltpu.VMEM((group - 1, lat_rows, lanes), BF),
+            pltpu.VMEM((nz, lat_rows, lanes), BF),
+            pltpu.VMEM((group, 16, 128), jnp.float32),
+            pltpu.VMEM((nz, 16, 128), jnp.float32),
+            pltpu.VMEM((nz, lat_rows, width), BF),
+            pltpu.SemaphoreType.DMA((copies,)),
+            pltpu.SemaphoreType.DMA((copies,)),
+            pltpu.SemaphoreType.DMA((3 + 3 * (width // col_block) + 3 * batches,)),
+        ],
+        compiler_params=pltpu.CompilerParams(
+            collective_id=1, has_side_effects=True, vmem_limit_bytes=61 * 2**20
+        ),
+    )(
+        landed,
+        all_keyval,
+        all_mats,
+        normed_all,
+        inverse,
+        weights_all,
+        sent_all,
+        pixel_query,
+        latents,
+        mlp_gain[None, :],
+        mixed_grad.reshape(rows, width),
+        gain_cols,
+        gain_back,
     )
 
 
@@ -548,105 +1241,46 @@
         sent_all,
         landed,
         pixel_query,
+        query,
     ) = front(dims, pixels, pixel_mask, in_gain, lat_gain, proj_blocks, keyval_weight, latents)
+    gathered = (
+        landed,
+        keyval_t,
+        mats,
+        normed_all,
+        inverse_all,
+        weights_all,
+        sent_all,
+        pixel_query,
+    )
+    mixed, pixel_grad, triple_owned, value_grad, query_total, gain_total, residual_total = back(
+        dims, channels, gathered, latents, mlp_gain, in_gain, mixed_grad
+    )
+    query_sum = query_total.reshape(all_rows, -1)[:, :channels]
+    gain_rows = gain_total.reshape(-1)
+    mlp_gain_sum = gain_rows[:width]
+    in_gain_sum = gain_rows[width : width + channels] / in_gain
     latent_all = latent_all.reshape(all_rows, width).astype(jnp.float32)
-    keyval_t = keyval_t.reshape(2 * width, -1)[:, :channels]
-    pixel_query = pixel_query[:, :channels]
+    key_t = keyval_t.reshape(2 * width, -1)[:width, :channels]
     query_weight = assemble(query_blocks, width, row_block, col_block)
-    rest_blocks = mats.reshape(-1, 3, owned_count, row_block, col_block).swapaxes(0, 1)
-    output_weight = assemble(rest_blocks[0], width, row_block, col_block)
-    mlp_in = assemble(rest_blocks[1], width, row_block, col_block)
-    mlp_out = assemble(rest_blocks[2], width, row_block, col_block)
-    key_t = keyval_t[:width]
-    value_t = keyval_t[width:]
     lat_hat, lat_inverse = normalize_parts(latent_all, 1)
     lat_normed = (lat_hat * lat_gain[None, :]).astype(BF)
-    query = matmul(lat_normed, query_weight).astype(BF)
-
-    incoming = landed.reshape(groups, batches * lat_rows, -1)
-    top_in = incoming[:, :, channels].astype(jnp.float32)
-    total_in = incoming[:, :, channels + 1].astype(jnp.float32)
-    peak = jnp.max(top_in, axis=0)
-    factor = jnp.exp(top_in - peak[None, :])
-    denominator = jnp.sum(factor * total_in, axis=0)
-    summed = jnp.sum(factor[:, :, None] * incoming[:, :, :channels].astype(jnp.float32), axis=0)
-    attended_chan = (summed / denominator[:, None]).astype(BF)
-
-    attended = contract(attended_chan, value_t, 1, 1)
-    attended_low = attended.astype(BF)
-    latents_tiled = jnp.tile(latents, (batches, 1))
-    middle = latents_tiled + matmul(attended_low, output_weight)
-    mid_hat, mid_inverse = normalize_parts(middle, 1)
-    mid_normed = (mid_hat * mlp_gain[None, :]).astype(BF)
-    pre_act = matmul(mid_normed, mlp_in)
-    hidden, gelu_pull = jax.vjp(gelu_exact, pre_act)
-    hidden_low = hidden.astype(BF)
-    mixed = (middle + matmul(hidden_low, mlp_out)).astype(BF)
-    grad_rows = mixed_grad.reshape(batches * lat_rows, width)
-    grad_hidden = contract(grad_rows, mlp_out, 1, 1).astype(BF)
-    (slope_grad,) = gelu_pull(grad_hidden.astype(jnp.float32))
-    grad_pre = slope_grad.astype(BF)
-    grad_mid_normed = contract(grad_pre, mlp_in, 1, 1)
-    mlp_gain_part = jnp.sum(grad_mid_normed * mid_hat, axis=0)
-    grad_mid = (
-        grad_rows.astype(jnp.float32)
-        + normalize_back(grad_mid_normed * mlp_gain[None, :], mid_hat, mid_inverse, 1)
-    ).astype(BF)
-    grad_attended = contract(grad_mid, output_weight, 1, 1).astype(BF)
-    row_delta = jnp.sum(attended * grad_attended.astype(jnp.float32), axis=1)
-    grad_chan = (matmul(grad_attended, value_t) / denominator[:, None]).astype(BF)
-    delta_low = (row_delta / denominator).astype(BF)
-    back_own = jnp.concatenate([grad_chan, peak.astype(BF)[:, None], delta_low[:, None]], axis=1)
-    back_own = back_own.reshape(batches, lat_rows, channels + 2)
-    back_all = lax.all_gather(back_own, "pix", axis=1, tiled=True)
-
-    out_term = split_blocks(contract(attended_low, grad_mid, 0, 0).astype(BF), row_block, col_block)
-    in_term = split_blocks(contract(mid_normed, grad_pre, 0, 0).astype(BF), row_block, col_block)
-    down_term = split_blocks(contract(hidden_low, grad_rows, 0, 0).astype(BF), row_block, col_block)
-    triple_term = jnp.stack([out_term, in_term, down_term], axis=1)
-    triple_owned = lax.psum_scatter(triple_term, everyone, scatter_dimension=0, tiled=True)
-    residual = jnp.sum(grad_mid.astype(jnp.float32).reshape(batches, lat_rows, width), axis=0)
-    residual_total = lax.psum(residual.astype(BF), "samp").astype(jnp.float32)
-
-    query_acc = jnp.zeros((all_rows, channels), jnp.float32)
-    in_gain_part = jnp.zeros((channels,), jnp.float32)
-    pixel_list = []
-    for slot in range(batches):
-        normed = normed_all[slot, :channels]
-        top = sent_all[slot, :, channels]
-        weights = weights_all[slot]
-        back = back_all[slot]
-        share = jnp.exp(top.astype(jnp.float32) - back[:, channels].astype(jnp.float32))
-        back_chan = (back[:, :channels].astype(jnp.float32) * share[:, None]).astype(BF)
-        back_total = share * back[:, channels + 1].astype(jnp.float32)
-        grad_weights = matmul(back_chan, normed) - back_total[:, None]
-        grad_scores = (weights.astype(jnp.float32) * grad_weights).astype(BF)
-        query_acc = query_acc + contract(grad_scores, normed, 1, 1)
-        grad_normed = contract(pixel_query, grad_scores, 0, 0) + contract(back_chan, weights, 0, 0)
-        normal_hat, inverse = normalize_parts(pixels[slot].astype(jnp.float32), 0)
-        in_gain_part = in_gain_part + jnp.sum(grad_normed * normal_hat, axis=1)
-        pixel_list.append(
-            normalize_back(grad_normed * in_gain[:, None], normal_hat, inverse, 0)
-        )
-    pixel_grad = jnp.stack(pixel_list, axis=0)
-
-    query_sum, in_gain_sum, mlp_gain_sum = lax.psum(
-        (query_acc, in_gain_part, mlp_gain_part), everyone
-    )
-    value_term = contract(grad_attended, attended_chan, 0, 0)
-    key_term = contract(query, query_acc.astype(BF), 0, 0) * scale
-    keyval_term = jnp.concatenate([key_term, value_term], axis=0).astype(BF)
-    keyval_grad = lax.psum_scatter(keyval_term, everyone, scatter_dimension=0, tiled=True)
-    keyval_grad = keyval_grad.astype(jnp.float32).T
-
-    grad_query = (contract(query_sum.astype(BF), key_t, 1, 1) * scale).astype(BF)
+
+    key_rows = keyval_weight.shape[1]
+    device = lax.axis_index(everyone)
+    half_devices = width // key_rows
+    own_query = lax.dynamic_slice_in_dim(query, device % half_devices * key_rows, key_rows, 1)
+    key_grad = contract(query_sum, own_query, 0, 0) * scale
+    keyval_grad = jnp.where(device < half_devices, key_grad, value_grad[:, :channels].T)
+
+    grad_query = (contract(query_sum, key_t, 1, 1) * scale).astype(BF)
     grad_lat_normed = contract(grad_query, query_weight, 1, 1)
     lat_gain_grad = jnp.sum(grad_lat_normed * lat_hat, axis=0)
     latent_path = normalize_back(grad_lat_normed * lat_gain[None, :], lat_hat, lat_inverse, 1)
     row_start = lax.axis_index("pix") * lat_rows
     own_path = lax.dynamic_slice_in_dim(latent_path, row_start, lat_rows, 0)
     latent_grad = residual_total + own_path
-    first_block = lax.axis_index(everyone) * owned_count
+    first_block = device * owned_count
     col_count = width // col_block
     query_list = []
     for offset in range(owned_count):
@@ -657,7 +1291,7 @@
         grad_slice = lax.dynamic_slice_in_dim(grad_query, block_col, col_block, 1)
         query_list.append(contract(normed_slice, grad_slice, 0, 0))
     query_grad = jnp.stack(query_list, axis=0)
-    proj_grad = jnp.concatenate([query_grad[:, None], triple_owned.astype(jnp.float32)], axis=1)
+    proj_grad = jnp.concatenate([query_grad[:, None], triple_owned.swapaxes(0, 1)], axis=1)
     left_new = STAT_DECAY * proj_left + (1.0 - STAT_DECAY) * jnp.einsum(
         "nsab,nscb->nsac", proj_grad, proj_grad, precision=HIGHEST
     )

time: 435 us -> 235 us (0.54)
  waiting for transfers between devices: 99.4 us -> 0 us
  Pallas kernels: 84.3 us -> 173 us
  matrix products: 77.6 us -> 23.1 us
  blocking collectives: 47.3 us -> 0 us
  local copies, waits for them, and re-layouts: 67.5 us -> 28.3 us
  other arithmetic: 34.2 us -> 5.79 us
  between operations: 16.8 us -> 1.18 us
    reduce_scatter x1 -> x0, waiting for transfers between devices: 91 us -> none  [body(): lax.psum_scatter(triple_term, everyone, scatter_dimension=0, tiled=True)]
    pallas_call x0 -> x1, Pallas kernels: none -> 88.7 us  [back(): pl.pallas_call(functools.partial(back_kernel, dims, channels), out_shape=...]
    psum x1 -> x0, blocking collectives: 47.3 us -> none  [body(): lax.psum((query_acc, in_gain_part, mlp_gain_part), everyone)]
    dot_general x27 -> x7, matrix products: 48 us -> 15.9 us  [contract(): lax.dot_general(former, latter, (((former_dim,), (latter_dim,)), ((), ())...]
    dot_general x8 -> x0, matrix products: 20.1 us -> none  [matmul(): return jnp.dot(former, latter, preferred_element_type=jnp.float32)]
    unnamed x132 -> x50, local copies, waits for them, and re-layouts: 33.7 us -> 20.1 us
    transpose x10 -> x0, local copies, waits for them, and re-layouts: 13.4 us -> none  [the longest x3 5.34 us: assemble(): return shaped.transpose(0, 2, 1, 3).reshape(model_width, model_width)]
    slice x7 -> x1, local copies, waits for them, and re-layouts: 11.5 us -> 0.01 us  [body(): mlp_gain_sum = gain_rows[:width]]
  transfers between devices with their start and end apart: 4 -> 0, of which waited for: 2 -> 0; matrix products, arithmetic and copies ran while one was open for 29% -> 0% of each run, Pallas kernels for 0% -> 0%
where the time goes in v3:
time: 235 us; the launch traced here: 231 us
  Pallas kernels  173 us (74%)
  local copies, waits for them, and re-layouts  28.3 us (12%)
  matrix products  23.1 us (10%)
  other arithmetic  5.79 us (2%)
    pallas_call x1, Pallas kernels, back(): pl.pallas_call(functools.partial(back_kernel, dims, channels), out_shape=...  88.7 us
    pallas_call x1, Pallas kernels, front(): pl.pallas_call(functools.partial(front_kernel, dims), out_shape=(jax.Shap...  84.4 us
    unnamed x50, local copies, waits for them, and re-layouts  20.1 us
    dot_general x7, matrix products, contract(): lax.dot_general(former, latter, (((former_dim,), (latter_dim,)), ((), ())...  15.9 us

profile of v3, /device:TPU:0, one launch (start us, length us, event | category | flops | bytes accessed | tf_op | source)
XLA Modules:
  0.0 231.5 jit_solution(12395675416492238333)
XLA Ops:
  0.7 0.8 broadcast_divide_fusion
  1.4 0.8 broadcast_in_dim.12.gain_cols
  2.2 1.4 fusion.36
  3.6 6.7 %copy.36.pixels = bf16[4,261,2048]{2,1,0:T(8,128)(2,1)} copy(bf16[4,261,2048]{2,0,1:T(4,128)(2,1)} %param.14) | data formatting | bytes 8552448 | tf_op args[0]
  10.2 0.7 convert_element_type.34.own_latents
  11.6 84.4 %shard_map.253 = (bf16[4,2,2,2,4,64,128]{6,5,4,3,2,1,0:T(8,128)(2,1)}, bf16[4,2,2,2,64,384]{5,4,3,2,1,0:T(8,128)(2,1)}, bf16[2,2,2,64,1024]{4,3,2,1,0:T(8,128)(2...) custom-call(bf16[4,261,2048]{2,1,0:T(8,128)(2,1)} %copy.36.pixels, ...), custom_call_target="tpu_custom_call" | custom-call | tf_op jit(solution)/shard_map/pallas_call | solution.py:460
  95.9 0.8 broadcast_in_dim.15.gain_cols
  96.7 0.8 broadcast_in_dim.16.gain_back
  97.5 88.7 %shard_map.254 = (bf16[256,1024]{1,0:T(8,128)(2,1)}, f32[4,261,2048]{2,1,0:T(8,128)}, f32[3,4,64,128]{3,2,1,0:T(8,128)}, f32[64,384]{1,0:T(8,128)}, bf16[8,64,38...) custom-call(bf16[8,4,64,384]{3,2,1,0:T(8,128)(2,1)} %get-tuple-element.33.landed, ...), custom_call_target="tpu_custom_call" | custom-call | tf_op jit(solution)/shard_map/pallas_call | solution.py:1121
  186.2 3.1 %multiply_convert_fusion = bf16[512,1024]{1,0:T(8,128)(2,1)} fusion(bf16[2048,384]{1,0:T(8,128)(2,1)} %bitcast.54, bf16[512,384]{1,0:T(8,128)(2,1)} %bitcast.61), kind=kOutput, calls=%fused_computation.7 | convolution fusion | flops 274726912 | bytes 2228224 | tf_op jit(solution)/shard_map/dot_general | solution.py:30
  190.1 3.5 %copy.41 = bf16[16,8,64,128]{3,1,2,0:T(8,128)(2,1)S(1)} copy(bf16[16,8,64,128]{3,2,1,0:T(8,128)(2,1)} %bitcast.52) | data formatting | bytes 4194304 | tf_op jit(solution)/shard_map/reshape | solution.py:57
  193.6 4.0 %fusion.31 = (f32[512]{0:T(512)S(1)}, f32[512]{0:T(512)S(1)}, f32[1024]{0:T(1024)S(1)}, f32[512,1024]{1,0:T(8,128)}, bf16[512,1024]{1,0:T(8,128)(2,1)}, /*index=5*/f32[512,1024]{1,0:T(8,128)}) fusion(f32[512]{0:T(512)S(1)} %rsqrt.12, f32[512]{0:T(512)S(1)} %div.64, bf16[2,2,2,64,1024]{4,3,2,1,0:T(8,128)(2,1)S(1)} %copy-done.2, f32[1024]{0:T(1024)S(1)} %copy-done.19, ...), kind=kOutput, calls=%fused_computation.65 | convolution fusion | flops 1079506944 | bytes 9453568 | tf_op jit(solution)/shard_map/dot_general | solution.py:30
  198.7 2.2 divide_subtract_fusion
  200.9 2.1 divide_subtract_fusion.1
  203.0 1.9 convolution_bitcast_fusion.3
  204.9 1.8 convolution_bitcast_fusion.2
  206.7 1.8 convolution_bitcast_fusion.1
  208.5 1.2 convolution_bitcast_fusion
  209.7 0.8 maximum_bitcast_fusion
  210.6 2.8 %fusion.4 = f32[4,4,128,128]{3,2,1,0:T(8,128)} fusion(f32[4,4,128,128]{3,2,1,0:T(8,128)S(1)} %copy-done.6, f32[4,4,64,128]{3,2,1,0:T(8,128)S(1)} %copy.43), kind=kOutput, calls=%fused_computation.11 | convolution fusion | flops 201850880 | bytes 2621440 | tf_op jit(solution)/shard_map/nsab,nsac->nsbc/dot_general | solution.py:1298
  214.1 1.9 fusion.5
  215.9 2.0 fusion.6
  217.9 12.5 %copy.42 = f32[4,261,2048]{2,0,1:T(4,128)} copy(f32[4,261,2048]{2,1,0:T(8,128)} %get-tuple-element.67) | data formatting | bytes 17104896
  230.4 0.8 copy.52
  (68 shorter events, 3.2 us)
Async XLA Ops:
  0.6 213.4 %copy-start = (f32[4,4,128,128]{3,2,1,0:T(8,128)S(1)}, f32[4,4,128,128]{3,2,1,0:T(8,128)}, u32[]{:S(2)}) copy-start(f32[4,4,128,128]{3,2,1,0:T(8,128)} %param.20) | copy-start | bytes 3145732
  3.6 6.7 %copy-start.3 = (f32[64,1024]{1,0:T(8,128)S(1)}, f32[64,1024]{1,0:T(8,128)}, u32[]{:S(2)}) copy-start(f32[64,1024]{1,0:T(8,128)} %latents.1) | copy-start | bytes 786436
  3.6 7.3 %copy-start.15 = (f32[261,64]{0,1:T(8,128)S(1)}, f32[261,64]{0,1:T(8,128)}, u32[]{:S(2)}) copy-start(f32[261,64]{0,1:T(8,128)} %param.21) | copy-start | bytes 200452
  186.2 3.1 %copy-start.2 = (bf16[2,2,2,64,1024]{4,3,2,1,0:T(8,128)(2,1)S(1)}, bf16[2,2,2,64,1024]{4,3,2,1,0:T(8,128)(2,1)}, u32[]{:S(2)}) copy-start(bf16[2,2,2,64,1024]{4,3,2,1,0:T(8,128)(2,1)} %get-tuple-element.43) | copy-start | bytes 3145732
  190.1 3.5 %copy-start.13 = (bf16[512,1024]{1,0:T(8,128)(2,1)S(1)}, bf16[512,1024]{1,0:T(8,128)(2,1)}, u32[]{:S(2)}) copy-start(bf16[512,1024]{1,0:T(8,128)(2,1)} %multiply_convert_fusion) | copy-start | bytes 3145732
  190.1 3.5 %copy-start.19 = (f32[1024]{0:T(1024)S(1)}, f32[1024]{0:T(1024)}, u32[]{:S(2)}) copy-start(f32[1024]{0:T(1024)} %get-tuple-element.97) | copy-start | bytes 12292
  193.6 4.1 %copy-start.21 = (f32[16,128]{1,0:T(8,128)S(1)}, f32[16,128]{1,0:T(8,128)}, u32[]{:S(2)}) copy-start(f32[16,128]{1,0:T(8,128)} %get-tuple-element.50) | copy-start | bytes 24580
  193.6 4.1 %copy-start.17 = (f32[2309]{0:T(1024)S(1)}, f32[2309]{0:T(1024)}, u32[]{:S(2)}) copy-start(f32[2309]{0:T(1024)} %param.25) | copy-start | bytes 27712
  193.6 4.2 %copy-start.20 = (f32[2309]{0:T(1024)S(1)}, f32[2309]{0:T(1024)}, u32[]{:S(2)}) copy-start(f32[2309]{0:T(1024)} %param.26) | copy-start | bytes 27712
  193.6 5.1 %copy-start.4 = (f32[64,1024]{1,0:T(8,128)S(1)}, f32[64,1024]{1,0:T(8,128)}, u32[]{:S(2)}) copy-start(f32[64,1024]{1,0:T(8,128)} %latents.1) | copy-start | bytes 786436
  193.6 5.0 %copy-start.11 = (f32[64,1024]{1,0:T(8,128)S(1)}, f32[64,1024]{1,0:T(8,128)}, u32[]{:S(2)}) copy-start(f32[64,1024]{1,0:T(8,128)} %param.24) | copy-start | bytes 786436
  193.6 5.0 %copy-start.12 = (f32[64,1024]{1,0:T(8,128)S(1)}, f32[64,1024]{1,0:T(8,128)}, u32[]{:S(2)}) copy-start(f32[64,1024]{1,0:T(8,128)} %get-tuple-element.48) | copy-start | bytes 786436
  197.7 3.2 %copy-start.16 = (f32[261,64]{0,1:T(8,128)S(1)}, f32[261,64]{0,1:T(8,128)}, u32[]{:S(2)}) copy-start(f32[261,64]{0,1:T(8,128)} %param.21) | copy-start | bytes 200452
  197.7 3.2 %copy-start.22 = (f32[261,64]{0,1:T(8,128)S(1)}, f32[261,64]{0,1:T(8,128)}, u32[]{:S(2)}) copy-start(f32[261,64]{0,1:T(8,128)} %param.22) | copy-start | bytes 200452
  197.7 5.3 %copy-start.14 = (bf16[512,1024]{1,0:T(8,128)(2,1)S(1)}, bf16[512,1024]{1,0:T(8,128)(2,1)}, u32[]{:S(2)}) copy-start(bf16[512,1024]{1,0:T(8,128)(2,1)} %multiply_convert_fusion) | copy-start | bytes 3145732
  197.8 8.9 %copy-start.18 = (f32[2309]{0:T(1024)}, f32[2309]{0:T(1024)S(1)}, u32[]{:S(2)}) copy-start(f32[2309]{0:T(1024)S(1)} %concatenate.7) | copy-start | bytes 27712
  198.7 11.8 %copy-start.10 = (f32[3,4,64,128]{3,2,1,0:T(8,128)S(1)}, f32[3,4,64,128]{3,2,1,0:T(8,128)}, u32[]{:S(2)}) copy-start(f32[3,4,64,128]{3,2,1,0:T(8,128)} %get-tuple-element.45) | copy-start | bytes 1179652
  203.0 7.6 %copy-start.6 = (f32[4,4,128,128]{3,2,1,0:T(8,128)S(1)}, f32[4,4,128,128]{3,2,1,0:T(8,128)}, u32[]{:S(2)}) copy-start(f32[4,4,128,128]{3,2,1,0:T(8,128)} %param.18) | copy-start | bytes 3145732
  210.5 2.9 %copy-start.7 = (f32[4,4,64,64]{3,2,1,0:T(8,128)S(1)}, f32[4,4,64,64]{3,2,1,0:T(8,128)}, u32[]{:S(2)}) copy-start(f32[4,4,64,64]{3,2,1,0:T(8,128)} %param.19) | copy-start | bytes 786436
  210.6 5.3 %copy-start.1 = (f32[4,4,64,128]{3,2,1,0:T(8,128)}, f32[4,4,64,128]{3,2,1,0:T(8,128)S(1)}, u32[]{:S(2)}) copy-start(f32[4,4,64,128]{3,2,1,0:T(8,128)S(1)} %copy.43) | copy-start | bytes 1572868
  210.6 3.4 %copy-start.5 = (f32[4,4,64,128]{3,2,1,0:T(8,128)S(1)}, f32[4,4,64,128]{3,2,1,0:T(8,128)}, u32[]{:S(2)}) copy-start(f32[4,4,64,128]{3,2,1,0:T(8,128)} %own_proj.1) | copy-start | bytes 1572868
  213.4 2.5 %copy-start.9 = (f32[4,4,64,64]{3,2,1,0:T(8,128)S(1)}, f32[4,4,64,64]{3,2,1,0:T(8,128)}, u32[]{:S(2)}) copy-start(f32[4,4,64,64]{3,2,1,0:T(8,128)} %param.17) | copy-start | bytes 786436
  217.9 12.5 %copy-start.8 = (bf16[256,1024]{1,0:T(8,128)(2,1)S(1)}, bf16[256,1024]{1,0:T(8,128)(2,1)}, u32[]{:S(2)}) copy-start(bf16[256,1024]{1,0:T(8,128)(2,1)} %get-tuple-element.41) | copy-start | bytes 1572868

commit v4 on v3

--- a/solution.py
+++ b/solution.py
@@ -20,50 +20,6 @@
 BF = jnp.bfloat16
 MESH = pl.DeviceIdType.MESH
 NT = (((1,), (1,)), ((), ()))
-
-
-def matmul(former, latter):
-    return jnp.dot(former, latter, preferred_element_type=jnp.float32)
-
-
-def contract(former, latter, former_dim, latter_dim):
-    return lax.dot_general(
-        former,
-        latter,
-        (((former_dim,), (latter_dim,)), ((), ())),
-        preferred_element_type=jnp.float32,
-    )
-
-
-def gelu_exact(values):
-    return jax.nn.gelu(values, approximate=False)
-
-
-def normalize_parts(values, axis):
-    row_mean = jnp.mean(values, axis=axis, keepdims=True)
-    centered = values - row_mean
-    variance = jnp.mean(centered * centered, axis=axis, keepdims=True)
-    inverse = lax.rsqrt(variance + EPSILON)
-    return (centered * inverse, inverse)
-
-
-def normalize_back(grad_hat, normal_hat, inverse, axis):
-    first_mean = jnp.mean(grad_hat, axis=axis, keepdims=True)
-    second_mean = jnp.mean(grad_hat * normal_hat, axis=axis, keepdims=True)
-    return inverse * (grad_hat - first_mean - normal_hat * second_mean)
-
-
-def assemble(blocks, model_width, row_block, col_block):
-    shaped = blocks.reshape(
-        model_width // row_block, model_width // col_block, row_block, col_block
-    )
-    return shaped.transpose(0, 2, 1, 3).reshape(model_width, model_width)
-
-
-def split_blocks(matrix, row_block, col_block):
-    rows, cols = matrix.shape
-    shaped = matrix.reshape(rows // row_block, row_block, cols // col_block, col_block)
-    return shaped.transpose(0, 2, 1, 3).reshape(-1, row_block, col_block)
 
 
 def moment_step(weight, grad, second, rate):
@@ -204,8 +160,7 @@
     dims,
     pixels,
     mask,
-    gain_cols,
-    lat_gain,
+    gain_rows,
     own_proj,
     own_keyval,
     own_latents,
@@ -220,6 +175,8 @@
     landed,
     pixel_query,
     query_out,
+    raw,
+    gain_cols,
     mats_own,
     g_query,
     g_keyval,
@@ -233,7 +190,7 @@
     recv_sems,
     local_sems,
 ):
-    batches, channels, shard_pixels = pixels.shape
+    channels, batches, shard_pixels = pixels.shape
     lat_rows, width = own_latents.shape
     owned, _, row_block, col_block = own_proj.shape
     col_blocks = width // col_block
@@ -245,12 +202,7 @@
     half_rows = row_block // 2
     half_width = width // 2
     every = slice(None)
-
-    g_query[z, y, x, c] = own_proj[:, 0].astype(BF)
-    g_keyval[z, y, x, c] = own_keyval[...]
-    g_latents[y, x, c] = own_latents[...]
-    for mat in range(3):
-        mats_own[mat] = own_proj[:, mat + 1].astype(BF)
+    quarter = shard_pixels // 4
     local = []
 
     def local_copy(source, target):
@@ -259,6 +211,18 @@
         local.append(copy)
         return copy
 
+    g_query[z, y, x, c] = own_proj[:, 0].astype(BF)
+    pixel_copies = [
+        local_copy(pixels.at[:, :, pl.ds(part, quarter)], raw.at[:, :, pl.ds(part, quarter)])
+        for part in range(0, shard_pixels, quarter)
+    ]
+    keyval_rows, lanes = g_keyval.shape[4:]
+    g_keyval[z, y, x, c] = jnp.zeros((keyval_rows, lanes), BF)
+    g_keyval[z, y, x, c, :, 0:channels] = own_keyval[...].astype(BF)
+    gain_cols[...] = jnp.broadcast_to(gain_rows[1:2, 0:lanes], (128, lanes)).T
+    g_latents[y, x, c] = own_latents[...].astype(BF)
+    for mat in range(3):
+        mats_own[mat] = own_proj[:, mat + 1].astype(BF)
     own_mats_copy = local_copy(mats_own, all_mats.at[z, y, x, c])
     place.barrier()
 
@@ -289,44 +253,40 @@
 
     lane_chunk = 128
     bias_row = channels - main
-
-    def norm_image(image):
-        @pl.loop(0, shard_pixels // lane_chunk)
+    row = lax.broadcasted_iota(jnp.int32, (padded - main, lane_chunk), 0)
+
+    def norm_quarter(part):
+        pixel_copies[part].wait()
+
+        @pl.loop(0, quarter // lane_chunk)
         def _(chunk):
-            cols = pl.ds(pl.multiple_of(chunk * lane_chunk, lane_chunk), lane_chunk)
-            top = pixels[image, 0:main, cols].astype(jnp.float32)
-            tail = pixels[image, main:channels, cols].astype(jnp.float32)
-            mean = (
-                jnp.sum(top, axis=0, keepdims=True) + jnp.sum(tail, axis=0, keepdims=True)
-            ) / channels
-            top = top - mean
-            tail = tail - mean
-            variance = (
-                jnp.sum(top * top, axis=0, keepdims=True)
-                + jnp.sum(tail * tail, axis=0, keepdims=True)
-            ) / channels
-            inverse = lax.rsqrt(variance + EPSILON)
-            inverse_out[image : image + 1, cols] = inverse
-            normed[image, 0:main, cols] = (top * inverse * gain_cols[0:main, :]).astype(BF)
-            tail = tail * inverse * gain_cols[main:channels, :]
-            bias = jnp.where(mask[image : image + 1, cols] == 1, 0.0, NEGATIVE)
-            row = lax.broadcasted_iota(jnp.int32, (padded - main, lane_chunk), 0)
-            rest = jnp.where(row == bias_row + 1, 1.0, 0.0)
-            rest = jnp.where(row == bias_row, bias, rest)
-            for index in range(channels - main):
-                rest = jnp.where(row == index, tail[index : index + 1], rest)
-            normed[image, main:padded, cols] = rest.astype(BF)
-
-        local_copy(normed.at[image], normed_out.at[image])
-
-    norm_image(0)
+            start = part * quarter + chunk * lane_chunk
+            cols = pl.ds(pl.multiple_of(start, lane_chunk), lane_chunk)
+            together = raw[:, :, cols].astype(jnp.float32)
+            for image in range(batches):
+                value = together[:, image, :]
+                value = value - jnp.sum(value, axis=0, keepdims=True) / channels
+                variance = jnp.sum(value * value, axis=0, keepdims=True) / channels
+                inverse = lax.rsqrt(variance + EPSILON)
+                inverse_out[image : image + 1, cols] = inverse
+                value = value * inverse * gain_cols[0:channels, :]
+                normed[image, 0:main, cols] = value[0:main].astype(BF)
+                tail = value[main:channels]
+                bias = jnp.where(mask[image : image + 1, cols] == 1, 0.0, NEGATIVE)
+                rest = jnp.where(row == bias_row + 1, 1.0, 0.0)
+                rest = jnp.where(row == bias_row, bias, rest)
+                for index in range(channels - main):
+                    rest = jnp.where(row == index, tail[index : index + 1], rest)
+                normed[image, main:padded, cols] = rest.astype(BF)
+
+    norm_quarter(0)
     for step in range(1, place.nz):
         z_query[step - 1].wait_recv()
         z_keyval[step - 1].wait_recv()
         firsts.append(first_of(step))
     own_mats_copy.wait()
     z_mats = place.push_z(links, all_mats)
-    norm_image(1)
+    norm_quarter(1)
     seconds = []
     for step in range(place.nz):
         arrived(firsts[step])
@@ -334,12 +294,13 @@
     arrived(lat_first)
     seconds += place.push_second(links, g_latents, (), lat_a, "x")
     seconds += place.push_second(links, g_latents, (), lat_b, "y")
-    norm_image(2)
+    norm_quarter(2)
     arrived(seconds)
     cores = place.push_core(links, g_query, (every,))
     cores += place.push_core(links, g_keyval, (every,))
     cores += place.push_core(links, g_latents, ())
-    norm_image(3)
+    norm_quarter(3)
+    local_copy(normed, normed_out)
 
     out_sub = 0
     mats_a = [((0, every, pl.ds(0, half_rows)), "x"), ((1,), "x")]
@@ -359,11 +320,11 @@
                 mean = jnp.mean(values, axis=1, keepdims=True)
                 values = values - mean
                 variance = jnp.mean(values * values, axis=1, keepdims=True)
-                values = values * lax.rsqrt(variance + EPSILON) * lat_gain[...]
+                values = values * lax.rsqrt(variance + EPSILON) * gain_rows[0:1, :]
                 lat_normed[rows, :] = values.astype(BF)
     local_copy(g_query, all_query)
     local_copy(g_keyval, all_keyval)
-    local_copy(g_latents, all_latents)
+    local_copy(lat_normed, all_latents)
     for pair in range(col_blocks // 2):
         query[:, 2 * col_block * pair : 2 * col_block * (pair + 1)] = jnp.dot(
             lat_normed[...],
@@ -421,7 +382,7 @@
     arrived(sent)
     arrived(core_m)
     links.drain()
-    for copy in local[1:]:
+    for copy in local[5:]:
         copy.wait()
 
 
@@ -438,21 +399,16 @@
     return count
 
 
-def front(dims, pixels, pixel_mask, in_gain, lat_gain, proj_blocks, keyval_weight, latents):
+def front(dims, pixels, pixel_mask, gain_rows, proj_blocks, keyval_t, latents):
     nz, ny, nx = dims
-    batches, channels, shard_pixels = pixels.shape
+    channels, batches, shard_pixels = pixels.shape
     lat_rows, width = latents.shape
     owned, mats, row_block, col_block = proj_blocks.shape
-    keyval_rows = keyval_weight.shape[1]
+    keyval_rows = keyval_t.shape[0]
     group = 2 * ny * nx
     all_rows = lat_rows * group
     padded = ceil_to(channels + 2, 16)
     lanes = ceil_to(padded, 128)
-    gain_cols = jnp.broadcast_to(
-        jnp.pad(in_gain, (0, ceil_to(channels, 8) - channels))[:, None],
-        (ceil_to(channels, 8), 128),
-    )
-    own_keyval = jnp.pad(keyval_weight.T.astype(BF), ((0, 0), (0, lanes - channels)))
     vmem = pl.BlockSpec(memory_space=pltpu.VMEM)
     anywhere = pl.BlockSpec(memory_space=pl.ANY)
     cube = (nz, ny, nx, 2)
@@ -462,7 +418,7 @@
         out_shape=(
             jax.ShapeDtypeStruct(cube + (owned, row_block, col_block), BF),
             jax.ShapeDtypeStruct(cube + (keyval_rows, lanes), BF),
-            jax.ShapeDtypeStruct(cube[1:] + (lat_rows, width), BF),
+            jax.ShapeDtypeStruct((all_rows, width), BF),
             jax.ShapeDtypeStruct(cube + (3, owned, row_block, col_block), BF),
             jax.ShapeDtypeStruct((batches, padded, shard_pixels), BF),
             jax.ShapeDtypeStruct((batches, shard_pixels), jnp.float32),
@@ -472,7 +428,7 @@
             jax.ShapeDtypeStruct((all_rows, lanes), BF),
             jax.ShapeDtypeStruct((all_rows, width), BF),
         ),
-        in_specs=[vmem] * 7,
+        in_specs=[anywhere] + [vmem] * 5,
         out_specs=(
             anywhere,
             anywhere,
@@ -487,6 +443,8 @@
             anywhere,
         ),
         scratch_shapes=[
+            pltpu.VMEM(pixels.shape, BF),
+            pltpu.VMEM((lanes, 128), jnp.float32),
             pltpu.VMEM((3, owned, row_block, col_block), BF),
             pltpu.VMEM(cube + (owned, row_block, col_block), BF),
             pltpu.VMEM(cube + (keyval_rows, lanes), BF),
@@ -498,7 +456,7 @@
             pltpu.VMEM((batches, all_rows, lanes), BF),
             pltpu.SemaphoreType.DMA((copies,)),
             pltpu.SemaphoreType.DMA((copies,)),
-            pltpu.SemaphoreType.DMA((5 + 4 * batches,)),
+            pltpu.SemaphoreType.DMA((10 + 3 * batches,)),
         ],
         compiler_params=pltpu.CompilerParams(
             collective_id=0, has_side_effects=True, vmem_limit_bytes=56 * 2**20
@@ -506,11 +464,10 @@
     )(
         pixels,
         pixel_mask,
-        gain_cols,
-        lat_gain[None, :],
+        gain_rows,
         proj_blocks,
-        own_keyval,
-        latents.astype(BF),
+        keyval_t,
+        latents,
     )
 
 
@@ -655,10 +612,8 @@
     sent_all,
     pixel_query,
     latents,
-    mlp_gain,
+    gain_rows,
     grad_rows,
-    gain_cols,
-    gain_back,
     mixed,
     pixel_grad,
     mats_grad,
@@ -688,6 +643,7 @@
     query_turned,
     query_acc,
     gain_acc,
+    gain_cols,
     staged,
     terms,
     buffers,
@@ -787,7 +743,7 @@
         value = value * scale
         mid_hat[part, :] = value
         mid_inverse[part, :] = jnp.broadcast_to(scale, (lat_rows, 128))
-        mid_normed[part, :] = (value * mlp_gain[...]).astype(BF)
+        mid_normed[part, :] = (value * gain_rows[2:3, :]).astype(BF)
 
     arrived_local(mats_copies[1])
     for index in range(tiles):
@@ -854,7 +810,7 @@
     @pl.loop(0, rows // lat_rows)
     def _(step):
         part = pl.ds(pl.multiple_of(step * lat_rows, lat_rows), lat_rows)
-        grad = grad_mid_normed[part, :] * mlp_gain[...]
+        grad = grad_mid_normed[part, :] * gain_rows[2:3, :]
         hat = mid_hat[part, :]
         grad = (
             grad
@@ -921,6 +877,8 @@
     ).T[0:padded].astype(BF)
     query_acc[...] = jnp.zeros(query_acc.shape, jnp.float32)
     gain_acc[...] = jnp.zeros(gain_acc.shape, jnp.float32)
+    gain_cols[0] = jnp.broadcast_to(gain_rows[1:2, 0:lanes], (128, lanes)).T[0:padded]
+    gain_cols[1] = jnp.broadcast_to(gain_rows[3:4, 0:lanes], (128, lanes)).T[0:padded]
     chunk = min(512, shard_pixels)
     staged_out = []
     tops_copy.wait()
@@ -957,14 +915,14 @@
             folded = sum(product[:, at : at + 128] for at in range(0, chunk, 128))
             gain_acc[0:padded, :] += folded
             second_mean = jnp.sum(product, axis=0, keepdims=True) / channels
-            spread = jnp.concatenate([gain_cols[...]] * (chunk // 128), axis=1)
-            spread_back = jnp.concatenate([gain_back[...]] * (chunk // 128), axis=1)
+            spread = jnp.concatenate([gain_cols[0]] * (chunk // 128), axis=1)
+            spread_back = jnp.concatenate([gain_cols[1]] * (chunk // 128), axis=1)
             grad_hat = grad_normed * spread
             first_mean = jnp.sum(grad_hat, axis=0, keepdims=True) / channels
             result = (grad_hat - first_mean - normal * spread_back * second_mean) * inverse[
                 image : image + 1, cols
             ]
-            staged[slot, :, cols] = result[0:channels]
+            staged[slot, :, cols] = result[0:channels].astype(BF)
 
         staged_out.append(local_copy(staged.at[slot], pixel_grad.at[image]))
         if image + 2 < batches:
@@ -1078,7 +1036,7 @@
     return count
 
 
-def back(dims, channels, gathered, latents, mlp_gain, in_gain, mixed_grad):
+def back(dims, channels, gathered, latents, gain_rows, mixed_grad):
     landed, all_keyval, all_mats, normed_all, inverse, weights_all, sent_all, pixel_query = gathered
     nz, ny, nx = dims
     group, batches, lat_rows, lanes = landed.shape
@@ -1089,10 +1047,6 @@
     owned, row_block, col_block = all_mats.shape[5:]
     keyval_rows = all_keyval.shape[4]
     half_rows = row_block // 2
-    column = jnp.pad(in_gain, (0, padded - channels))[:, None]
-    column_back = jnp.pad(1.0 / in_gain, (0, padded - channels))[:, None]
-    gain_cols = jnp.broadcast_to(column, (padded, 128))
-    gain_back = jnp.broadcast_to(column_back, (padded, 128))
     vmem = pl.BlockSpec(memory_space=pltpu.VMEM)
     anywhere = pl.BlockSpec(memory_space=pl.ANY)
     lead = (nz, ny, nx) if 2 * owned * col_block == width else (nz, ny)
@@ -1122,7 +1076,7 @@
         functools.partial(back_kernel, dims, channels),
         out_shape=(
             jax.ShapeDtypeStruct((rows, width), BF),
-            jax.ShapeDtypeStruct((batches, channels, shard_pixels), jnp.float32),
+            jax.ShapeDtypeStruct((batches, channels, shard_pixels), BF),
             jax.ShapeDtypeStruct((3, owned, row_block, col_block), jnp.float32),
             jax.ShapeDtypeStruct((keyval_rows, lanes), jnp.float32),
             jax.ShapeDtypeStruct((group, lat_rows, lanes), BF),
@@ -1137,8 +1091,6 @@
             vmem,
             anywhere,
             anywhere,
-            vmem,
-            vmem,
             vmem,
             vmem,
             vmem,
@@ -1168,7 +1120,8 @@
             pltpu.VMEM((padded, all_rows), BF),
             pltpu.VMEM((all_rows, lanes), jnp.float32),
             pltpu.VMEM((lanes, 128), jnp.float32),
-            pltpu.VMEM((2, channels, shard_pixels), jnp.float32),
+            pltpu.VMEM((2, padded, 128), jnp.float32),
+            pltpu.VMEM((2, channels, shard_pixels), BF),
             terms,
             buffers,
             pltpu.VMEM((all_rows, lanes), BF),
@@ -1194,10 +1147,272 @@
         sent_all,
         pixel_query,
         latents,
-        mlp_gain[None, :],
+        gain_rows,
         mixed_grad.reshape(rows, width),
-        gain_cols,
-        gain_back,
+    )
+
+
+TN = (((0,), (0,)), ((), ()))
+
+
+def tail_kernel(
+    dims,
+    channels,
+    query_total,
+    residual_total,
+    mats_grad,
+    value_grad,
+    proj_blocks,
+    proj_left,
+    proj_right,
+    left_roots,
+    right_roots,
+    keyval_weight,
+    keyval_second,
+    latents,
+    latent_second,
+    gain_rows,
+    query_in,
+    lat_normed_in,
+    query_blocks,
+    all_keyval,
+    pixel_low,
+    pixel_grad,
+    proj_grad,
+    left_new,
+    right_new,
+    proj_new,
+    keyval_grad,
+    keyval_second_new,
+    keyval_new,
+    latent_grad,
+    latent_second_new,
+    latent_new,
+    lat_gain_grad,
+    query,
+    lat_normed,
+    query_weight,
+    keys,
+    pixel_came,
+    pixel_wide,
+    grad_query,
+    grad_normed,
+    query_grad,
+    key_rows,
+    local_sems,
+):
+    place = Place(*dims)
+    group, lat_rows, lanes = query_total.shape
+    all_rows = group * lat_rows
+    width = latents.shape[1]
+    batches = pixel_low.shape[0]
+    owned, mats, row_block, col_block = proj_blocks.shape
+    col_blocks = width // col_block
+    keyval_rows = keyval_weight.shape[0]
+    device = place.z * group + place.p
+    every = slice(None)
+    local = []
+
+    def local_copy(source, target):
+        copy = pltpu.make_async_copy(source, target, local_sems.at[len(local)])
+        copy.start()
+        local.append(copy)
+        return copy
+
+    keys_copy = local_copy(all_keyval.at[pl.ds(0, place.nz // 2)], keys)
+    weight_copies = []
+    for block in range(col_blocks):
+        lead = (every,) * (len(query_weight.shape) - 1)
+        weight_copies.append(
+            local_copy(
+                query_blocks.at[block_index(block, col_blocks, owned)],
+                query_weight.at[lead + (pl.ds(block * col_block, col_block),)],
+            )
+        )
+    normed_copy = local_copy(lat_normed_in, lat_normed)
+    query_copy = local_copy(query_in, query)
+    pixel_copies = [local_copy(pixel_low.at[i], pixel_came.at[i]) for i in range(batches)]
+    pixel_sent = []
+
+    def widen(image):
+        pixel_copies[image].wait()
+
+        @pl.loop(0, pixel_low.shape[2] // 256)
+        def _(step):
+            cols = pl.ds(pl.multiple_of(step * 256, 256), 256)
+            pixel_wide[image, :, cols] = pixel_came[image, :, cols].astype(jnp.float32)
+
+        pixel_sent.append(local_copy(pixel_wide.at[image], pixel_grad.at[:, image]))
+
+    def moments(weight, grad, second, rate, second_out, weight_out):
+        second_value = STAT_DECAY * second[...] + (1.0 - STAT_DECAY) * grad * grad
+        second_out[...] = second_value
+        weight_out[...] = weight[...] - rate * grad / (jnp.sqrt(second_value) + MOMENT_FLOOR)
+
+    def precondition(mat, index, grad):
+        low = grad.astype(BF)
+        proj_grad[index, mat] = grad
+        left_new[index, mat] = STAT_DECAY * proj_left[index, mat] + (
+            1.0 - STAT_DECAY
+        ) * lax.dot_general(low, low, NT, preferred_element_type=jnp.float32)
+        right_new[index, mat] = STAT_DECAY * proj_right[index, mat] + (
+            1.0 - STAT_DECAY
+        ) * lax.dot_general(low, low, TN, preferred_element_type=jnp.float32)
+        step = jnp.dot(
+            left_roots[index, mat].astype(BF), low, preferred_element_type=jnp.float32
+        ).astype(BF)
+        step = jnp.dot(
+            step, right_roots[index, mat].astype(BF), preferred_element_type=jnp.float32
+        )
+        proj_new[index, mat] = proj_blocks[index, mat] - MATRIX_RATE * step
+
+    for mat in range(3):
+        for index in range(owned):
+            precondition(mat + 1, index, mats_grad[mat, index])
+    widen(0)
+    keys_copy.wait()
+    scale = width ** (-0.5)
+    query_sum = query_total[...].reshape(all_rows, lanes)
+    key_t = keys[...].reshape(width, lanes)
+    for start in range(0, width, 256):
+        grad_query[:, start : start + 256] = (
+            lax.dot_general(
+                query_sum, key_t[start : start + 256], NT, preferred_element_type=jnp.float32
+            )
+            * scale
+        ).astype(BF)
+    widen(1)
+    arrived_local(weight_copies)
+    normed_copy.wait()
+    row_tile = width // place.nz
+    for index in range(place.nz):
+        cols = slice(index * row_tile, (index + 1) * row_tile)
+        part = lax.dot_general(
+            grad_query[...],
+            query_weight[index].reshape(row_tile, width),
+            NT,
+            preferred_element_type=jnp.float32,
+        )
+        grad_normed[:, cols] = part
+        lat_gain_grad[:, cols] = (
+            jnp.sum(part * lat_normed[:, cols].astype(jnp.float32), axis=0, keepdims=True)
+            / gain_rows[0:1, cols]
+        )
+    widen(2)
+    values = latents[...]
+    centered = values - jnp.mean(values, axis=1, keepdims=True)
+    inverse = lax.rsqrt(jnp.mean(centered * centered, axis=1, keepdims=True) + EPSILON)
+    hat = centered * inverse
+    own = pl.ds(pl.multiple_of(place.p * lat_rows, lat_rows), lat_rows)
+    grad = grad_normed[own, :] * gain_rows[0:1, :]
+    grad = (
+        grad
+        - jnp.mean(grad, axis=1, keepdims=True)
+        - hat * jnp.mean(grad * hat, axis=1, keepdims=True)
+    ) * inverse
+    grad = residual_total[...] + grad
+    latent_grad[...] = grad
+    moments(latents, grad, latent_second, LATENT_RATE, latent_second_new, latent_new)
+
+    block_row = device * owned // col_blocks
+    block_col = lax.rem(device * owned, col_blocks)
+    per_lane = 128 // row_block
+    rows = pl.ds(pl.multiple_of(block_row // per_lane * 128, 128), 128)
+    cols = pl.ds(pl.multiple_of(block_col * col_block, col_block), owned * col_block)
+    query_grad[...] = lax.dot_general(
+        lat_normed[:, rows], grad_query[:, cols], TN, preferred_element_type=jnp.float32
+    )
+    part = pl.ds(pl.multiple_of(lax.rem(block_row, per_lane) * row_block, row_block), row_block)
+    for index in range(owned):
+        precondition(0, index, query_grad[part, index * col_block : (index + 1) * col_block])
+    widen(3)
+
+    query_copy.wait()
+    half_devices = width // keyval_rows
+    start = lax.rem(device, half_devices) * keyval_rows
+    cols = pl.ds(pl.multiple_of(start // 128 * 128, 128), 128)
+    key_rows[...] = (
+        lax.dot_general(query[:, cols], query_sum, TN, preferred_element_type=jnp.float32) * scale
+    )
+    part = pl.ds(pl.multiple_of(lax.rem(start, 128), keyval_rows), keyval_rows)
+    grad = jnp.where(device < half_devices, key_rows[part, :], value_grad[...])[:, 0:channels]
+    keyval_grad[...] = grad
+    moments(keyval_weight, grad, keyval_second, KEYVAL_RATE, keyval_second_new, keyval_new)
+    for copy in pixel_sent:
+        copy.wait()
+
+
+def tail(
+    dims,
+    query_total,
+    residual_total,
+    mats_grad,
+    value_grad,
+    owned_arrays,
+    gain_rows,
+    query,
+    lat_normed,
+    query_blocks,
+    all_keyval,
+    pixel_low,
+):
+    nz, ny, nx = dims
+    proj_blocks, keyval_weight, latents = owned_arrays[0], owned_arrays[5], owned_arrays[7]
+    group, lat_rows, lanes = query_total.shape
+    all_rows = group * lat_rows
+    width = latents.shape[1]
+    batches, channels, shard_pixels = pixel_low.shape
+    owned, mats, row_block, col_block = proj_blocks.shape
+    lead = (nz, ny, nx) if 2 * owned * col_block == width else (nz, ny)
+    vmem = pl.BlockSpec(memory_space=pltpu.VMEM)
+    anywhere = pl.BlockSpec(memory_space=pl.ANY)
+    like = lambda array: jax.ShapeDtypeStruct(array.shape, array.dtype)
+    wide = jax.ShapeDtypeStruct((channels, batches, shard_pixels), jnp.float32)
+    results = [
+        wide,
+        like(proj_blocks),
+        like(owned_arrays[1]),
+        like(owned_arrays[2]),
+        like(proj_blocks),
+        like(keyval_weight),
+        like(keyval_weight),
+        like(keyval_weight),
+        like(latents),
+        like(latents),
+        like(latents),
+        jax.ShapeDtypeStruct((1, width), jnp.float32),
+    ]
+    return pl.pallas_call(
+        functools.partial(tail_kernel, dims, channels),
+        out_shape=results,
+        in_specs=[vmem] * 14 + [anywhere] * 5,
+        out_specs=[anywhere] + [vmem] * 11,
+        scratch_shapes=[
+            pltpu.VMEM((all_rows, width), BF),
+            pltpu.VMEM((all_rows, width), BF),
+            pltpu.VMEM(lead + (row_block, width), BF),
+            pltpu.VMEM((nz // 2, ny, nx, 2) + all_keyval.shape[4:], BF),
+            pltpu.VMEM((batches, channels, shard_pixels), BF),
+            pltpu.VMEM((batches, channels, shard_pixels), jnp.float32),
+            pltpu.VMEM((all_rows, width), BF),
+            pltpu.VMEM((all_rows, width), jnp.float32),
+            pltpu.VMEM((128, owned * col_block), jnp.float32),
+            pltpu.VMEM((128, lanes), jnp.float32),
+            pltpu.SemaphoreType.DMA((3 + width // col_block + 2 * batches,)),
+        ],
+        compiler_params=pltpu.CompilerParams(vmem_limit_bytes=56 * 2**20),
+    )(
+        query_total,
+        residual_total,
+        mats_grad,
+        value_grad,
+        *owned_arrays,
+        gain_rows,
+        query,
+        lat_normed,
+        query_blocks,
+        all_keyval,
+        pixel_low,
     )
 
 
@@ -1220,20 +1435,20 @@
     batches, channels, shard_pixels = pixels.shape
     lat_rows, width = latents.shape
     groups = lax.axis_size("pix")
-    all_rows = lat_rows * groups
-    owned_count, _, row_block, col_block = proj_blocks.shape
     scale = width ** (-0.5)
-    everyone = ("samp", "pix")
 
     lat_gain = gains[:width]
     in_gain = gains[width : width + channels]
     mlp_gain = gains[width + channels :]
     side = math.isqrt(groups // 2)
     dims = (lax.axis_size("samp"), side, side)
+    widen = lambda row: jnp.pad(row, (0, width - row.shape[0]))
+    gain_rows = jnp.stack([lat_gain, widen(in_gain), mlp_gain, widen(1.0 / in_gain)])
+    keyval_own = keyval_weight.T
     (
         query_blocks,
         keyval_t,
-        latent_all,
+        lat_normed,
         mats,
         normed_all,
         inverse_all,
@@ -1242,7 +1457,9 @@
         landed,
         pixel_query,
         query,
-    ) = front(dims, pixels, pixel_mask, in_gain, lat_gain, proj_blocks, keyval_weight, latents)
+    ) = front(
+        dims, pixels.swapaxes(0, 1), pixel_mask, gain_rows, proj_blocks, keyval_own, latents
+    )
     gathered = (
         landed,
         keyval_t,
@@ -1253,62 +1470,10 @@
         sent_all,
         pixel_query,
     )
-    mixed, pixel_grad, triple_owned, value_grad, query_total, gain_total, residual_total = back(
-        dims, channels, gathered, latents, mlp_gain, in_gain, mixed_grad
+    mixed, pixel_low, mats_grad, value_grad, query_total, gain_total, residual_total = back(
+        dims, channels, gathered, latents, gain_rows, mixed_grad
     )
-    query_sum = query_total.reshape(all_rows, -1)[:, :channels]
-    gain_rows = gain_total.reshape(-1)
-    mlp_gain_sum = gain_rows[:width]
-    in_gain_sum = gain_rows[width : width + channels] / in_gain
-    latent_all = latent_all.reshape(all_rows, width).astype(jnp.float32)
-    key_t = keyval_t.reshape(2 * width, -1)[:width, :channels]
-    query_weight = assemble(query_blocks, width, row_block, col_block)
-    lat_hat, lat_inverse = normalize_parts(latent_all, 1)
-    lat_normed = (lat_hat * lat_gain[None, :]).astype(BF)
-
-    key_rows = keyval_weight.shape[1]
-    device = lax.axis_index(everyone)
-    half_devices = width // key_rows
-    own_query = lax.dynamic_slice_in_dim(query, device % half_devices * key_rows, key_rows, 1)
-    key_grad = contract(query_sum, own_query, 0, 0) * scale
-    keyval_grad = jnp.where(device < half_devices, key_grad, value_grad[:, :channels].T)
-
-    grad_query = (contract(query_sum, key_t, 1, 1) * scale).astype(BF)
-    grad_lat_normed = contract(grad_query, query_weight, 1, 1)
-    lat_gain_grad = jnp.sum(grad_lat_normed * lat_hat, axis=0)
-    latent_path = normalize_back(grad_lat_normed * lat_gain[None, :], lat_hat, lat_inverse, 1)
-    row_start = lax.axis_index("pix") * lat_rows
-    own_path = lax.dynamic_slice_in_dim(latent_path, row_start, lat_rows, 0)
-    latent_grad = residual_total + own_path
-    first_block = device * owned_count
-    col_count = width // col_block
-    query_list = []
-    for offset in range(owned_count):
-        block_index = first_block + offset
-        block_row = block_index // col_count * row_block
-        block_col = block_index % col_count * col_block
-        normed_slice = lax.dynamic_slice_in_dim(lat_normed, block_row, row_block, 1)
-        grad_slice = lax.dynamic_slice_in_dim(grad_query, block_col, col_block, 1)
-        query_list.append(contract(normed_slice, grad_slice, 0, 0))
-    query_grad = jnp.stack(query_list, axis=0)
-    proj_grad = jnp.concatenate([query_grad[:, None], triple_owned.swapaxes(0, 1)], axis=1)
-    left_new = STAT_DECAY * proj_left + (1.0 - STAT_DECAY) * jnp.einsum(
-        "nsab,nscb->nsac", proj_grad, proj_grad, precision=HIGHEST
-    )
-    right_new = STAT_DECAY * proj_right + (1.0 - STAT_DECAY) * jnp.einsum(
-        "nsab,nsac->nsbc", proj_grad, proj_grad, precision=HIGHEST
-    )
-    partial_step = jnp.einsum("nsab,nsbc->nsac", left_roots, proj_grad, precision=HIGHEST)
-    direction = jnp.einsum("nsac,nscd->nsad", partial_step, right_roots, precision=HIGHEST)
-    proj_new = proj_blocks - MATRIX_RATE * direction
-    keyval_second_new, keyval_new = moment_step(
-        keyval_weight, keyval_grad, keyval_second, KEYVAL_RATE
-    )
-    latent_second_new, latent_new = moment_step(latents, latent_grad, latent_second, LATENT_RATE)
-    gain_grad = jnp.concatenate([lat_gain_grad, in_gain_sum, mlp_gain_sum], axis=0)
-    gain_second_new, gain_new = moment_step(gains, gain_grad, gain_second, GAIN_RATE)
-    return (
-        mixed.reshape(batches, lat_rows, width),
+    (
         pixel_grad,
         proj_grad,
         left_new,
@@ -1317,6 +1482,54 @@
         keyval_grad,
         keyval_second_new,
         keyval_new,
+        latent_grad,
+        latent_second_new,
+        latent_new,
+        lat_gain_grad,
+    ) = tail(
+        dims,
+        query_total,
+        residual_total,
+        mats_grad,
+        value_grad,
+        (
+            proj_blocks,
+            proj_left,
+            proj_right,
+            left_roots,
+            right_roots,
+            keyval_own,
+            keyval_second.T,
+            latents,
+            latent_second,
+        ),
+        gain_rows,
+        query,
+        lat_normed,
+        query_blocks,
+        keyval_t,
+        pixel_low,
+    )
+    gain_sums = gain_total.reshape(-1)
+    gain_grad = jnp.concatenate(
+        [
+            lat_gain_grad[0],
+            gain_sums[width : width + channels] / in_gain,
+            gain_sums[:width],
+        ],
+        axis=0,
+    )
+    gain_second_new, gain_new = moment_step(gains, gain_grad, gain_second, GAIN_RATE)
+    return (
+        mixed.reshape(batches, lat_rows, width),
+        pixel_grad.swapaxes(0, 1),
+        proj_grad,
+        left_new,
+        right_new,
+        proj_new,
+        keyval_grad.T,
+        keyval_second_new.T,
+        keyval_new.T,
         latent_grad,
         latent_second_new,
         latent_new,

time: 235 us -> 192 us (0.82); the launches traced: 231 us -> 191 us
  local copies, waits for them, and re-layouts: 28.3 us -> 3.06 us
  matrix products: 23.1 us -> 0 us
  Pallas kernels: 173 us -> 185 us
  other arithmetic: 5.79 us -> 2.63 us
    dot_general x11 -> x0, matrix products: 23.1 us -> none  [the longest x7 15.9 us: contract(): lax.dot_general(former, latter, (((former_dim,), (latter_dim,)), ((), ())...]
    unnamed x50 -> x9, local copies, waits for them, and re-layouts: 20.1 us -> 0.81 us
    pallas_call x0 -> x1, Pallas kernels: none -> 12.2 us  [tail(): pl.pallas_call(functools.partial(tail_kernel, dims, channels), out_shape=...]
    reshape x1 -> x0, local copies, waits for them, and re-layouts: 3.46 us -> none  [assemble(): blocks.reshape(model_width // row_block, model_width // col_block, row_bl...]
where the time goes in v4:
time: 192 us; the launch traced here: 191 us
  Pallas kernels  185 us (96%)
  local copies, waits for them, and re-layouts  3.06 us (2%)
  other arithmetic  2.63 us (1%)
    pallas_call x1, Pallas kernels, back(): pl.pallas_call(functools.partial(back_kernel, dims, channels), out_shape=...  88.8 us
    pallas_call x1, Pallas kernels, front(): pl.pallas_call(functools.partial(front_kernel, dims), out_shape=(jax.Shap...  83.6 us
    pallas_call x1, Pallas kernels, tail(): pl.pallas_call(functools.partial(tail_kernel, dims, channels), out_shape=...  12.2 us

profile of v4, /device:TPU:0, one launch (start us, length us, event | category | flops | bytes accessed | tf_op | source)
XLA Modules:
  0.0 191.0 jit_solution(3213460604838682484)
XLA Ops:
  0.6 0.7 fusion.3
  1.3 0.8 fusion.2
  2.1 0.6 pad_maximum_fusion.gain_rows
  2.8 83.6 %shard_map.253 = (bf16[4,2,2,2,4,64,128]{6,5,4,3,2,1,0:T(8,128)(2,1)}, bf16[4,2,2,2,64,384]{5,4,3,2,1,0:T(8,128)(2,1)}, bf16[512,1024]{1,0:T(8,128)(2,1)}, bf16[...) custom-call(bf16[261,4,2048]{2,1,0:T(4,128)(2,1)} %bitcast.17, ...), custom_call_target="tpu_custom_call" | custom-call | tf_op jit(solution)/shard_map/pallas_call | solution.py:416
  86.4 0.0 copy-start.1
  86.4 88.8 %shard_map.254 = (bf16[256,1024]{1,0:T(8,128)(2,1)}, bf16[4,261,2048]{2,1,0:T(8,128)(2,1)}, f32[3,4,64,128]{3,2,1,0:T(8,128)}, f32[64,384]{1,0:T(8,128)}, bf16[8...) custom-call(bf16[8,4,64,384]{3,2,1,0:T(8,128)(2,1)} %get-tuple-element.45.landed, ...), custom_call_target="tpu_custom_call" | custom-call | tf_op jit(solution)/shard_map/pallas_call | solution.py:1075
  175.2 0.0 copy-done.1
  175.2 0.7 slice_divide_fusion
  175.9 0.7 slice_bitcast_fusion
  176.6 0.0 copy-start.3
  176.6 0.0 copy-start
  176.6 12.2 %shard_map.255 = (f32[261,4,2048]{2,1,0:T(4,128)}, f32[4,4,64,128]{3,2,1,0:T(8,128)}, f32[4,4,64,64]{3,2,1,0:T(8,128)}, f32[4,4,128,128]{3,2,1,0:T(8,128)}, f32[...) custom-call(bf16[8,64,384]{2,1,0:T(8,128)(2,1)} %get-tuple-element.5, ...), custom_call_target="tpu_custom_call" | custom-call | tf_op jit(solution)/shard_map/pallas_call | solution.py:1385
  188.8 0.8 concatenate.3
  189.6 0.0 copy-done.3
  189.6 0.0 copy-start.2
  189.6 0.6 divide_subtract_fusion
  190.2 0.0 copy-done
  190.2 0.8 copy.30
  191.0 0.0 copy-done.2
  (2 shorter events, 0.0 us)
Async XLA Ops:
  86.4 88.8 %copy-start.1 = (f32[2309]{0:T(1024)S(1)}, f32[2309]{0:T(1024)}, u32[]{:S(2)}) copy-start(f32[2309]{0:T(1024)} %param.25) | copy-start | bytes 27712
  176.6 13.0 %copy-start.3 = (f32[2309]{0:T(1024)S(1)}, f32[2309]{0:T(1024)}, u32[]{:S(2)}) copy-start(f32[2309]{0:T(1024)} %param.26) | copy-start | bytes 27712
  176.6 13.6 %copy-start = (bf16[256,1024]{1,0:T(8,128)(2,1)S(1)}, bf16[256,1024]{1,0:T(8,128)(2,1)}, u32[]{:S(2)}) copy-start(bf16[256,1024]{1,0:T(8,128)(2,1)} %get-tuple-element.53) | copy-start | bytes 1572868
  189.6 1.4 copy-start.2

commit v5 on v4

--- a/solution.py
+++ b/solution.py
@@ -93,12 +93,9 @@
             )
         pl.semaphore_wait(semaphore, self.nz - 1 + self.group - 1)
 
-    def push_z(self, links, array, sub=()):
-        copies = []
-        for step in range(1, self.nz):
-            own = array.at[(self.z, self.y, self.x, self.c) + sub]
-            copies.append(links.push(own, own, lax.rem(self.z - step + self.nz, self.nz), self.p))
-        return copies
+    def push_z(self, links, array, step):
+        own = array.at[self.z, self.y, self.x, self.c]
+        return [links.push(own, own, lax.rem(self.z - step + self.nz, self.nz), self.p)]
 
     def push_first(self, links, array, lead, sub, along):
         own = array.at[lead + (self.y, self.x, self.c) + sub]
@@ -186,6 +183,8 @@
     normed,
     weights,
     outgoing,
+    paired,
+    merged,
     send_sems,
     recv_sems,
     local_sems,
@@ -202,7 +201,7 @@
     half_rows = row_block // 2
     half_width = width // 2
     every = slice(None)
-    quarter = shard_pixels // 4
+    quarter = shard_pixels // 8
     local = []
 
     def local_copy(source, target):
@@ -228,28 +227,41 @@
 
     sub_a = (every, pl.ds(0, half_rows))
     sub_b = (every, pl.ds(half_rows, half_rows))
-
-    def first_of(step):
-        zz = lax.rem(z + step, place.nz)
-        copies = place.push_first(links, g_query, (zz,), sub_a, "x")
-        copies += place.push_first(links, g_query, (zz,), sub_b, "y")
-        copies += place.push_first(links, g_keyval, (zz,), (), "xy"[step % 2])
+    mats_subs = [
+        ((1,), "x"),
+        ((2,), "y"),
+        ((0, every, pl.ds(0, half_rows)), "x"),
+        ((0, every, pl.ds(half_rows, half_rows)), "y"),
+    ]
+
+    def level(step):
+        return lax.rem(z + step, place.nz)
+
+    def hand_on(push, step):
+        copies = push(links, g_query, (level(step),), sub_a, "x")
+        copies += push(links, g_query, (level(step),), sub_b, "y")
+        copies += push(links, g_keyval, (level(step),), (), "xy"[step % 2])
         return copies
 
-    def second_of(step):
-        zz = lax.rem(z + step, place.nz)
-        copies = place.push_second(links, g_query, (zz,), sub_a, "x")
-        copies += place.push_second(links, g_query, (zz,), sub_b, "y")
-        copies += place.push_second(links, g_keyval, (zz,), (), "xy"[step % 2])
+    def hand_on_mats(push, step):
+        copies = []
+        for sub, along in mats_subs:
+            copies += push(links, all_mats, (level(step),), sub, along)
         return copies
 
-    z_query = place.push_z(links, g_query)
-    z_keyval = place.push_z(links, g_keyval)
-    firsts = [first_of(0)]
+    z_group = []
+    for step in range(1, place.nz):
+        z_group.append(
+            place.push_z(links, g_query, step) + place.push_z(links, g_keyval, step)
+        )
+    firsts = [hand_on(place.push_first, 0)]
     lat_a = (every, pl.ds(0, half_width))
     lat_b = (every, pl.ds(half_width, half_width))
     lat_first = place.push_first(links, g_latents, (), lat_a, "x")
     lat_first += place.push_first(links, g_latents, (), lat_b, "y")
+    own_mats_copy.wait()
+    z_mats = [place.push_z(links, all_mats, step) for step in range(1, place.nz)]
+    firsts_m = [hand_on_mats(place.push_first, 0)]
 
     lane_chunk = 128
     bias_row = channels - main
@@ -279,37 +291,59 @@
                     rest = jnp.where(row == index, tail[index : index + 1], rest)
                 normed[image, main:padded, cols] = rest.astype(BF)
 
+    seconds = []
+    seconds_m = []
+    cores_m = []
+
+    def first(step):
+        arrived(z_group[step - 1])
+        firsts.append(hand_on(place.push_first, step))
+
+    def second(step):
+        arrived(firsts[step])
+        seconds.extend(hand_on(place.push_second, step))
+
+    def first_m(step):
+        arrived(z_mats[step - 1])
+        firsts_m.append(hand_on_mats(place.push_first, step))
+
+    def second_m(step):
+        arrived(firsts_m[step])
+        seconds_m.append(hand_on_mats(place.push_second, step))
+
+    def core_m(step):
+        arrived(seconds_m[step])
+        cores_m.extend(place.push_core(links, all_mats, (level(step),)))
+
     norm_quarter(0)
-    for step in range(1, place.nz):
-        z_query[step - 1].wait_recv()
-        z_keyval[step - 1].wait_recv()
-        firsts.append(first_of(step))
-    own_mats_copy.wait()
-    z_mats = place.push_z(links, all_mats)
     norm_quarter(1)
-    seconds = []
-    for step in range(place.nz):
-        arrived(firsts[step])
-        seconds += second_of(step)
+    second(0)
     arrived(lat_first)
     seconds += place.push_second(links, g_latents, (), lat_a, "x")
     seconds += place.push_second(links, g_latents, (), lat_b, "y")
     norm_quarter(2)
+    first(1)
+    norm_quarter(3)
+    norm_quarter(4)
+    first(2)
+    second(1)
+    norm_quarter(5)
+    for step in range(3, place.nz):
+        first(step)
+    second(2)
+    norm_quarter(6)
+    for step in range(3, place.nz):
+        second(step)
+    norm_quarter(7)
+    second_m(0)
+    first_m(1)
+    local_copy(normed, normed_out)
     arrived(seconds)
     cores = place.push_core(links, g_query, (every,))
     cores += place.push_core(links, g_keyval, (every,))
     cores += place.push_core(links, g_latents, ())
-    norm_quarter(3)
-    local_copy(normed, normed_out)
-
-    out_sub = 0
-    mats_a = [((0, every, pl.ds(0, half_rows)), "x"), ((1,), "x")]
-    mats_b = [((0, every, pl.ds(half_rows, half_rows)), "y"), ((2,), "y")]
-
-    arrived(z_mats)
-    firsts_m = []
-    for sub, along in mats_a + mats_b:
-        firsts_m += place.push_first(links, all_mats, (every,), sub, along)
+    second_m(1)
+    first_m(2)
 
     arrived(cores)
     for yy in range(place.ny):
@@ -322,6 +356,7 @@
                 variance = jnp.mean(values * values, axis=1, keepdims=True)
                 values = values * lax.rsqrt(variance + EPSILON) * gain_rows[0:1, :]
                 lat_normed[rows, :] = values.astype(BF)
+    second_m(2)
     local_copy(g_query, all_query)
     local_copy(g_keyval, all_keyval)
     local_copy(lat_normed, all_latents)
@@ -338,11 +373,11 @@
     lane = lax.broadcasted_iota(jnp.int32, projected.shape, 1)
     pixel_query[...] = jnp.where(lane == channels, 1.0, projected).astype(BF)
 
-    all_rows = lat_rows * place.group
-    tile = min(256, all_rows)
+    tile = place.nx * 2 * lat_rows
+    rows_here = place.ny * place.nx * lat_rows
 
     def attend(image):
-        @pl.loop(0, all_rows // tile)
+        @pl.loop(0, place.ny)
         def _(step):
             rows = pl.ds(pl.multiple_of(step * tile, tile), tile)
             scores = jnp.dot(
@@ -356,47 +391,78 @@
                 share, normed[image], NT, preferred_element_type=jnp.float32
             )
             lane = lax.broadcasted_iota(jnp.int32, numer.shape, 1)
-            outgoing[image, rows, 0:padded] = jnp.where(lane == channels, top, numer).astype(BF)
+            numer = jnp.where(lane == channels, top, numer).astype(BF)
+            outgoing[image, step, :, :, :, 0:padded] = numer.reshape(
+                place.nx, 2, lat_rows, padded
+            )
 
         local_copy(weights.at[image], weights_out.at[image])
-        local_copy(outgoing.at[image], sent_out.at[image])
-        own_rows = pl.ds(pl.multiple_of(p * lat_rows, lat_rows), lat_rows)
-        local_copy(outgoing.at[image, own_rows], landed.at[p, image])
+        last = pl.ds(lanes - 128, 128)
+        local_copy(
+            outgoing.at[image, :, :, :, :, last], sent_out.at[image]
+        )
+        return [
+            links.push(
+                outgoing.at[image, :, :, 1 - c], paired.at[image], z, p + 1 - 2 * c
+            )
+        ]
+
+    def merge(image, pair):
+        arrived(pair)
+        mine = outgoing[image, :, :, c].reshape(rows_here, lanes).astype(jnp.float32)
+        other = paired[image].reshape(rows_here, lanes).astype(jnp.float32)
+        my_top = mine[:, channels : channels + 1]
+        other_top = other[:, channels : channels + 1]
+        top = jnp.maximum(my_top, other_top)
+        lane = lax.broadcasted_iota(jnp.int32, mine.shape, 1)
+        both = jnp.exp(my_top - top) * mine + jnp.exp(other_top - top) * other
+        both = jnp.where(lane == channels, top, both)
+        merged[image] = both.astype(BF).reshape(place.ny, place.nx, lat_rows, lanes)
+        chip = y * place.nx + x
+        chips = place.ny * place.nx
+        local_copy(merged.at[image, y, x], landed.at[chip, image])
         copies = []
-        for step in range(1, place.group):
-            q = lax.rem(p + step, place.group)
-            rows = pl.ds(pl.multiple_of(q * lat_rows, lat_rows), lat_rows)
-            copies.append(links.push(outgoing.at[image, rows], landed.at[p, image], z, q))
+        for step in range(1, chips):
+            q = lax.rem(chip + step, chips)
+            copies.append(
+                links.push(
+                    merged.at[image, q // place.nx, lax.rem(q, place.nx)],
+                    landed.at[chip, image],
+                    z,
+                    2 * q + c,
+                )
+            )
         return copies
 
-    sent = attend(0)
-    arrived(firsts_m)
-    seconds_m = []
-    for sub, along in mats_a + mats_b:
-        seconds_m += place.push_second(links, all_mats, (every,), sub, along)
-    sent += attend(1)
-    sent += attend(2)
-    arrived(seconds_m)
-    core_m = place.push_core(links, all_mats, (every,))
-    sent += attend(3)
+    for step in range(3, place.nz):
+        first_m(step)
+    core_m(0)
+    pair = attend(0)
+    sent = []
+    for step in range(3, place.nz):
+        second_m(step)
+    core_m(1)
+    for image in range(1, batches):
+        following = attend(image)
+        sent += merge(image - 1, pair)
+        pair = following
+        if image == 1:
+            core_m(2)
+    sent += merge(batches - 1, pair)
+    for step in range(3, place.nz):
+        core_m(step)
     arrived(sent)
-    arrived(core_m)
+    arrived(cores_m)
     links.drain()
-    for copy in local[5:]:
+    for copy in local[9:]:
         copy.wait()
 
 
 def front_copies(nz, ny, nx, batches):
-    plane_first = lambda a, b: a * (nx - 1) + b * (ny - 1)
-    count = 2 * (nz - 1)
-    for step in range(nz):
-        ab = plane_first(1, 1) + (plane_first(1, 0) if step % 2 == 0 else plane_first(0, 1))
-        ba = plane_first(1, 1) + (plane_first(0, 1) if step % 2 == 0 else plane_first(1, 0))
-        count += ab + ba
-    count += 2 * plane_first(1, 1)
-    count += 3 + (nz - 1) + 2 * plane_first(2, 2) + 1
-    count += batches * (2 * nx * ny - 1)
-    return count
+    both = nx + ny - 2
+    count = 3 * (nz - 1) + 2 * nz * (both + max(nx, ny) - 1) + 2 * both
+    count += 2 * nz * 2 * both + 3 + nz
+    return count + batches * nx * ny
 
 
 def front(dims, pixels, pixel_mask, gain_rows, proj_blocks, keyval_t, latents):
@@ -423,8 +489,8 @@
             jax.ShapeDtypeStruct((batches, padded, shard_pixels), BF),
             jax.ShapeDtypeStruct((batches, shard_pixels), jnp.float32),
             jax.ShapeDtypeStruct((batches, all_rows, shard_pixels), BF),
-            jax.ShapeDtypeStruct((batches, all_rows, lanes), BF),
-            jax.ShapeDtypeStruct((group, batches, lat_rows, lanes), BF),
+            jax.ShapeDtypeStruct((batches, ny, nx, 2, lat_rows, 128), BF),
+            jax.ShapeDtypeStruct((ny * nx, batches, lat_rows, lanes), BF),
             jax.ShapeDtypeStruct((all_rows, lanes), BF),
             jax.ShapeDtypeStruct((all_rows, width), BF),
         ),
@@ -453,10 +519,12 @@
             pltpu.VMEM((all_rows, width), BF),
             pltpu.VMEM((batches, padded, shard_pixels), BF),
             pltpu.VMEM((batches, all_rows, shard_pixels), BF),
-            pltpu.VMEM((batches, all_rows, lanes), BF),
+            pltpu.VMEM((batches, ny, nx, 2, lat_rows, lanes), BF),
+            pltpu.VMEM((batches, ny, nx, lat_rows, lanes), BF),
+            pltpu.VMEM((batches, ny, nx, lat_rows, lanes), BF),
             pltpu.SemaphoreType.DMA((copies,)),
             pltpu.SemaphoreType.DMA((copies,)),
-            pltpu.SemaphoreType.DMA((10 + 3 * batches,)),
+            pltpu.SemaphoreType.DMA((14 + 3 * batches,)),
         ],
         compiler_params=pltpu.CompilerParams(
             collective_id=0, has_side_effects=True, vmem_limit_bytes=56 * 2**20
@@ -642,7 +710,8 @@
     shares,
     query_turned,
     query_acc,
-    gain_acc,
+    back_turned,
+    grad_scores,
     gain_cols,
     staged,
     terms,
@@ -652,6 +721,8 @@
     query_levels,
     gain_plane,
     gain_levels,
+    residual_parts,
+    residual_came,
     residual_levels,
     send_sems,
     recv_sems,
@@ -660,7 +731,8 @@
     place = Place(*dims)
     links = Links(send_sems, recv_sems)
     z, y, x, c, p = place.z, place.y, place.x, place.c, place.p
-    group, batches, lat_rows, lanes = landed.shape
+    chips, batches, lat_rows, lanes = landed.shape
+    group = place.group
     rows = batches * lat_rows
     all_rows = group * lat_rows
     width = latents.shape[1]
@@ -690,7 +762,7 @@
             lead = (mat,) + (every,) * (len(mats.shape) - 2)
             copies.append(local_copy(source, mats.at[lead + (cols,)]))
         mats_copies.append(copies)
-    tops_copy = local_copy(sent_all.at[:, :, pl.ds(lanes - 128, 128)], tops)
+    tops_copy = local_copy(sent_all, tops)
 
     def fetch(image):
         slot = image % 2
@@ -713,7 +785,7 @@
 
     came_copy.wait()
     lane = lax.broadcasted_iota(jnp.int32, (rows, lanes), 1)
-    parts = [came[g].reshape(rows, lanes).astype(jnp.float32) for g in range(group)]
+    parts = [came[g].reshape(rows, lanes).astype(jnp.float32) for g in range(chips)]
     top = [part[:, channels : channels + 1] for part in parts]
     peak = functools.reduce(jnp.maximum, top)
     factor = [jnp.exp(value - peak) for value in top]
@@ -774,16 +846,19 @@
                     lead = shape[:3] if 2 * owned == col_blocks else shape[:2]
                     target[where] = pieces.reshape(lead + (height, col_block))
 
-    jobs = [
-        Reduce(place, links, terms[0], buffers[0], "y"),
-        Reduce(place, links, terms[1], buffers[1], "x"),
-        Reduce(place, links, terms[2], buffers[2], "x"),
-        Reduce(place, links, terms[3], buffers[3], "y"),
-        Reduce(place, links, terms[4], buffers[4], "x", place.nz // 2),
-    ]
-    down, inward, out_a, out_b, value_job = jobs
-    store_term([terms[0]], hidden, grad_rows)
-    down.push_core()
+    pairs = []
+    for index in range(3):
+        pairs.append(
+            [
+                Reduce(place, links, terms[2 * index + side], buffers[2 * index + side], along)
+                for side, along in enumerate("xy")
+            ]
+        )
+    down, inward, outer = pairs
+    value_job = Reduce(place, links, terms[6], buffers[6], "x", place.nz // 2)
+    store_term(terms[0:2], hidden, grad_rows)
+    for job in down:
+        job.push_core()
 
     arrived_local(mats_copies[2])
     for index in range(place.nz):
@@ -794,7 +869,8 @@
         grad_pre[:, cols] = (
             grad_hidden.astype(BF).astype(jnp.float32) * slope[:, cols]
         ).astype(BF)
-    down.push_first()
+    for job in down:
+        job.push_first()
     gain_plane[p] = jnp.zeros(gain_plane.shape[1:], jnp.float32)
     for index in range(place.nz):
         cols = slice(index * row_tile, (index + 1) * row_tile)
@@ -825,7 +901,12 @@
             grad_mid[...], rows_of(0, index), NT, preferred_element_type=jnp.float32
         ).astype(BF)
     grad_chan = jnp.dot(grad_attended[...], value_t, preferred_element_type=jnp.float32)
-    row_delta = jnp.sum(attended_chan[...].astype(jnp.float32) * grad_chan, axis=1, keepdims=True)
+    products = attended_chan[...].astype(jnp.float32) * grad_chan
+    row_delta = jnp.sum(products, axis=1, keepdims=True)
+    channel_sums = jnp.sum(products, axis=0, keepdims=True)
+    for sub in range(lanes // 128):
+        row = width // 128 + sub
+        gain_plane[p, row : row + 1, :] = channel_sums[:, sub * 128 : (sub + 1) * 128]
     back = jnp.where(lane == channels + 1, row_delta, grad_chan) / denominator
     back = jnp.where(lane == channels, peak, back)
     shares[y, x, c] = back.astype(BF).reshape(batches, lat_rows, lanes)
@@ -835,86 +916,116 @@
         share_first.append(
             place.push_first(links, shares, (), (image,), "xy"[image % 2])
         )
-    store_term([terms[1]], mid_normed, grad_pre)
-    inward.push_core()
+    gain_sent = []
+    for step in range(1, group):
+        own = gain_plane.at[p]
+        gain_sent.append(links.push(own, own, z, lax.rem(p + step, group)))
     share_second = []
-    for image in range(batches):
+    share_core = []
+
+    def share_on(image):
         arrived(share_first[image])
-        share_second.append(
-            place.push_second(links, shares, (), (image,), "xy"[image % 2])
-        )
-    store_term([terms[2], terms[3]], attended, grad_mid)
-    out_a.push_core()
-    out_b.push_core()
-    share_core = []
-    for image in range(batches):
+        share_second.append(place.push_second(links, shares, (), (image,), "xy"[image % 2]))
+
+    def share_pair(image):
         arrived(share_second[image])
         held = shares.at[:, :, c, image]
         share_core.append([links.push(held, held, z, p + 1 - 2 * c)])
-    terms[4][...] = (
+
+    store_term(terms[2:4], mid_normed, grad_pre)
+    for job in inward:
+        job.push_core()
+    share_on(0)
+    share_on(1)
+    store_term(terms[4:6], attended, grad_mid)
+    for job in outer:
+        job.push_core()
+    share_on(2)
+    share_on(3)
+    terms[6][...] = (
         jnp.dot(grad_attended[...].T, attended_chan[...], preferred_element_type=jnp.float32)
         .astype(BF)
-        .reshape(terms[4].shape)
+        .reshape(terms[6].shape)
     )
     value_job.push_core()
     residual = sum(
         grad_mid[image * lat_rows : (image + 1) * lat_rows].astype(jnp.float32)
         for image in range(batches)
     )
-    residual_levels[z] = residual.astype(BF)
+    part_width = width // place.nz
     residual_sent = []
+    for zz in range(place.nz):
+        residual_parts[zz] = residual[:, zz * part_width : (zz + 1) * part_width].astype(BF)
     for step in range(1, place.nz):
-        level = residual_levels.at[z]
+        zz = lax.rem(z + step, place.nz)
         residual_sent.append(
-            links.push(level, level, lax.rem(z + step, place.nz), p)
+            links.push(residual_parts.at[zz], residual_came.at[step - 1], zz, p)
         )
-    inward.push_first()
-    down.push_second()
+    share_pair(0)
+    share_pair(1)
+    for job in inward:
+        job.push_first()
+    for job in down:
+        job.push_second()
 
     lane_all = lax.broadcasted_iota(jnp.int32, (all_rows, lanes), 1)
     query_turned[...] = jnp.where(
         lane_all < channels, pixel_query[...].astype(jnp.float32), 0.0
     ).T[0:padded].astype(BF)
     query_acc[...] = jnp.zeros(query_acc.shape, jnp.float32)
-    gain_acc[...] = jnp.zeros(gain_acc.shape, jnp.float32)
     gain_cols[0] = jnp.broadcast_to(gain_rows[1:2, 0:lanes], (128, lanes)).T[0:padded]
     gain_cols[1] = jnp.broadcast_to(gain_rows[3:4, 0:lanes], (128, lanes)).T[0:padded]
     chunk = min(512, shard_pixels)
-    staged_out = []
     tops_copy.wait()
 
-    def attend_back(image):
+    def attend_query(image):
         slot = image % 2
         arrived(share_core[image])
         arrived_local(fetched[image])
-        if image >= 2:
-            staged_out[image - 2].wait()
         back = shares[:, :, :, image].reshape(all_rows, lanes).astype(jnp.float32)
-        top = tops[image].astype(jnp.float32)[:, channels - (lanes - 128) :][:, 0:1]
+        top = tops[image].reshape(all_rows, 128).astype(jnp.float32)[
+            :, channels - (lanes - 128) :
+        ][:, 0:1]
         share = jnp.exp(top - back[:, channels : channels + 1])
         back = jnp.where(lane_all == channels, 0.0, back * share)
         back = jnp.where(lane_all > channels + 1, 0.0, back)
         back_low = jnp.where(lane_all == channels + 1, -back, back).astype(BF)[:, 0:padded]
-        back_turned = jnp.where(lane_all < channels, back, 0.0).T[0:padded].astype(BF)
+        back_turned[image] = jnp.where(lane_all < channels, back, 0.0).T[0:padded].astype(BF)
 
         @pl.loop(0, shard_pixels // chunk)
         def _(step):
             cols = pl.ds(pl.multiple_of(step * chunk, chunk), chunk)
             normed_chunk = normed[slot, :, cols]
-            share_chunk = weights[slot, :, cols]
             grad_weights = jnp.dot(back_low, normed_chunk, preferred_element_type=jnp.float32)
-            grad_scores = (share_chunk.astype(jnp.float32) * grad_weights).astype(BF)
+            grad_chunk = (weights[slot, :, cols].astype(jnp.float32) * grad_weights).astype(BF)
+            grad_scores[image, :, cols] = grad_chunk
             query_acc[:, 0:padded] += lax.dot_general(
-                grad_scores, normed_chunk, NT, preferred_element_type=jnp.float32
+                grad_chunk, normed_chunk, NT, preferred_element_type=jnp.float32
             )
+
+        if image + 2 < batches:
+            fetched.append(fetch(image + 2))
+
+    order = list(range(2, batches)) + [0, 1]
+    staged_out = []
+
+    def attend_pixels(turn):
+        image = order[turn]
+        slot = image % 2
+        if turn >= 2:
+            arrived_local(fetched[batches + turn - 2])
+            staged_out[turn - 2].wait()
+
+        @pl.loop(0, shard_pixels // chunk)
+        def _(step):
+            cols = pl.ds(pl.multiple_of(step * chunk, chunk), chunk)
             grad_normed = jnp.dot(
-                query_turned[...], grad_scores, preferred_element_type=jnp.float32
-            ) + jnp.dot(back_turned, share_chunk, preferred_element_type=jnp.float32)
-            normal = normed_chunk.astype(jnp.float32)
-            product = grad_normed * normal
-            folded = sum(product[:, at : at + 128] for at in range(0, chunk, 128))
-            gain_acc[0:padded, :] += folded
-            second_mean = jnp.sum(product, axis=0, keepdims=True) / channels
+                query_turned[...], grad_scores[image, :, cols], preferred_element_type=jnp.float32
+            ) + jnp.dot(
+                back_turned[image], weights[slot, :, cols], preferred_element_type=jnp.float32
+            )
+            normal = normed[slot, :, cols].astype(jnp.float32)
+            second_mean = jnp.sum(grad_normed * normal, axis=0, keepdims=True) / channels
             spread = jnp.concatenate([gain_cols[0]] * (chunk // 128), axis=1)
             spread_back = jnp.concatenate([gain_cols[1]] * (chunk // 128), axis=1)
             grad_hat = grad_normed * spread
@@ -922,28 +1033,35 @@
             result = (grad_hat - first_mean - normal * spread_back * second_mean) * inverse[
                 image : image + 1, cols
             ]
-            staged[slot, :, cols] = result[0:channels].astype(BF)
-
-        staged_out.append(local_copy(staged.at[slot], pixel_grad.at[image]))
-        if image + 2 < batches:
-            fetched.append(fetch(image + 2))
-
-    attend_back(0)
-    out_a.push_first()
-    out_b.push_first()
-    value_job.push_first()
-    inward.push_second()
-    down.push_z()
-    attend_back(1)
-    out_a.push_second()
-    out_b.push_second()
-    value_job.push_second()
-    inward.push_z()
-    attend_back(2)
-    out_a.push_z()
-    out_b.push_z()
-    value_job.push_z()
-    attend_back(3)
+            staged[turn % 2, :, cols] = result[0:channels].astype(BF)
+
+        staged_out.append(local_copy(staged.at[turn % 2], pixel_grad.at[image]))
+        if turn + 2 < batches:
+            fetched.append(fetch(order[turn + 2]))
+
+    attend_query(0)
+    share_pair(2)
+    share_pair(3)
+    attend_query(1)
+    arrived(gain_sent)
+    gain_levels[z] = sum(gain_plane[g] for g in range(group))
+    gain_up = []
+    for step in range(1, place.nz):
+        own = gain_levels.at[z]
+        gain_up.append(links.push(own, own, lax.rem(z + step, place.nz), p))
+    arrived(residual_sent)
+    residual_levels[z] = (
+        residual_parts[z].astype(jnp.float32)
+        + sum(residual_came[slot].astype(jnp.float32) for slot in range(place.nz - 1))
+    ).astype(BF)
+    residual_up = []
+    for step in range(1, place.nz):
+        own = residual_levels.at[z]
+        residual_up.append(links.push(own, own, lax.rem(z + step, place.nz), p))
+    attend_query(2)
+    for job in down:
+        job.push_z()
+    attend_query(3)
 
     query_low[...] = query_acc[...].astype(BF)
     query_sent = []
@@ -951,32 +1069,12 @@
         q = lax.rem(p + step, group)
         part = pl.ds(pl.multiple_of(q * lat_rows, lat_rows), lat_rows)
         query_sent.append(links.push(query_low.at[part], query_came.at[step - 1], z, q))
-    gain_rows = lax.dot_general(
-        jnp.ones((8, 128), jnp.float32),
-        gain_acc[...],
-        NT,
-        precision=HIGHEST,
-        preferred_element_type=jnp.float32,
-    )
-    for sub in range(lanes // 128):
-        row = width // 128 + sub
-        gain_plane[p, row : row + 1, :] = gain_rows[0:1, sub * 128 : (sub + 1) * 128]
-    gain_sent = []
-    for step in range(1, group):
-        own = gain_plane.at[p]
-        gain_sent.append(links.push(own, own, z, lax.rem(p + step, group)))
-
-    def finish(job, target):
-        held, came_z = job.total()
-        for part in came_z:
-            held = held + part[...].astype(jnp.float32)
-        target[...] = held
-
-    finish(down, mats_grad.at[2])
-    finish(inward, mats_grad.at[1])
-    finish(out_a, mats_grad.at[0, :, pl.ds(0, half_rows)])
-    finish(out_b, mats_grad.at[0, :, pl.ds(half_rows, half_rows)])
-
+    for job in outer:
+        job.push_first()
+    value_job.push_first()
+    attend_pixels(0)
+    for job in inward:
+        job.push_second()
     arrived(query_sent)
     own_rows = pl.ds(pl.multiple_of(p * lat_rows, lat_rows), lat_rows)
     held = query_acc[own_rows, :]
@@ -987,35 +1085,54 @@
     for step in range(1, place.nz):
         own = query_levels.at[z]
         query_up.append(links.push(own, own, lax.rem(z + step, place.nz), p))
-    arrived(gain_sent)
-    gain_levels[z] = sum(gain_plane[g] for g in range(group))
-    gain_up = []
-    for step in range(1, place.nz):
-        own = gain_levels.at[z]
-        gain_up.append(links.push(own, own, lax.rem(z + step, place.nz), p))
-
-    held, came_z = value_job.total()
-    above = place.z >= place.nz // 2
-    for part in came_z:
-        held = held + part[...].astype(jnp.float32)
-    value_grad[...] = jnp.where(above, held, 0.0)
-    arrived(residual_sent)
-    residual_total[...] = sum(residual_levels[zz].astype(jnp.float32) for zz in range(place.nz))
-
+    attend_pixels(1)
     arrived(query_up)
     query_total[p] = sum(query_levels[zz].astype(jnp.float32) for zz in range(place.nz)).astype(BF)
     query_all = []
     for step in range(1, group):
         own = query_total.at[p]
         query_all.append(links.push(own, own, z, lax.rem(p + step, group)))
-    arrived(gain_up)
-    gain_total[...] = sum(gain_levels[zz] for zz in range(place.nz))
+    attend_pixels(2)
+    for job in outer:
+        job.push_second()
+    value_job.push_second()
+    for job in inward:
+        job.push_z()
+    attend_pixels(3)
     for index in range(tiles):
         cols = slice(index * tile, (index + 1) * tile)
         mixed[:, cols] = (
             middle[:, cols]
             + jnp.dot(hidden[...], columns_of(2, index), preferred_element_type=jnp.float32)
         ).astype(BF)
+    for job in outer:
+        job.push_z()
+    value_job.push_z()
+
+    def finish(job, target):
+        held, came_z = job.total()
+        for part in came_z:
+            held = held + part[...].astype(jnp.float32)
+        target[...] = held
+
+    def finish_mat(mat, jobs):
+        for side, job in enumerate(jobs):
+            finish(job, mats_grad.at[mat, :, pl.ds(side * half_rows, half_rows)])
+
+    finish_mat(2, down)
+    arrived(gain_up)
+    gain_total[...] = sum(gain_levels[zz] for zz in range(place.nz))
+    arrived(residual_up)
+    for zz in range(place.nz):
+        residual_total[:, zz * part_width : (zz + 1) * part_width] = residual_levels[zz].astype(
+            jnp.float32
+        )
+    finish_mat(1, inward)
+    finish_mat(0, outer)
+    held, came_z = value_job.total()
+    for part in came_z:
+        held = held + part[...].astype(jnp.float32)
+    value_grad[...] = jnp.where(place.z >= place.nz // 2, held, 0.0)
     arrived(query_all)
     links.drain()
     for copy in staged_out[batches - 2 :]:
@@ -1031,15 +1148,16 @@
     group = 2 * ny * nx
     both = nx + ny - 2
     count = batches // 2 * 2 * both + batches
-    count += 5 * (1 + both + nz - 1)
-    count += 2 * (nz - 1) + group - 1 + group - 1 + nz - 1 + group - 1
+    count += 7 * (1 + both + nz - 1)
+    count += 4 * (nz - 1) + 3 * (group - 1)
     return count
 
 
 def back(dims, channels, gathered, latents, gain_rows, mixed_grad):
     landed, all_keyval, all_mats, normed_all, inverse, weights_all, sent_all, pixel_query = gathered
     nz, ny, nx = dims
-    group, batches, lat_rows, lanes = landed.shape
+    batches, lat_rows, lanes = landed.shape[1:]
+    group = 2 * ny * nx
     rows = batches * lat_rows
     all_rows = group * lat_rows
     width = latents.shape[1]
@@ -1051,13 +1169,8 @@
     anywhere = pl.BlockSpec(memory_space=pl.ANY)
     lead = (nz, ny, nx) if 2 * owned * col_block == width else (nz, ny)
     cube = (nz, ny, nx, 2)
-    inners = [
-        (nz, (owned, row_block, col_block), "y"),
-        (nz, (owned, row_block, col_block), "x"),
-        (nz, (owned, half_rows, col_block), "x"),
-        (nz, (owned, half_rows, col_block), "y"),
-        (nz // 2, (keyval_rows, lanes), "x"),
-    ]
+    inners = [(nz, (owned, half_rows, col_block), along) for along in "xyxyxy"]
+    inners.append((nz // 2, (keyval_rows, lanes), "x"))
     terms = [pltpu.VMEM((levels, ny, nx, 2) + inner, BF) for levels, inner, _ in inners]
     buffers = []
     for levels, inner, along in inners:
@@ -1098,12 +1211,12 @@
         ],
         out_specs=(vmem, anywhere, vmem, vmem, vmem, vmem, vmem),
         scratch_shapes=[
-            pltpu.VMEM((group, batches, lat_rows, lanes), BF),
+            pltpu.VMEM((ny * nx, batches, lat_rows, lanes), BF),
             pltpu.VMEM((nz // 2, ny, nx, 2, keyval_rows, lanes), BF),
             pltpu.VMEM((3,) + lead + (row_block, width), BF),
             pltpu.VMEM((2, padded, shard_pixels), BF),
             pltpu.VMEM((2, all_rows, shard_pixels), BF),
-            pltpu.VMEM((batches, all_rows, 128), BF),
+            pltpu.VMEM((batches, ny, nx, 2, lat_rows, 128), BF),
             pltpu.VMEM((rows, lanes), BF),
             wide(BF),
             wide(jnp.float32),
@@ -1119,7 +1232,8 @@
             pltpu.VMEM(cube[1:] + (batches, lat_rows, lanes), BF),
             pltpu.VMEM((padded, all_rows), BF),
             pltpu.VMEM((all_rows, lanes), jnp.float32),
-            pltpu.VMEM((lanes, 128), jnp.float32),
+            pltpu.VMEM((batches, padded, all_rows), BF),
+            pltpu.VMEM((batches, all_rows, shard_pixels), BF),
             pltpu.VMEM((2, padded, 128), jnp.float32),
             pltpu.VMEM((2, channels, shard_pixels), BF),
             terms,
@@ -1129,10 +1243,12 @@
             pltpu.VMEM((nz, lat_rows, lanes), BF),
             pltpu.VMEM((group, 16, 128), jnp.float32),
             pltpu.VMEM((nz, 16, 128), jnp.float32),
-            pltpu.VMEM((nz, lat_rows, width), BF),
+            pltpu.VMEM((nz, lat_rows, width // nz), BF),
+            pltpu.VMEM((nz - 1, lat_rows, width // nz), BF),
+            pltpu.VMEM((nz, lat_rows, width // nz), BF),
             pltpu.SemaphoreType.DMA((copies,)),
             pltpu.SemaphoreType.DMA((copies,)),
-            pltpu.SemaphoreType.DMA((3 + 3 * (width // col_block) + 3 * batches,)),
+            pltpu.SemaphoreType.DMA((3 + 3 * (width // col_block) + 5 * batches,)),
         ],
         compiler_params=pltpu.CompilerParams(
             collective_id=1, has_side_effects=True, vmem_limit_bytes=61 * 2**20
@@ -1177,6 +1293,8 @@
     query_blocks,
     all_keyval,
     pixel_low,
+    pixel_query,
+    gain_total,
     pixel_grad,
     proj_grad,
     left_new,
@@ -1189,6 +1307,7 @@
     latent_second_new,
     latent_new,
     lat_gain_grad,
+    channel_gain_grad,
     query,
     lat_normed,
     query_weight,
@@ -1274,6 +1393,14 @@
     scale = width ** (-0.5)
     query_sum = query_total[...].reshape(all_rows, lanes)
     key_t = keys[...].reshape(width, lanes)
+    products = query_sum.astype(jnp.float32) * pixel_query[...].astype(jnp.float32)
+    sums = jnp.sum(products, axis=0, keepdims=True)
+    first = width // 128
+    for sub in range(lanes // 128):
+        cols = slice(sub * 128, (sub + 1) * 128)
+        channel_gain_grad[:, cols] = (
+            sums[:, cols] + gain_total[first + sub : first + sub + 1, :]
+        ) * gain_rows[3:4, cols]
     for start in range(0, width, 256):
         grad_query[:, start : start + 256] = (
             lax.dot_general(
@@ -1355,6 +1482,8 @@
     query_blocks,
     all_keyval,
     pixel_low,
+    pixel_query,
+    gain_total,
 ):
     nz, ny, nx = dims
     proj_blocks, keyval_weight, latents = owned_arrays[0], owned_arrays[5], owned_arrays[7]
@@ -1381,12 +1510,13 @@
         like(latents),
         like(latents),
         jax.ShapeDtypeStruct((1, width), jnp.float32),
+        jax.ShapeDtypeStruct((1, lanes), jnp.float32),
     ]
     return pl.pallas_call(
         functools.partial(tail_kernel, dims, channels),
         out_shape=results,
-        in_specs=[vmem] * 14 + [anywhere] * 5,
-        out_specs=[anywhere] + [vmem] * 11,
+        in_specs=[vmem] * 14 + [anywhere] * 5 + [vmem] * 2,
+        out_specs=[anywhere] + [vmem] * 12,
         scratch_shapes=[
             pltpu.VMEM((all_rows, width), BF),
             pltpu.VMEM((all_rows, width), BF),
@@ -1413,6 +1543,8 @@
         query_blocks,
         all_keyval,
         pixel_low,
+        pixel_query,
+        gain_total,
     )
 
 
@@ -1486,6 +1618,7 @@
         latent_second_new,
         latent_new,
         lat_gain_grad,
+        channel_gain_grad,
     ) = tail(
         dims,
         query_total,
@@ -1509,12 +1642,14 @@
         query_blocks,
         keyval_t,
         pixel_low,
+        pixel_query,
+        gain_total,
     )
     gain_sums = gain_total.reshape(-1)
     gain_grad = jnp.concatenate(
         [
             lat_gain_grad[0],
-            gain_sums[width : width + channels] / in_gain,
+            channel_gain_grad[0, :channels],
             gain_sums[:width],
         ],
         axis=0,

time: 192 us -> 168 us (0.88)
  Pallas kernels: 185 us -> 161 us
    pallas_call x1, Pallas kernels: 83.6 us -> 70 us  [front(): pl.pallas_call(functools.partial(front_kernel, dims), out_shape=(jax.Shap...]
    pallas_call x1, Pallas kernels: 88.8 us -> 78.5 us  [back(): pl.pallas_call(functools.partial(back_kernel, dims, channels), out_shape=...]
where the time goes in v5:
time: 168 us; the launch traced here: 167 us
  Pallas kernels  161 us (96%)
  local copies, waits for them, and re-layouts  3.75 us (2%)
  other arithmetic  1.94 us (1%)
    pallas_call x1, Pallas kernels, back(): pl.pallas_call(functools.partial(back_kernel, dims, channels), out_shape=...  78.5 us
    pallas_call x1, Pallas kernels, front(): pl.pallas_call(functools.partial(front_kernel, dims), out_shape=(jax.Shap...  70 us
    pallas_call x1, Pallas kernels, tail(): pl.pallas_call(functools.partial(tail_kernel, dims, channels), out_shape=...  12.4 us

profile of v5, /device:TPU:0, one launch (start us, length us, event | category | flops | bytes accessed | tf_op | source)
XLA Modules:
  0.0 167.2 jit_solution(5186725732786987314)
XLA Ops:
  0.6 0.7 fusion.3
  1.3 0.8 fusion.2
  2.1 0.6 pad_maximum_fusion.gain_rows
  2.8 70.0 %shard_map.253 = (bf16[4,2,2,2,4,64,128]{6,5,4,3,2,1,0:T(8,128)(2,1)}, bf16[4,2,2,2,64,384]{5,4,3,2,1,0:T(8,128)(2,1)}, bf16[512,1024]{1,0:T(8,128)(2,1)}, bf16[...) custom-call(bf16[261,4,2048]{2,1,0:T(4,128)(2,1)} %bitcast.16, ...), custom_call_target="tpu_custom_call" | custom-call | tf_op jit(solution)/shard_map/pallas_call | solution.py:482
  72.8 78.5 %shard_map.254 = (bf16[256,1024]{1,0:T(8,128)(2,1)}, bf16[4,261,2048]{2,1,0:T(8,128)(2,1)}, f32[3,4,64,128]{3,2,1,0:T(8,128)}, f32[64,384]{1,0:T(8,128)}, bf16[8...) custom-call(bf16[4,4,64,384]{3,2,1,0:T(8,128)(2,1)} %get-tuple-element.46.landed, ...), custom_call_target="tpu_custom_call" | custom-call | tf_op jit(solution)/shard_map/pallas_call | solution.py:1188
  151.2 0.7 slice_bitcast_fusion
  151.9 0.0 copy-start.2
  151.9 0.0 copy-start.3
  151.9 0.0 copy-start
  151.9 12.4 %shard_map.255 = (f32[261,4,2048]{2,1,0:T(4,128)}, f32[4,4,64,128]{3,2,1,0:T(8,128)}, f32[4,4,64,64]{3,2,1,0:T(8,128)}, f32[4,4,128,128]{3,2,1,0:T(8,128)}, f32[...) custom-call(bf16[8,64,384]{2,1,0:T(8,128)(2,1)} %get-tuple-element.5, ...), custom_call_target="tpu_custom_call" | custom-call | tf_op jit(solution)/shard_map/pallas_call | solution.py:1515
  164.3 0.7 slice_reduce_fusion
  165.0 0.8 concatenate.3
  165.8 0.0 copy-done.2
  165.8 0.0 copy-done.3
  165.8 0.0 copy-start.1
  165.8 0.6 divide_subtract_fusion
  166.4 0.0 copy-done
  166.4 0.8 copy.30
  167.2 0.0 copy-done.1
  (2 shorter events, 0.0 us)
Async XLA Ops:
  151.9 13.8 %copy-start.2 = (f32[2309]{0:T(1024)S(1)}, f32[2309]{0:T(1024)}, u32[]{:S(2)}) copy-start(f32[2309]{0:T(1024)} %param.25) | copy-start | bytes 27712
  151.9 13.8 %copy-start.3 = (f32[2309]{0:T(1024)S(1)}, f32[2309]{0:T(1024)}, u32[]{:S(2)}) copy-start(f32[2309]{0:T(1024)} %param.26) | copy-start | bytes 27712
  151.9 14.5 %copy-start = (bf16[256,1024]{1,0:T(8,128)(2,1)S(1)}, bf16[256,1024]{1,0:T(8,128)(2,1)}, u32[]{:S(2)}) copy-start(bf16[256,1024]{1,0:T(8,128)(2,1)} %get-tuple-element.54) | copy-start | bytes 1572868
  165.8 1.4 copy-start.1

commit v6 on v5

--- a/solution.py
+++ b/solution.py
@@ -544,10 +544,9 @@
 
 
 class Reduce:
-    def __init__(self, place, links, term, buffers, along, base=0):
+    def __init__(self, place, links, term, buffers, along):
         self.place, self.links, self.term, self.along = place, links, term, along
         self.by_core, self.by_first, self.by_second, self.by_z = buffers
-        self.base = base
         self.waiting = []
 
     def wait(self):
@@ -625,40 +624,84 @@
         for slot in range(self.by_second.shape[0]):
             held = held + self.by_second[slot].astype(jnp.float32)
         self.by_second[0] = held.astype(BF)
-        self.sends = []
         for step in range(1, place.nz):
             zz = lax.rem(place.z - step + place.nz, place.nz)
-            if self.base == 0:
-                self.waiting.append(
-                    self.links.push(
-                        self.by_second.at[0, zz], self.by_z.at[step - 1], zz, place.p
-                    )
+            self.waiting.append(
+                self.links.push(self.by_second.at[0, zz], self.by_z.at[step - 1], zz, place.p)
+            )
+
+    def total(self):
+        self.wait()
+        held = self.by_second[0, self.place.z].astype(jnp.float32)
+        return held, [self.by_z.at[slot] for slot in range(self.by_z.shape[0])]
+
+
+class ReduceDown(Reduce):
+    def push_z(self):
+        place = self.place
+        self.wait()
+
+        @pl.loop(0, self.by_core.shape[0])
+        def _(level):
+            self.by_core[level] = add_low(
+                self.by_core[level], self.term[level, :, :, place.c]
+            )
+
+        for step in range(1, place.nz):
+            zz = lax.rem(place.z - step + place.nz, place.nz)
+            self.waiting.append(
+                self.links.push(self.by_core.at[zz], self.by_z.at[step - 1], zz, place.p)
+            )
+
+    def push_first(self):
+        place = self.place
+        self.wait()
+        held = self.by_core[place.z].astype(jnp.float32)
+        for slot in range(self.by_z.shape[0]):
+            held = held + self.by_z[slot].astype(jnp.float32)
+        self.by_z[0] = held.astype(BF)
+        every = slice(None)
+        for step in range(1, place.nx if self.along == "x" else place.ny):
+            if self.along == "x":
+                other = lax.rem(place.x + step, place.nx)
+                source = self.by_z.at[0, every, other]
+                target = place.pix(place.y, other, place.c)
+            else:
+                other = lax.rem(place.y + step, place.ny)
+                source = self.by_z.at[0, other]
+                target = place.pix(other, place.x, place.c)
+            self.waiting.append(
+                self.links.push(source, self.by_first.at[step - 1], place.z, target)
+            )
+
+    def push_second(self):
+        place = self.place
+        self.wait()
+        if self.along == "x":
+            held = self.by_z[0, :, place.x].astype(jnp.float32)
+        else:
+            held = self.by_z[0, place.y].astype(jnp.float32)
+        for slot in range(self.by_first.shape[0]):
+            held = held + self.by_first[slot].astype(jnp.float32)
+        self.by_first[0] = held.astype(BF)
+        for step in range(1, place.ny if self.along == "x" else place.nx):
+            if self.along == "x":
+                other = lax.rem(place.y + step, place.ny)
+                target = place.pix(other, place.x, place.c)
+            else:
+                other = lax.rem(place.x + step, place.nx)
+                target = place.pix(place.y, other, place.c)
+            self.waiting.append(
+                self.links.push(
+                    self.by_first.at[0, other], self.by_second.at[step - 1], place.z, target
                 )
-            else:
-                level = jnp.maximum(zz - self.base, 0)
-                copy = self.links.make(
-                    self.by_second.at[0, level], self.by_z.at[step - 1], zz, place.p
-                )
-                pl.when(zz >= self.base)(copy.start)
-                self.sends.append((zz, copy))
+            )
 
     def total(self):
-        place = self.place
-        level = place.z
-        if self.base == 0:
-            self.wait()
-        else:
-            level = jnp.maximum(place.z - self.base, 0)
-
-            @pl.when(place.z >= self.base)
-            def _():
-                for _, copy in self.sends:
-                    copy.wait_recv()
-
-            for zz, copy in self.sends:
-                pl.when(zz >= self.base)(copy.wait_send)
-        held = self.by_second[0, level].astype(jnp.float32)
-        return held, [self.by_z.at[slot] for slot in range(self.by_z.shape[0])]
+        self.wait()
+        mine = self.place.y if self.along == "x" else self.place.x
+        held = self.by_first[0, mine].astype(jnp.float32)
+        return held, [self.by_second.at[slot] for slot in range(self.by_second.shape[0])]
 
 
 def block_index(block, col_blocks, owned):
@@ -685,7 +728,7 @@
     mixed,
     pixel_grad,
     mats_grad,
-    value_grad,
+    chan_total,
     query_total,
     gain_total,
     residual_total,
@@ -847,15 +890,15 @@
                     target[where] = pieces.reshape(lead + (height, col_block))
 
     pairs = []
-    for index in range(3):
+    for index, kind in enumerate((ReduceDown, Reduce)):
         pairs.append(
             [
-                Reduce(place, links, terms[2 * index + side], buffers[2 * index + side], along)
+                kind(place, links, terms[2 * index + side], buffers[2 * index + side], along)
                 for side, along in enumerate("xy")
             ]
         )
-    down, inward, outer = pairs
-    value_job = Reduce(place, links, terms[6], buffers[6], "x", place.nz // 2)
+    down, inward = pairs
+    chan_job = Reduce(place, links, terms[4], buffers[4], "x")
     store_term(terms[0:2], hidden, grad_rows)
     for job in down:
         job.push_core()
@@ -870,7 +913,7 @@
             grad_hidden.astype(BF).astype(jnp.float32) * slope[:, cols]
         ).astype(BF)
     for job in down:
-        job.push_first()
+        job.push_z()
     gain_plane[p] = jnp.zeros(gain_plane.shape[1:], jnp.float32)
     for index in range(place.nz):
         cols = slice(index * row_tile, (index + 1) * row_tile)
@@ -932,22 +975,20 @@
         held = shares.at[:, :, c, image]
         share_core.append([links.push(held, held, z, p + 1 - 2 * c)])
 
+    terms[4][...] = (
+        jnp.dot(grad_mid[...].T, attended_chan[...], preferred_element_type=jnp.float32)
+        .astype(BF)
+        .reshape(terms[4].shape)
+    )
+    chan_job.push_core()
     store_term(terms[2:4], mid_normed, grad_pre)
     for job in inward:
         job.push_core()
-    share_on(0)
-    share_on(1)
-    store_term(terms[4:6], attended, grad_mid)
-    for job in outer:
-        job.push_core()
-    share_on(2)
-    share_on(3)
-    terms[6][...] = (
-        jnp.dot(grad_attended[...].T, attended_chan[...], preferred_element_type=jnp.float32)
-        .astype(BF)
-        .reshape(terms[6].shape)
-    )
-    value_job.push_core()
+    for image in range(batches):
+        share_on(image)
+    chan_job.push_first()
+    for job in inward:
+        job.push_first()
     residual = sum(
         grad_mid[image * lat_rows : (image + 1) * lat_rows].astype(jnp.float32)
         for image in range(batches)
@@ -961,12 +1002,6 @@
         residual_sent.append(
             links.push(residual_parts.at[zz], residual_came.at[step - 1], zz, p)
         )
-    share_pair(0)
-    share_pair(1)
-    for job in inward:
-        job.push_first()
-    for job in down:
-        job.push_second()
 
     lane_all = lax.broadcasted_iota(jnp.int32, (all_rows, lanes), 1)
     query_turned[...] = jnp.where(
@@ -1039,9 +1074,12 @@
         if turn + 2 < batches:
             fetched.append(fetch(order[turn + 2]))
 
+    share_pair(0)
+    share_pair(1)
     attend_query(0)
     share_pair(2)
     share_pair(3)
+    chan_job.push_second()
     attend_query(1)
     arrived(gain_sent)
     gain_levels[z] = sum(gain_plane[g] for g in range(group))
@@ -1049,18 +1087,10 @@
     for step in range(1, place.nz):
         own = gain_levels.at[z]
         gain_up.append(links.push(own, own, lax.rem(z + step, place.nz), p))
-    arrived(residual_sent)
-    residual_levels[z] = (
-        residual_parts[z].astype(jnp.float32)
-        + sum(residual_came[slot].astype(jnp.float32) for slot in range(place.nz - 1))
-    ).astype(BF)
-    residual_up = []
-    for step in range(1, place.nz):
-        own = residual_levels.at[z]
-        residual_up.append(links.push(own, own, lax.rem(z + step, place.nz), p))
     attend_query(2)
-    for job in down:
-        job.push_z()
+    chan_job.push_z()
+    for job in inward:
+        job.push_second()
     attend_query(3)
 
     query_low[...] = query_acc[...].astype(BF)
@@ -1069,12 +1099,16 @@
         q = lax.rem(p + step, group)
         part = pl.ds(pl.multiple_of(q * lat_rows, lat_rows), lat_rows)
         query_sent.append(links.push(query_low.at[part], query_came.at[step - 1], z, q))
-    for job in outer:
+    attend_pixels(0)
+    held, came_z = chan_job.total()
+    for part in came_z:
+        held = held + part[...].astype(jnp.float32)
+    chan_total[z, y, x, c] = held.astype(BF)
+    chan_z = []
+    for step in range(1, place.nz):
+        chan_z += place.push_z(links, chan_total, step)
+    for job in down:
         job.push_first()
-    value_job.push_first()
-    attend_pixels(0)
-    for job in inward:
-        job.push_second()
     arrived(query_sent)
     own_rows = pl.ds(pl.multiple_of(p * lat_rows, lat_rows), lat_rows)
     held = query_acc[own_rows, :]
@@ -1086,29 +1120,39 @@
         own = query_levels.at[z]
         query_up.append(links.push(own, own, lax.rem(z + step, place.nz), p))
     attend_pixels(1)
+    arrived(chan_z)
+    chan_first = place.push_first(links, chan_total, (every,), (), "x")
     arrived(query_up)
     query_total[p] = sum(query_levels[zz].astype(jnp.float32) for zz in range(place.nz)).astype(BF)
     query_all = []
     for step in range(1, group):
         own = query_total.at[p]
         query_all.append(links.push(own, own, z, lax.rem(p + step, group)))
-    attend_pixels(2)
-    for job in outer:
-        job.push_second()
-    value_job.push_second()
     for job in inward:
         job.push_z()
+    for job in down:
+        job.push_second()
+    attend_pixels(2)
+    arrived(chan_first)
+    chan_second = place.push_second(links, chan_total, (every,), (), "x")
+    arrived(residual_sent)
+    residual_levels[z] = (
+        residual_parts[z].astype(jnp.float32)
+        + sum(residual_came[slot].astype(jnp.float32) for slot in range(place.nz - 1))
+    ).astype(BF)
+    residual_up = []
+    for step in range(1, place.nz):
+        own = residual_levels.at[z]
+        residual_up.append(links.push(own, own, lax.rem(z + step, place.nz), p))
     attend_pixels(3)
+    arrived(chan_second)
+    chan_core = place.push_core(links, chan_total, (every,))
     for index in range(tiles):
         cols = slice(index * tile, (index + 1) * tile)
         mixed[:, cols] = (
             middle[:, cols]
             + jnp.dot(hidden[...], columns_of(2, index), preferred_element_type=jnp.float32)
         ).astype(BF)
-    for job in outer:
-        job.push_z()
-    value_job.push_z()
-
     def finish(job, target):
         held, came_z = job.total()
         for part in came_z:
@@ -1119,7 +1163,7 @@
         for side, job in enumerate(jobs):
             finish(job, mats_grad.at[mat, :, pl.ds(side * half_rows, half_rows)])
 
-    finish_mat(2, down)
+    finish_mat(1, down)
     arrived(gain_up)
     gain_total[...] = sum(gain_levels[zz] for zz in range(place.nz))
     arrived(residual_up)
@@ -1127,12 +1171,8 @@
         residual_total[:, zz * part_width : (zz + 1) * part_width] = residual_levels[zz].astype(
             jnp.float32
         )
-    finish_mat(1, inward)
-    finish_mat(0, outer)
-    held, came_z = value_job.total()
-    for part in came_z:
-        held = held + part[...].astype(jnp.float32)
-    value_grad[...] = jnp.where(place.z >= place.nz // 2, held, 0.0)
+    finish_mat(0, inward)
+    arrived(chan_core)
     arrived(query_all)
     links.drain()
     for copy in staged_out[batches - 2 :]:
@@ -1148,7 +1188,7 @@
     group = 2 * ny * nx
     both = nx + ny - 2
     count = batches // 2 * 2 * both + batches
-    count += 7 * (1 + both + nz - 1)
+    count += 5 * (1 + both + nz - 1) + nz - 1 + both + 1
     count += 4 * (nz - 1) + 3 * (group - 1)
     return count
 
@@ -1169,18 +1209,19 @@
     anywhere = pl.BlockSpec(memory_space=pl.ANY)
     lead = (nz, ny, nx) if 2 * owned * col_block == width else (nz, ny)
     cube = (nz, ny, nx, 2)
-    inners = [(nz, (owned, half_rows, col_block), along) for along in "xyxyxy"]
-    inners.append((nz // 2, (keyval_rows, lanes), "x"))
+    inners = [(nz, (owned, half_rows, col_block), along) for along in "xyxy"]
+    inners.append((nz, (width // (group * nz), lanes), "x"))
     terms = [pltpu.VMEM((levels, ny, nx, 2) + inner, BF) for levels, inner, _ in inners]
     buffers = []
-    for levels, inner, along in inners:
+    for index, (levels, inner, along) in enumerate(inners):
         one, two = (nx, ny) if along == "x" else (ny, nx)
+        plane_last = index < 2
         buffers.append(
             [
                 pltpu.VMEM((levels, ny, nx) + inner, BF),
-                pltpu.VMEM((one - 1, levels, two) + inner, BF),
-                pltpu.VMEM((two - 1, levels) + inner, BF),
-                pltpu.VMEM((nz - 1,) + inner, BF),
+                pltpu.VMEM((one - 1,) + (() if plane_last else (levels,)) + (two,) + inner, BF),
+                pltpu.VMEM((two - 1,) + (() if plane_last else (levels,)) + inner, BF),
+                pltpu.VMEM((nz - 1,) + ((ny, nx) if plane_last else ()) + inner, BF),
             ]
         )
     wide = lambda kind: pltpu.VMEM((rows, width), kind)
@@ -1190,8 +1231,8 @@
         out_shape=(
             jax.ShapeDtypeStruct((rows, width), BF),
             jax.ShapeDtypeStruct((batches, channels, shard_pixels), BF),
-            jax.ShapeDtypeStruct((3, owned, row_block, col_block), jnp.float32),
-            jax.ShapeDtypeStruct((keyval_rows, lanes), jnp.float32),
+            jax.ShapeDtypeStruct((2, owned, row_block, col_block), jnp.float32),
+            jax.ShapeDtypeStruct(cube + (width // (group * nz), lanes), BF),
             jax.ShapeDtypeStruct((group, lat_rows, lanes), BF),
             jax.ShapeDtypeStruct((16, 128), jnp.float32),
             jax.ShapeDtypeStruct((lat_rows, width), jnp.float32),
@@ -1277,7 +1318,7 @@
     query_total,
     residual_total,
     mats_grad,
-    value_grad,
+    chan_grad,
     proj_blocks,
     proj_left,
     proj_right,
@@ -1295,6 +1336,8 @@
     pixel_low,
     pixel_query,
     gain_total,
+    all_rows_keyval,
+    all_mats,
     pixel_grad,
     proj_grad,
     left_new,
@@ -1318,6 +1361,8 @@
     grad_normed,
     query_grad,
     key_rows,
+    value_block,
+    output_block,
     local_sems,
 ):
     place = Place(*dims)
@@ -1349,6 +1394,20 @@
             )
         )
     normed_copy = local_copy(lat_normed_in, lat_normed)
+    block_row = device * owned // col_blocks
+    block_col = lax.rem(device * owned, col_blocks)
+    half_devices = width // keyval_rows
+    key_start = lax.rem(device, half_devices) * keyval_rows
+    value_rows = pl.ds(pl.multiple_of(width + block_row * row_block, row_block), row_block)
+    value_copy = local_copy(all_rows_keyval.at[value_rows], value_block)
+    output_row = key_start // row_block
+    if 2 * owned == col_blocks:
+        across = lax.rem(output_row, place.nx)
+        along = lax.rem(output_row // place.nx, place.ny)
+        source = all_mats.at[output_row // (place.nx * place.ny), along, across, :, 0]
+    else:
+        source = all_mats.at[output_row // place.ny, lax.rem(output_row, place.ny), :, :, 0, 0]
+    output_copy = local_copy(source, output_block)
     query_copy = local_copy(query_in, query)
     pixel_copies = [local_copy(pixel_low.at[i], pixel_came.at[i]) for i in range(batches)]
     pixel_sent = []
@@ -1385,10 +1444,17 @@
         )
         proj_new[index, mat] = proj_blocks[index, mat] - MATRIX_RATE * step
 
-    for mat in range(3):
+    for mat in range(2):
         for index in range(owned):
-            precondition(mat + 1, index, mats_grad[mat, index])
+            precondition(mat + 2, index, mats_grad[mat, index])
     widen(0)
+    value_copy.wait()
+    own_cols = pl.ds(pl.multiple_of(block_col * col_block, col_block), owned * col_block)
+    output_grad = lax.dot_general(
+        value_block[...], chan_grad[own_cols, :], NT, preferred_element_type=jnp.float32
+    )
+    for index in range(owned):
+        precondition(1, index, output_grad[:, index * col_block : (index + 1) * col_block])
     keys_copy.wait()
     scale = width ** (-0.5)
     query_sum = query_total[...].reshape(all_rows, lanes)
@@ -1441,8 +1507,6 @@
     latent_grad[...] = grad
     moments(latents, grad, latent_second, LATENT_RATE, latent_second_new, latent_new)
 
-    block_row = device * owned // col_blocks
-    block_col = lax.rem(device * owned, col_blocks)
     per_lane = 128 // row_block
     rows = pl.ds(pl.multiple_of(block_row // per_lane * 128, 128), 128)
     cols = pl.ds(pl.multiple_of(block_col * col_block, col_block), owned * col_block)
@@ -1455,14 +1519,24 @@
     widen(3)
 
     query_copy.wait()
-    half_devices = width // keyval_rows
-    start = lax.rem(device, half_devices) * keyval_rows
-    cols = pl.ds(pl.multiple_of(start // 128 * 128, 128), 128)
+    cols = pl.ds(pl.multiple_of(key_start // 128 * 128, 128), 128)
     key_rows[...] = (
         lax.dot_general(query[:, cols], query_sum, TN, preferred_element_type=jnp.float32) * scale
     )
-    part = pl.ds(pl.multiple_of(lax.rem(start, 128), keyval_rows), keyval_rows)
-    grad = jnp.where(device < half_devices, key_rows[part, :], value_grad[...])[:, 0:channels]
+    part = pl.ds(pl.multiple_of(lax.rem(key_start, 128), keyval_rows), keyval_rows)
+    grad = key_rows[part, :]
+    output_copy.wait()
+    blocks = output_block[...].reshape(col_blocks, row_block, col_block)
+    key_rows[0:row_block, :] = sum(
+        jnp.dot(
+            blocks[block],
+            chan_grad[block * col_block : (block + 1) * col_block, :],
+            preferred_element_type=jnp.float32,
+        )
+        for block in range(col_blocks)
+    )
+    part = pl.ds(pl.multiple_of(lax.rem(key_start, row_block), keyval_rows), keyval_rows)
+    grad = jnp.where(device < half_devices, grad, key_rows[part, :])[:, 0:channels]
     keyval_grad[...] = grad
     moments(keyval_weight, grad, keyval_second, KEYVAL_RATE, keyval_second_new, keyval_new)
     for copy in pixel_sent:
@@ -1474,7 +1548,7 @@
     query_total,
     residual_total,
     mats_grad,
-    value_grad,
+    chan_grad,
     owned_arrays,
     gain_rows,
     query,
@@ -1484,6 +1558,7 @@
     pixel_low,
     pixel_query,
     gain_total,
+    all_mats,
 ):
     nz, ny, nx = dims
     proj_blocks, keyval_weight, latents = owned_arrays[0], owned_arrays[5], owned_arrays[7]
@@ -1515,7 +1590,7 @@
     return pl.pallas_call(
         functools.partial(tail_kernel, dims, channels),
         out_shape=results,
-        in_specs=[vmem] * 14 + [anywhere] * 5 + [vmem] * 2,
+        in_specs=[vmem] * 14 + [anywhere] * 5 + [vmem] * 2 + [anywhere] * 2,
         out_specs=[anywhere] + [vmem] * 12,
         scratch_shapes=[
             pltpu.VMEM((all_rows, width), BF),
@@ -1528,14 +1603,16 @@
             pltpu.VMEM((all_rows, width), jnp.float32),
             pltpu.VMEM((128, owned * col_block), jnp.float32),
             pltpu.VMEM((128, lanes), jnp.float32),
-            pltpu.SemaphoreType.DMA((3 + width // col_block + 2 * batches,)),
+            pltpu.VMEM((row_block, lanes), BF),
+            pltpu.VMEM((2, owned, row_block, col_block) if len(lead) == 3 else (nx, 2, row_block, col_block), BF),
+            pltpu.SemaphoreType.DMA((5 + width // col_block + 2 * batches,)),
         ],
         compiler_params=pltpu.CompilerParams(vmem_limit_bytes=56 * 2**20),
     )(
         query_total,
         residual_total,
         mats_grad,
-        value_grad,
+        chan_grad.reshape(width, lanes),
         *owned_arrays,
         gain_rows,
         query,
@@ -1545,6 +1622,8 @@
         pixel_low,
         pixel_query,
         gain_total,
+        all_keyval.reshape(2 * width, lanes),
+        all_mats,
     )
 
 
@@ -1602,7 +1681,7 @@
         sent_all,
         pixel_query,
     )
-    mixed, pixel_low, mats_grad, value_grad, query_total, gain_total, residual_total = back(
+    mixed, pixel_low, mats_grad, chan_grad, query_total, gain_total, residual_total = back(
         dims, channels, gathered, latents, gain_rows, mixed_grad
     )
     (
@@ -1624,7 +1703,7 @@
         query_total,
         residual_total,
         mats_grad,
-        value_grad,
+        chan_grad,
         (
             proj_blocks,
             proj_left,
@@ -1644,6 +1723,7 @@
         pixel_low,
         pixel_query,
         gain_total,
+        mats,
     )
     gain_sums = gain_total.reshape(-1)
     gain_grad = jnp.concatenate(

time: 168 us -> 160 us (0.952)
  Pallas kernels: 161 us -> 153 us
    pallas_call x1, Pallas kernels: 78.5 us -> 70.2 us  [back(): pl.pallas_call(functools.partial(back_kernel, dims, channels), out_shape=...]
where the time goes in v6:
time: 160 us; the launch traced here: 159 us
  Pallas kernels  153 us (96%)
  local copies, waits for them, and re-layouts  3.08 us (2%)
  other arithmetic  1.94 us (1%)
    pallas_call x1, Pallas kernels, back(): pl.pallas_call(functools.partial(back_kernel, dims, channels), out_shape=...  70.2 us
    pallas_call x1, Pallas kernels, front(): pl.pallas_call(functools.partial(front_kernel, dims), out_shape=(jax.Shap...  70 us
    pallas_call x1, Pallas kernels, tail(): pl.pallas_call(functools.partial(tail_kernel, dims, channels), out_shape=...  13.3 us

profile of v6, /device:TPU:0, one launch (start us, length us, event | category | flops | bytes accessed | tf_op | source)
XLA Modules:
  0.0 159.2 jit_solution(16736630954461443646)
XLA Ops:
  0.6 0.7 fusion.3
  1.3 0.8 fusion.2
  2.1 0.6 pad_maximum_fusion.gain_rows
  2.8 70.0 %shard_map.253 = (bf16[4,2,2,2,4,64,128]{6,5,4,3,2,1,0:T(8,128)(2,1)}, bf16[4,2,2,2,64,384]{5,4,3,2,1,0:T(8,128)(2,1)}, bf16[512,1024]{1,0:T(8,128)(2,1)}, bf16[...) custom-call(bf16[261,4,2048]{2,1,0:T(4,128)(2,1)} %bitcast.19, ...), custom_call_target="tpu_custom_call" | custom-call | tf_op jit(solution)/shard_map/pallas_call | solution.py:482
  72.8 70.2 %shard_map.254 = (bf16[256,1024]{1,0:T(8,128)(2,1)}, bf16[4,261,2048]{2,1,0:T(8,128)(2,1)}, f32[2,4,64,128]{3,2,1,0:T(8,128)}, bf16[4,2,2,2,32,384]{5,4,3,2,1,0:...) custom-call(bf16[4,4,64,384]{3,2,1,0:T(8,128)(2,1)} %get-tuple-element.46.landed, ...), custom_call_target="tpu_custom_call" | custom-call | tf_op jit(solution)/shard_map/pallas_call | solution.py:1229
  142.9 0.0 copy-start.3
  143.0 0.0 copy-start.2
  143.0 0.0 copy-start.4
  143.0 0.0 copy-start
  143.0 13.3 %shard_map.255 = (f32[261,4,2048]{2,1,0:T(4,128)}, f32[4,4,64,128]{3,2,1,0:T(8,128)}, f32[4,4,64,64]{3,2,1,0:T(8,128)}, f32[4,4,128,128]{3,2,1,0:T(8,128)}, f32[...) custom-call(bf16[8,64,384]{2,1,0:T(8,128)(2,1)} %get-tuple-element.5, ...), custom_call_target="tpu_custom_call" | custom-call | tf_op jit(solution)/shard_map/pallas_call | solution.py:1590
  156.3 0.7 slice_reduce_fusion
  157.0 0.0 copy-done.3
  157.0 0.8 concatenate.3
  157.8 0.0 copy-done.2
  157.8 0.0 copy-done.4
  157.8 0.0 copy-start.1
  157.8 0.6 divide_subtract_fusion
  158.4 0.0 copy-done
  158.4 0.8 copy.30
  159.2 0.0 copy-done.1
  (3 shorter events, 0.0 us)
Async XLA Ops:
  142.9 14.0 %copy-start.3 = (f32[16,128]{1,0:T(8,128)S(1)}, f32[16,128]{1,0:T(8,128)}, u32[]{:S(2)}) copy-start(f32[16,128]{1,0:T(8,128)} %get-tuple-element.63.gain_total) | copy-start | bytes 24580
  143.0 14.8 %copy-start.2 = (f32[2309]{0:T(1024)S(1)}, f32[2309]{0:T(1024)}, u32[]{:S(2)}) copy-start(f32[2309]{0:T(1024)} %param.25) | copy-start | bytes 27712
  143.0 14.8 %copy-start.4 = (f32[2309]{0:T(1024)S(1)}, f32[2309]{0:T(1024)}, u32[]{:S(2)}) copy-start(f32[2309]{0:T(1024)} %param.26) | copy-start | bytes 27712
  143.0 15.4 %copy-start = (bf16[256,1024]{1,0:T(8,128)(2,1)S(1)}, bf16[256,1024]{1,0:T(8,128)(2,1)}, u32[]{:S(2)}) copy-start(bf16[256,1024]{1,0:T(8,128)(2,1)} %get-tuple-element.54) | copy-start | bytes 1572868
  157.8 1.4 copy-start.1

commit v7 on v6

--- a/solution.py
+++ b/solution.py
@@ -260,8 +260,8 @@
     lat_first = place.push_first(links, g_latents, (), lat_a, "x")
     lat_first += place.push_first(links, g_latents, (), lat_b, "y")
     own_mats_copy.wait()
-    z_mats = [place.push_z(links, all_mats, step) for step in range(1, place.nz)]
-    firsts_m = [hand_on_mats(place.push_first, 0)]
+    z_mats = []
+    firsts_m = []
 
     lane_chunk = 128
     bias_row = channels - main
@@ -331,6 +331,8 @@
     for step in range(3, place.nz):
         first(step)
     second(2)
+    z_mats.extend(place.push_z(links, all_mats, step) for step in range(1, place.nz))
+    firsts_m.append(hand_on_mats(place.push_first, 0))
     norm_quarter(6)
     for step in range(3, place.nz):
         second(step)
@@ -753,6 +755,7 @@
     shares,
     query_turned,
     query_acc,
+    turned_acc,
     back_turned,
     grad_scores,
     gain_cols,
@@ -1007,7 +1010,7 @@
     query_turned[...] = jnp.where(
         lane_all < channels, pixel_query[...].astype(jnp.float32), 0.0
     ).T[0:padded].astype(BF)
-    query_acc[...] = jnp.zeros(query_acc.shape, jnp.float32)
+    turned_acc[...] = jnp.zeros(turned_acc.shape, jnp.float32)
     gain_cols[0] = jnp.broadcast_to(gain_rows[1:2, 0:lanes], (128, lanes)).T[0:padded]
     gain_cols[1] = jnp.broadcast_to(gain_rows[3:4, 0:lanes], (128, lanes)).T[0:padded]
     chunk = min(512, shard_pixels)
@@ -1034,8 +1037,8 @@
             grad_weights = jnp.dot(back_low, normed_chunk, preferred_element_type=jnp.float32)
             grad_chunk = (weights[slot, :, cols].astype(jnp.float32) * grad_weights).astype(BF)
             grad_scores[image, :, cols] = grad_chunk
-            query_acc[:, 0:padded] += lax.dot_general(
-                grad_chunk, normed_chunk, NT, preferred_element_type=jnp.float32
+            turned_acc[0:padded, :] += lax.dot_general(
+                normed_chunk, grad_chunk, NT, preferred_element_type=jnp.float32
             )
 
         if image + 2 < batches:
@@ -1093,6 +1096,7 @@
         job.push_second()
     attend_query(3)
 
+    query_acc[...] = turned_acc[...].T
     query_low[...] = query_acc[...].astype(BF)
     query_sent = []
     for step in range(1, group):
@@ -1273,6 +1277,7 @@
             pltpu.VMEM(cube[1:] + (batches, lat_rows, lanes), BF),
             pltpu.VMEM((padded, all_rows), BF),
             pltpu.VMEM((all_rows, lanes), jnp.float32),
+            pltpu.VMEM((lanes, all_rows), jnp.float32),
             pltpu.VMEM((batches, padded, all_rows), BF),
             pltpu.VMEM((batches, all_rows, shard_pixels), BF),
             pltpu.VMEM((2, padded, 128), jnp.float32),
@@ -1320,10 +1325,10 @@
     mats_grad,
     chan_grad,
     proj_blocks,
-    proj_left,
-    proj_right,
-    left_roots,
-    right_roots,
+    left_in,
+    right_in,
+    left_roots_in,
+    right_roots_in,
     keyval_weight,
     keyval_second,
     latents,
@@ -1338,6 +1343,7 @@
     gain_total,
     all_rows_keyval,
     all_mats,
+    mixed_in,
     pixel_grad,
     proj_grad,
     left_new,
@@ -1349,8 +1355,8 @@
     latent_grad,
     latent_second_new,
     latent_new,
-    lat_gain_grad,
-    channel_gain_grad,
+    gain_grad,
+    mixed_out,
     query,
     lat_normed,
     query_weight,
@@ -1363,6 +1369,10 @@
     key_rows,
     value_block,
     output_block,
+    proj_left,
+    proj_right,
+    left_roots,
+    right_roots,
     local_sems,
 ):
     place = Place(*dims)
@@ -1408,7 +1418,14 @@
     else:
         source = all_mats.at[output_row // place.ny, lax.rem(output_row, place.ny), :, :, 0, 0]
     output_copy = local_copy(source, output_block)
+    stat_copies = [
+        local_copy(left_in, proj_left),
+        local_copy(right_in, proj_right),
+        local_copy(left_roots_in, left_roots),
+        local_copy(right_roots_in, right_roots),
+    ]
     query_copy = local_copy(query_in, query)
+    mixed_out[...] = mixed_in[...]
     pixel_copies = [local_copy(pixel_low.at[i], pixel_came.at[i]) for i in range(batches)]
     pixel_sent = []
 
@@ -1444,17 +1461,6 @@
         )
         proj_new[index, mat] = proj_blocks[index, mat] - MATRIX_RATE * step
 
-    for mat in range(2):
-        for index in range(owned):
-            precondition(mat + 2, index, mats_grad[mat, index])
-    widen(0)
-    value_copy.wait()
-    own_cols = pl.ds(pl.multiple_of(block_col * col_block, col_block), owned * col_block)
-    output_grad = lax.dot_general(
-        value_block[...], chan_grad[own_cols, :], NT, preferred_element_type=jnp.float32
-    )
-    for index in range(owned):
-        precondition(1, index, output_grad[:, index * col_block : (index + 1) * col_block])
     keys_copy.wait()
     scale = width ** (-0.5)
     query_sum = query_total[...].reshape(all_rows, lanes)
@@ -1464,9 +1470,12 @@
     first = width // 128
     for sub in range(lanes // 128):
         cols = slice(sub * 128, (sub + 1) * 128)
-        channel_gain_grad[:, cols] = (
+        gain_grad[:, width + sub * 128 : width + (sub + 1) * 128] = (
             sums[:, cols] + gain_total[first + sub : first + sub + 1, :]
         ) * gain_rows[3:4, cols]
+    for sub in range(first):
+        at = width + lanes + sub * 128
+        gain_grad[:, at : at + 128] = gain_total[sub : sub + 1, :]
     for start in range(0, width, 256):
         grad_query[:, start : start + 256] = (
             lax.dot_general(
@@ -1474,7 +1483,7 @@
             )
             * scale
         ).astype(BF)
-    widen(1)
+    widen(0)
     arrived_local(weight_copies)
     normed_copy.wait()
     row_tile = width // place.nz
@@ -1487,10 +1496,22 @@
             preferred_element_type=jnp.float32,
         )
         grad_normed[:, cols] = part
-        lat_gain_grad[:, cols] = (
+        gain_grad[:, cols] = (
             jnp.sum(part * lat_normed[:, cols].astype(jnp.float32), axis=0, keepdims=True)
             / gain_rows[0:1, cols]
         )
+    widen(1)
+    arrived_local(stat_copies)
+    for mat in range(2):
+        for index in range(owned):
+            precondition(mat + 2, index, mats_grad[mat, index])
+    value_copy.wait()
+    own_cols = pl.ds(pl.multiple_of(block_col * col_block, col_block), owned * col_block)
+    output_grad = lax.dot_general(
+        value_block[...], chan_grad[own_cols, :], NT, preferred_element_type=jnp.float32
+    )
+    for index in range(owned):
+        precondition(1, index, output_grad[:, index * col_block : (index + 1) * col_block])
     widen(2)
     values = latents[...]
     centered = values - jnp.mean(values, axis=1, keepdims=True)
@@ -1559,6 +1580,7 @@
     pixel_query,
     gain_total,
     all_mats,
+    mixed,
 ):
     nz, ny, nx = dims
     proj_blocks, keyval_weight, latents = owned_arrays[0], owned_arrays[5], owned_arrays[7]
@@ -1584,13 +1606,21 @@
         like(latents),
         like(latents),
         like(latents),
-        jax.ShapeDtypeStruct((1, width), jnp.float32),
-        jax.ShapeDtypeStruct((1, lanes), jnp.float32),
+        jax.ShapeDtypeStruct((1, 2 * width + lanes), jnp.float32),
+        like(mixed),
     ]
     return pl.pallas_call(
         functools.partial(tail_kernel, dims, channels),
         out_shape=results,
-        in_specs=[vmem] * 14 + [anywhere] * 5 + [vmem] * 2 + [anywhere] * 2,
+        in_specs=(
+            [vmem] * 5
+            + [anywhere] * 4
+            + [vmem] * 5
+            + [anywhere] * 5
+            + [vmem] * 2
+            + [anywhere] * 2
+            + [vmem]
+        ),
         out_specs=[anywhere] + [vmem] * 12,
         scratch_shapes=[
             pltpu.VMEM((all_rows, width), BF),
@@ -1605,7 +1635,8 @@
             pltpu.VMEM((128, lanes), jnp.float32),
             pltpu.VMEM((row_block, lanes), BF),
             pltpu.VMEM((2, owned, row_block, col_block) if len(lead) == 3 else (nx, 2, row_block, col_block), BF),
-            pltpu.SemaphoreType.DMA((5 + width // col_block + 2 * batches,)),
+            *[pltpu.VMEM(array.shape, jnp.float32) for array in owned_arrays[1:5]],
+            pltpu.SemaphoreType.DMA((10 + width // col_block + 2 * batches,)),
         ],
         compiler_params=pltpu.CompilerParams(vmem_limit_bytes=56 * 2**20),
     )(
@@ -1624,6 +1655,7 @@
         gain_total,
         all_keyval.reshape(2 * width, lanes),
         all_mats,
+        mixed,
     )
 
 
@@ -1696,8 +1728,8 @@
         latent_grad,
         latent_second_new,
         latent_new,
-        lat_gain_grad,
-        channel_gain_grad,
+        gain_row,
+        mixed,
     ) = tail(
         dims,
         query_total,
@@ -1724,15 +1756,11 @@
         pixel_query,
         gain_total,
         mats,
+        mixed,
     )
-    gain_sums = gain_total.reshape(-1)
+    lanes = ceil_to(ceil_to(channels + 2, 16), 128)
     gain_grad = jnp.concatenate(
-        [
-            lat_gain_grad[0],
-            channel_gain_grad[0, :channels],
-            gain_sums[:width],
-        ],
-        axis=0,
+        [gain_row[0, : width + channels], gain_row[0, width + lanes :]], axis=0
     )
     gain_second_new, gain_new = moment_step(gains, gain_grad, gain_second, GAIN_RATE)
     return (

time: 160 us -> 157 us (0.981)
    pallas_call x1, Pallas kernels: 70.2 us -> 65.8 us  [back(): pl.pallas_call(functools.partial(back_kernel, dims, channels), out_shape=...]
    pallas_call x1, Pallas kernels: 70 us -> 72.6 us  [front(): pl.pallas_call(functools.partial(front_kernel, dims), out_shape=(jax.Shap...]
where the time goes in v7:
time: 157 us
  Pallas kernels  152 us (97%)
  local copies, waits for them, and re-layouts  2.21 us (1%)
  other arithmetic  2.01 us (1%)
    pallas_call x1, Pallas kernels, front(): pl.pallas_call(functools.partial(front_kernel, dims), out_shape=(jax.Shap...  72.6 us
    pallas_call x1, Pallas kernels, back(): pl.pallas_call(functools.partial(back_kernel, dims, channels), out_shape=...  65.8 us
    pallas_call x1, Pallas kernels, tail(): pl.pallas_call(functools.partial(tail_kernel, dims, channels), out_shape=...  13.3 us

profile of v7, /device:TPU:0, one launch (start us, length us, event | category | flops | bytes accessed | tf_op | source)
XLA Modules:
  0.0 156.7 jit_solution(13402265367537322541)
XLA Ops:
  0.6 0.7 fusion.3
  1.3 0.8 fusion.2
  2.1 0.6 pad_maximum_fusion.gain_rows
  2.8 72.6 %shard_map.253 = (bf16[4,2,2,2,4,64,128]{6,5,4,3,2,1,0:T(8,128)(2,1)}, bf16[4,2,2,2,64,384]{5,4,3,2,1,0:T(8,128)(2,1)}, bf16[512,1024]{1,0:T(8,128)(2,1)}, bf16[...) custom-call(bf16[261,4,2048]{2,1,0:T(4,128)(2,1)} %bitcast.17, ...), custom_call_target="tpu_custom_call" | custom-call | tf_op jit(solution)/shard_map/pallas_call | solution.py:484
  75.4 65.8 %shard_map.254 = (bf16[256,1024]{1,0:T(8,128)(2,1)}, bf16[4,261,2048]{2,1,0:T(8,128)(2,1)}, f32[2,4,64,128]{3,2,1,0:T(8,128)}, bf16[4,2,2,2,32,384]{5,4,3,2,1,0:...) custom-call(bf16[4,4,64,384]{3,2,1,0:T(8,128)(2,1)} %get-tuple-element.46.landed, ...), custom_call_target="tpu_custom_call" | custom-call | tf_op jit(solution)/shard_map/pallas_call | solution.py:1233
  141.3 0.0 copy-start
  141.3 0.0 copy-start.1
  141.3 13.3 %shard_map.255 = (f32[261,4,2048]{2,1,0:T(4,128)}, f32[4,4,64,128]{3,2,1,0:T(8,128)}, f32[4,4,64,64]{3,2,1,0:T(8,128)}, f32[4,4,128,128]{3,2,1,0:T(8,128)}, f32[...) custom-call(bf16[8,64,384]{2,1,0:T(8,128)(2,1)} %get-tuple-element.5, ...), custom_call_target="tpu_custom_call" | custom-call | tf_op jit(solution)/shard_map/pallas_call | solution.py:1612
  154.6 0.7 slice.19
  155.3 0.7 slice_reduce_fusion
  156.0 0.0 copy-done
  156.0 0.0 copy-done.1
  156.0 0.7 divide_subtract_fusion
  (2 shorter events, 0.0 us)
Async XLA Ops:
  141.3 14.8 %copy-start = (f32[2309]{0:T(1024)S(1)}, f32[2309]{0:T(1024)}, u32[]{:S(2)}) copy-start(f32[2309]{0:T(1024)} %param.25) | copy-start | bytes 27712
  141.3 14.8 %copy-start.1 = (f32[2309]{0:T(1024)S(1)}, f32[2309]{0:T(1024)}, u32[]{:S(2)}) copy-start(f32[2309]{0:T(1024)} %param.26) | copy-start | bytes 27712

commit v8 on v7

--- a/solution.py
+++ b/solution.py
@@ -808,7 +808,6 @@
             lead = (mat,) + (every,) * (len(mats.shape) - 2)
             copies.append(local_copy(source, mats.at[lead + (cols,)]))
         mats_copies.append(copies)
-    tops_copy = local_copy(sent_all, tops)
 
     def fetch(image):
         slot = image % 2
@@ -817,7 +816,6 @@
             local_copy(weights_all.at[image], weights.at[slot]),
         ]
 
-    fetched = [fetch(0), fetch(1)]
     place.barrier()
 
     def columns_of(mat, index):
@@ -870,6 +868,9 @@
         below = 0.5 + 0.5 * lax.erf(pre * 0.5**0.5)
         hidden[:, cols] = (pre * below).astype(BF)
         slope[:, cols] = below + pre * jnp.exp(-0.5 * pre * pre) * (0.5 / math.pi) ** 0.5
+
+    tops_copy = local_copy(sent_all, tops)
+    fetched = [fetch(0), fetch(1)]
 
     half_rows = row_block // 2
 
@@ -1012,7 +1013,8 @@
     ).T[0:padded].astype(BF)
     turned_acc[...] = jnp.zeros(turned_acc.shape, jnp.float32)
     gain_cols[0] = jnp.broadcast_to(gain_rows[1:2, 0:lanes], (128, lanes)).T[0:padded]
-    gain_cols[1] = jnp.broadcast_to(gain_rows[3:4, 0:lanes], (128, lanes)).T[0:padded]
+    gain_value = gain_cols[0]
+    gain_cols[1] = jnp.where(gain_value > 0.0, 1.0 / gain_value, 0.0)
     chunk = min(512, shard_pixels)
     tops_copy.wait()
 
@@ -1077,11 +1079,9 @@
         if turn + 2 < batches:
             fetched.append(fetch(order[turn + 2]))
 
-    share_pair(0)
-    share_pair(1)
+    for image in range(batches):
+        share_pair(image)
     attend_query(0)
-    share_pair(2)
-    share_pair(3)
     chan_job.push_second()
     attend_query(1)
     arrived(gain_sent)
@@ -1092,8 +1092,6 @@
         gain_up.append(links.push(own, own, lax.rem(z + step, place.nz), p))
     attend_query(2)
     chan_job.push_z()
-    for job in inward:
-        job.push_second()
     attend_query(3)
 
     query_acc[...] = turned_acc[...].T
@@ -1103,6 +1101,8 @@
         q = lax.rem(p + step, group)
         part = pl.ds(pl.multiple_of(q * lat_rows, lat_rows), lat_rows)
         query_sent.append(links.push(query_low.at[part], query_came.at[step - 1], z, q))
+    for job in inward:
+        job.push_second()
     attend_pixels(0)
     held, came_z = chan_job.total()
     for part in came_z:
@@ -1424,7 +1424,8 @@
         local_copy(left_roots_in, left_roots),
         local_copy(right_roots_in, right_roots),
     ]
-    query_copy = local_copy(query_in, query)
+    key_cols = pl.ds(pl.multiple_of(key_start // 128 * 128, 128), 128)
+    query_copy = local_copy(query_in.at[:, key_cols], query)
     mixed_out[...] = mixed_in[...]
     pixel_copies = [local_copy(pixel_low.at[i], pixel_came.at[i]) for i in range(batches)]
     pixel_sent = []
@@ -1472,7 +1473,7 @@
         cols = slice(sub * 128, (sub + 1) * 128)
         gain_grad[:, width + sub * 128 : width + (sub + 1) * 128] = (
             sums[:, cols] + gain_total[first + sub : first + sub + 1, :]
-        ) * gain_rows[3:4, cols]
+        ) / jnp.where(gain_rows[1:2, cols] > 0.0, gain_rows[1:2, cols], 1.0)
     for sub in range(first):
         at = width + lanes + sub * 128
         gain_grad[:, at : at + 128] = gain_total[sub : sub + 1, :]
@@ -1540,9 +1541,8 @@
     widen(3)
 
     query_copy.wait()
-    cols = pl.ds(pl.multiple_of(key_start // 128 * 128, 128), 128)
     key_rows[...] = (
-        lax.dot_general(query[:, cols], query_sum, TN, preferred_element_type=jnp.float32) * scale
+        lax.dot_general(query[...], query_sum, TN, preferred_element_type=jnp.float32) * scale
     )
     part = pl.ds(pl.multiple_of(lax.rem(key_start, 128), keyval_rows), keyval_rows)
     grad = key_rows[part, :]
@@ -1623,7 +1623,7 @@
         ),
         out_specs=[anywhere] + [vmem] * 12,
         scratch_shapes=[
-            pltpu.VMEM((all_rows, width), BF),
+            pltpu.VMEM((all_rows, 128), BF),
             pltpu.VMEM((all_rows, width), BF),
             pltpu.VMEM(lead + (row_block, width), BF),
             pltpu.VMEM((nz // 2, ny, nx, 2) + all_keyval.shape[4:], BF),
@@ -1686,7 +1686,7 @@
     side = math.isqrt(groups // 2)
     dims = (lax.axis_size("samp"), side, side)
     widen = lambda row: jnp.pad(row, (0, width - row.shape[0]))
-    gain_rows = jnp.stack([lat_gain, widen(in_gain), mlp_gain, widen(1.0 / in_gain)])
+    gain_rows = jnp.stack([lat_gain, widen(in_gain), mlp_gain])
     keyval_own = keyval_weight.T
     (
         query_blocks,

time: 157 us -> 157 us (level)
  no operation moved by 1% of the time
where the time goes in v8:
time: 157 us; the launch traced here: 156 us
  Pallas kernels  151 us (96%)
  local copies, waits for them, and re-layouts  2.89 us (2%)
    pallas_call x1, Pallas kernels, front(): pl.pallas_call(functools.partial(front_kernel, dims), out_shape=(jax.Shap...  72.6 us
    pallas_call x1, Pallas kernels, back(): pl.pallas_call(functools.partial(back_kernel, dims, channels), out_shape=...  65.7 us
    pallas_call x1, Pallas kernels, tail(): pl.pallas_call(functools.partial(tail_kernel, dims, channels), out_shape=...  13.1 us

profile of v8, /device:TPU:0, one launch (start us, length us, event | category | flops | bytes accessed | tf_op | source)
XLA Modules:
  0.0 156.4 jit_solution(7692136743138971541)
XLA Ops:
  0.6 0.7 slice.16
  1.3 0.8 fusion.2
  2.1 0.6 pad_maximum_fusion.gain_rows
  2.7 72.6 %shard_map.253 = (bf16[4,2,2,2,4,64,128]{6,5,4,3,2,1,0:T(8,128)(2,1)}, bf16[4,2,2,2,64,384]{5,4,3,2,1,0:T(8,128)(2,1)}, bf16[512,1024]{1,0:T(8,128)(2,1)}, bf16[...) custom-call(bf16[261,4,2048]{2,1,0:T(4,128)(2,1)} %bitcast.16, ...), custom_call_target="tpu_custom_call" | custom-call | tf_op jit(solution)/shard_map/pallas_call | solution.py:484
  75.4 65.7 %shard_map.254 = (bf16[256,1024]{1,0:T(8,128)(2,1)}, bf16[4,261,2048]{2,1,0:T(8,128)(2,1)}, f32[2,4,64,128]{3,2,1,0:T(8,128)}, bf16[4,2,2,2,32,384]{5,4,3,2,1,0:...) custom-call(bf16[4,4,64,384]{3,2,1,0:T(8,128)(2,1)} %get-tuple-element.46.landed, ...), custom_call_target="tpu_custom_call" | custom-call | tf_op jit(solution)/shard_map/pallas_call | solution.py:1233
  141.1 0.0 copy-start
  141.1 0.0 copy-start.1
  141.1 13.1 %shard_map.255 = (f32[261,4,2048]{2,1,0:T(4,128)}, f32[4,4,64,128]{3,2,1,0:T(8,128)}, f32[4,4,64,64]{3,2,1,0:T(8,128)}, f32[4,4,128,128]{3,2,1,0:T(8,128)}, f32[...) custom-call(bf16[8,64,384]{2,1,0:T(8,128)(2,1)} %get-tuple-element.5, ...), custom_call_target="tpu_custom_call" | custom-call | tf_op jit(solution)/shard_map/pallas_call | solution.py:1612
  154.2 0.7 slice.19
  154.9 0.7 slice_reduce_fusion
  155.6 0.0 copy-done
  155.6 0.0 copy-done.1
  155.7 0.7 divide_subtract_fusion
  (1 shorter events, 0.0 us)
Async XLA Ops:
  141.1 14.5 %copy-start = (f32[2309]{0:T(1024)S(1)}, f32[2309]{0:T(1024)}, u32[]{:S(2)}) copy-start(f32[2309]{0:T(1024)} %param.25) | copy-start | bytes 27712
  141.1 14.5 %copy-start.1 = (f32[2309]{0:T(1024)S(1)}, f32[2309]{0:T(1024)}, u32[]{:S(2)}) copy-start(f32[2309]{0:T(1024)} %param.26) | copy-start | bytes 27712
